TPU v7x, 128 devices: a whole 4x4x4 slice. The times are simulated.
128 devices in a mesh: prow: 32 (over y, z, core), pcol: 4 (over x).
Axes of the slice: x: 4, y: 4, z: 4, core: 2. Of those that a mesh axis runs over, the one named last changes fastest.
Arguments:
- matrix: float32 [24576, 16384], P('prow', 'pcol'), may hold values from -6 to 6
- lower_panels: float32 [2, 24576, 256], P(None, ('prow', 'pcol')), may hold values from -0.375 to 0.375
- inverses: float32 [2, 256, 256], replicated
- pivots: int32 [2, 256], replicated, may hold values from 256 to 24575, as said below
Outputs:
- updated: float32 [24576, 16384], P('prow', 'pcol')
Inputs may be any that keep to these rules, and one draw needn't show every extreme that they name: `pivots`: the 256 entries of panel k are distinct matrix rows, each at least (k + 1) * 256; among them is a row of matrix block k + 1 and a row of matrix block k + 32 // 2; their spread over process rows is uneven.
All inputs are finite; a program needn't handle non-finite values.
Results may differ from a plain program's by a relative error of at most 0.0001.
Values sent between devices are 32-bit elements; how exact they have to be, the bound alone decides.
No kernel may reach another device: no remote copies, remote signals or barrier semaphores. Data moves between devices by JAX's collectives and lax.ppermute only.
A program may use at most 128 MiB of HBM per device.

v0:
```python
import jax
import jax.numpy as jnp
from jax import lax
from jax.sharding import PartitionSpec as P


def from_root(value, axis, source):
    kept = jnp.where(lax.axis_index(axis) == source, value, 0).astype(value.dtype)
    return lax.psum(kept, axis)


def body(matrix, lower_panels, inverses, pivots):
    prow_count = lax.axis_size("prow")
    row_rank = lax.axis_index("prow")
    row_count = matrix.shape[0]
    block_rows = inverses.shape[1]
    local_row = jnp.arange(row_count, dtype=jnp.int32)
    mat_index = (
        local_row // block_rows * prow_count + row_rank
    ) * block_rows + local_row % block_rows
    updated = matrix
    for panel in range(2):
        top_start = panel * block_rows
        lower_part = lax.all_gather(lower_panels[panel], "pcol", axis=0, tiled=True)
        pivot_list = pivots[panel]
        blocks = pivot_list // block_rows
        owner_rank = blocks % prow_count
        place_local = blocks // prow_count * block_rows + pivot_list % block_rows
        owned = owner_rank == row_rank
        picked = jnp.where(owned[:, None], updated[place_local], 0.0)
        old_top = from_root(updated[:block_rows], "prow", panel)
        target = jnp.where(owned, place_local, row_count)
        updated = updated.at[target].set(old_top, mode="drop")
        below = (mat_index >= top_start + block_rows)[:, None]
        is_root = row_rank == panel
        current = updated
        shared = lax.psum_scatter(picked, "prow", scatter_dimension=1, tiled=True)
        upper_share = jnp.dot(inverses[panel], shared, precision=lax.Precision.HIGHEST)
        column_piece = lax.all_gather(upper_share, "prow", axis=1, tiled=True)
        product = jnp.dot(lower_part, column_piece, precision=lax.Precision.HIGHEST)
        result = jnp.where(below, current - product, current)
        updated = result.at[:block_rows].set(jnp.where(is_root, column_piece, result[:block_rows]))
    return updated


def solution(mesh):
    placed = (P("prow", "pcol"), P(None, ("prow", "pcol"), None), P(), P())
    return jax.shard_map(
        body, mesh=mesh, in_specs=placed, out_specs=P("prow", "pcol"), check_vma=False
    )
```

profile of v0, /device:TPU:1, one launch (start us, length us, event | category | flops | bytes accessed | tf_op | source)
XLA Modules:
  0.0 628.4 jit_solution(5661176083629431800)
XLA Ops:
  6.5 0.0 copy-start.4
  6.5 0.0 reduce-scatter.3.cloned.1.call-start
  6.5 10.9 %copy.33 = f32[768,4096]{1,0:T(8,128)} copy(f32[768,4096]{1,0:T(8,128)} %param.8) | data formatting | bytes 25165824
  17.5 0.0 copy-done.4
  17.6 10.2 %gather_fusion = f32[256,4096]{1,0:T(8,128)} fusion(f32[768,4096]{1,0:T(8,128)} %copy.33, s32[1024]{0:T(1024)S(1)} %pad_clamp_fusion.1), kind=kCustom, calls=%fused_computation | custom fusion | bytes 8389632 | tf_op jit(solution)/shard_map/gather | solution.py:30
  27.8 5.6 copy.15
  33.4 4.4 broadcast_select_fusion.2
  37.8 0.0 reduce-scatter.3.cloned.1.call-update
  37.9 0.0 all-reduce.3.cloned.1.call-start
  37.9 4.6 slice.63
  42.5 5.6 copy.25
  48.1 2.2 broadcast_select_fusion.3
  50.4 0.0 copy-start.2
  50.4 0.0 copy-start.3
  50.4 0.0 all-reduce.3.cloned.1.call-update
  50.4 0.0 all-gather.5.cloned.1.call-start
  50.4 71.2 %reduce-scatter.3.cloned.1.call-done = f32[256,128]{0,1:T(8,128)} async-done(((f32[256,4096]{0,1:T(8,128)}), f32[256,128]{0,1:T(8,128)}) %reduce-scatter.3.cloned.1.call-update) | async-done | bytes 131088 | tf_op jit(solution)/shard_map/reduce_scatter | solution.py:37
  121.7 0.0 copy-done.2
  121.7 2.0 convolution_bitcast_fusion.1
  123.6 0.0 all-gather.5.cloned.1.call-update
  123.7 0.0 reduce-scatter.5.cloned.1.call-start
  123.8 0.0 copy-done.3
  123.8 11.2 %all-gather = f32[1,768,256]{2,1,0:T(8,128)S(1)} all-gather(f32[1,192,256]{2,1,0:T(8,128)S(1)} %get-tuple-element.38), channel_id=2, replica_groups=mesh['prow'=32,'pcol'=4] {'pcol'}, dimensions={1}, use_global_device_ids=true | all-gather | bytes 983040 | tf_op jit(solution)/shard_map/all_gather | solution.py:24
  135.0 103.1 %all-reduce.3.cloned.1.call-done = f32[256,4096]{0,1:T(8,128)} async-done(((f32[256,4096]{0,1:T(8,128)}), f32[256,4096]{0,1:T(8,128)}) %all-reduce.3.cloned.1.call-update) | async-done | bytes 4194320 | tf_op jit(solution)/shard_map/psum | solution.py:9
  238.1 5.6 copy.14
  243.7 13.9 %scatter_fusion = f32[768,4096]{1,0:T(8,128)} fusion(f32[768,4096]{1,0:T(8,128)} %copy.33, s32[256]{0:T(256)S(1)} %bitcast.54, f32[256,4096]{1,0:T(8,128)} %copy.14), kind=kCustom, calls=%fused_computation.2 | custom fusion | bytes 12583936 | tf_op jit(solution)/shard_map/scatter | solution.py:33
  257.6 12.6 %copy.16 = f32[768,4096]{0,1:T(8,128)} copy(f32[768,4096]{1,0:T(8,128)} %scatter_fusion) | data formatting | bytes 25165824 | tf_op jit(solution)/shard_map/scatter | solution.py:33
  270.2 16.8 %all-gather.5.cloned.1.call-done = f32[256,4096]{0,1:T(8,128)} async-done(((f32[256,128]{0,1:T(8,128)}), f32[256,4096]{0,1:T(8,128)}) %all-gather.5.cloned.1.call-update) | async-done | bytes 4194320 | tf_op jit(solution)/shard_map/all_gather | solution.py:39
  287.0 0.0 copy-start.1
  287.0 17.1 %subtract_select_fusion.1 = f32[768,4096]{0,1:T(8,128)} fusion(f32[768,4096]{0,1:T(8,128)} %copy.16, f32[256,4096]{0,1:T(8,128)} %all-gather.5.cloned.1.call-done, pred[768]{0:T(1024)(128)(4,1)S(1)} %broadcast_compare_fusion.1, f32[1,768,256]{2,1,0:T(8,128)S(1)} %all-gather), kind=kOutput, calls=%fused_computation.5 | convolution fusion | flops 9669967872 | bytes 30147328 | tf_op jit(solution)/shard_map/dot_general | solution.py:40
  304.1 0.0 copy-done.1
  304.1 6.0 broadcast_select_fusion.1
  310.1 12.6 %copy.18 = f32[768,4096]{1,0:T(8,128)} copy(f32[768,4096]{0,1:T(8,128)} %get-tuple-element.36) | data formatting | bytes 25165824 | tf_op jit(solution)/shard_map/scatter | solution.py:42
  322.7 10.3 %gather_fusion.1 = f32[256,4096]{1,0:T(8,128)} fusion(f32[768,4096]{1,0:T(8,128)} %copy.18, s32[1024]{0:T(1024)S(1)} %pad_clamp_fusion), kind=kCustom, calls=%fused_computation.1 | custom fusion | bytes 8389632 | tf_op jit(solution)/shard_map/gather | solution.py:30
  333.0 5.6 copy.21
  338.6 4.5 broadcast_select_fusion
  343.1 0.0 reduce-scatter.5.cloned.1.call-update
  343.1 0.0 all-reduce.5.cloned.1.call-start
  343.2 0.5 all-reduce.5.cloned.1.call-update
  343.7 0.0 all-gather.7.cloned.1.call-start
  343.8 78.8 %reduce-scatter.5.cloned.1.call-done = f32[256,128]{0,1:T(8,128)} async-done(((f32[256,4096]{0,1:T(8,128)}), f32[256,128]{0,1:T(8,128)}) %reduce-scatter.5.cloned.1.call-update) | async-done | bytes 131088 | tf_op jit(solution)/shard_map/reduce_scatter | solution.py:37
  422.6 2.0 convolution_bitcast_fusion
  424.5 0.0 all-gather.7.cloned.1.call-update
  424.6 11.3 %all-gather.1 = f32[1,768,256]{2,1,0:T(8,128)S(1)} all-gather(f32[1,192,256]{2,1,0:T(8,128)S(1)} %get-tuple-element.37), channel_id=3, replica_groups=mesh['prow'=32,'pcol'=4] {'pcol'}, dimensions={1}, use_global_device_ids=true | all-gather | bytes 983040 | tf_op jit(solution)/shard_map/all_gather | solution.py:24
  435.9 102.5 %all-reduce.5.cloned.1.call-done = f32[256,4096]{0,1:T(8,128)} async-done(((f32[256,4096]{0,1:T(8,128)}), f32[256,4096]{0,1:T(8,128)}) %all-reduce.5.cloned.1.call-update) | async-done | bytes 4194320 | tf_op jit(solution)/shard_map/psum | solution.py:9
  538.5 5.6 copy.19
  544.1 13.7 %scatter_fusion.1 = f32[768,4096]{1,0:T(8,128)} fusion(f32[768,4096]{1,0:T(8,128)} %copy.18, s32[256]{0:T(256)S(1)} %bitcast.55, f32[256,4096]{1,0:T(8,128)} %copy.19), kind=kCustom, calls=%fused_computation.3 | custom fusion | bytes 12583936 | tf_op jit(solution)/shard_map/scatter | solution.py:33
  557.7 12.6 %copy.22 = f32[768,4096]{0,1:T(8,128)} copy(f32[768,4096]{1,0:T(8,128)} %scatter_fusion.1) | data formatting | bytes 25165824 | tf_op jit(solution)/shard_map/scatter | solution.py:33
  570.3 16.7 %all-gather.7.cloned.1.call-done = f32[256,4096]{0,1:T(8,128)} async-done(((f32[256,128]{0,1:T(8,128)}), f32[256,4096]{0,1:T(8,128)}) %all-gather.7.cloned.1.call-update) | async-done | bytes 4194320 | tf_op jit(solution)/shard_map/all_gather | solution.py:39
  587.0 0.0 copy-start
  587.0 17.1 %subtract_select_fusion = f32[768,4096]{0,1:T(8,128)} fusion(f32[768,4096]{0,1:T(8,128)} %copy.22, f32[256,4096]{0,1:T(8,128)} %all-gather.7.cloned.1.call-done, pred[768]{0:T(1024)(128)(4,1)S(1)} %broadcast_compare_fusion, f32[1,768,256]{2,1,0:T(8,128)S(1)} %all-gather.1), kind=kOutput, calls=%fused_computation.4 | convolution fusion | flops 9669967872 | bytes 30147328 | tf_op jit(solution)/shard_map/dot_general | solution.py:40
  604.1 0.0 copy-done
  604.1 4.8 fusion
  608.9 12.6 %copy.24 = f32[768,4096]{1,0:T(8,128)} copy(f32[768,4096]{0,1:T(8,128)} %fusion) | data formatting | bytes 25165824 | tf_op jit(solution)/shard_map/scatter | solution.py:42
  (12 shorter events, 0.2 us)
Async XLA Ops:
  6.5 10.9 %copy-start.4 = (s32[2,256]{1,0:T(2,128)S(1)}, s32[2,256]{1,0:T(2,128)}, u32[]{:S(2)}) copy-start(s32[2,256]{1,0:T(2,128)} %param.11) | copy-start | bytes 6148
  6.5 115.1 %reduce-scatter.3.cloned.1.call-start = ((), (), s32[]{:S(2)}) async-start(), calls=%async_computation.3 | async-start | bytes 4325376 | tf_op jit(solution)/shard_map/reduce_scatter | solution.py:37
  37.9 200.2 %all-reduce.3.cloned.1.call-start = ((), (), s32[]{:S(2)}) async-start(), calls=%async_computation.2 | async-start | bytes 8388608 | tf_op jit(solution)/shard_map/psum | solution.py:9
  50.4 71.3 %copy-start.2 = (f32[2,256,256]{2,1,0:T(8,128)S(1)}, f32[2,256,256]{2,1,0:T(8,128)}, u32[]{:S(2)}) copy-start(f32[2,256,256]{2,1,0:T(8,128)} %param.10) | copy-start | bytes 1572868
  50.4 73.4 %copy-start.3 = (f32[2,192,256]{2,1,0:T(8,128)S(1)}, f32[2,192,256]{2,1,0:T(8,128)}, u32[]{:S(2)}) copy-start(f32[2,192,256]{2,1,0:T(8,128)} %param.9) | copy-start | bytes 1179652
  50.4 236.6 %all-gather.5.cloned.1.call-start = ((), (), s32[]{:S(2)}) async-start(), calls=%async_computation.4 | async-start | bytes 4325376 | tf_op jit(solution)/shard_map/all_gather | solution.py:39
  123.7 298.9 %reduce-scatter.5.cloned.1.call-start = ((), (), s32[]{:S(2)}) async-start(), calls=%async_computation.6 | async-start | bytes 4325376 | tf_op jit(solution)/shard_map/reduce_scatter | solution.py:37
  287.0 17.1 %copy-start.1 = (f32[256,4096]{0,1:T(8,128)S(1)}, f32[256,4096]{0,1:T(8,128)}, u32[]{:S(2)}) copy-start(f32[256,4096]{0,1:T(8,128)} %all-gather.5.cloned.1.call-done) | copy-start | bytes 12582916
  343.1 195.3 %all-reduce.5.cloned.1.call-start = ((), (), s32[]{:S(2)}) async-start(), calls=%async_computation.5 | async-start | bytes 8388608 | tf_op jit(solution)/shard_map/psum | solution.py:9
  343.7 243.3 %all-gather.7.cloned.1.call-start = ((), (), s32[]{:S(2)}) async-start(), calls=%async_computation.7 | async-start | bytes 4325376 | tf_op jit(solution)/shard_map/all_gather | solution.py:39
  587.0 17.1 %copy-start = (f32[256,4096]{0,1:T(8,128)S(1)}, f32[256,4096]{0,1:T(8,128)}, u32[]{:S(2)}) copy-start(f32[256,4096]{0,1:T(8,128)} %all-gather.7.cloned.1.call-done) | copy-start | bytes 12582916
Sparse Core Ops, SparseCore 0:
  38.0 83.6 reduce-scatter.2
  125.4 112.6 all-reduce.2
  240.6 46.3 all-gather.4
  343.3 79.2 reduce-scatter.4
  425.8 112.6 all-reduce.4
  540.6 46.3 all-gather.6
where the time goes:
time: 630 us; the launch traced here: 628 us
  waiting for transfers between devices  390 us (62%)
  local copies, waits for them, and re-layouts  142 us (23%)
  matrix products  38.1 us (6%)
  blocking collectives  22.5 us (4%)
  other arithmetic  22.1 us (4%)
  between operations  13.6 us (2%)
    psum x2, waiting for transfers between devices, from_root(): return lax.psum(kept, axis)  206 us
    reduce_scatter x2, waiting for transfers between devices, body(): shared = lax.psum_scatter(picked, 'prow', scatter_dimension=1, tiled=True)  150 us
    scatter x4, local copies, waits for them, and re-layouts, body(): updated = updated.at[target].set(old_top, mode='drop')  52.8 us
    dot_general x2, matrix products, body(): product = jnp.dot(lower_part, column_piece, precision=lax.Precision.HIGHEST)  34.2 us
    all_gather x2, waiting for transfers between devices, body(): column_piece = lax.all_gather(upper_share, 'prow', axis=1, tiled=True)  33.5 us
    gather x4, local copies, waits for them, and re-layouts, body(): picked = jnp.where(owned[:, None], updated[place_local], 0.0)  31.7 us
    scatter x2, local copies, waits for them, and re-layouts, body(): result.at[:block_rows]  25.2 us
    all_gather x2, blocking collectives, body(): lower_part = lax.all_gather(lower_panels[panel], 'pcol', axis=0, tiled=True)  22.5 us
  transfers between devices with their start and end apart: 6, of which 6 were waited for; matrix products, arithmetic and copies ran while one was open for 13% of the time, Pallas kernels for 0%

commit v1 on v0

v1 whole, which is shorter than its diff:
```python
import jax
import jax.numpy as jnp
from jax import lax
from jax.experimental import pallas as pl
from jax.experimental.pallas import tpu as pltpu
from jax.sharding import PartitionSpec as P

F32 = jnp.float32
BF16 = jnp.bfloat16
HIGHEST = lax.Precision.HIGHEST
NB = 256
LANES = 128
VMEM_LIMIT = 56 * 1024 * 1024


def rank_of(y, z, core):
    return ((y % 4) * 4 + z % 4) * 2 + core


def shift_pairs(dy, dz):
    return [
        (rank_of(y, z, core), rank_of(y + dy, z + dz, core))
        for y in range(4)
        for z in range(4)
        for core in range(2)
    ]


SWAP_CORES = [(rank, rank ^ 1) for rank in range(32)]


def shift(value, dy=0, dz=0):
    return lax.ppermute(value, "prow", shift_pairs(dy, dz))


def split_two(value):
    high = value.astype(BF16)
    low = (value - high.astype(F32)).astype(BF16)
    return high, low


def pick_kernel(place_ref, select_ref, matrix_ref, first_ref, second_ref):
    high, low = split_two(matrix_ref[...])
    select = select_ref[...]
    rows = jnp.dot(select, high, preferred_element_type=F32)
    rows = rows + jnp.dot(select, low, preferred_element_type=F32)
    for z_share in range(4):
        apart = (z_share + 4 - place_ref[2]) % 4
        part = rows[:, z_share * LANES : (z_share + 1) * LANES]
        first_ref[apart, 0] = part[:NB]
        second_ref[0, apart] = part[NB:]


def pick_rows(place, select, matrix):
    return pl.pallas_call(
        pick_kernel,
        out_shape=(
            jax.ShapeDtypeStruct((4, 4, NB, LANES), F32),
            jax.ShapeDtypeStruct((4, 4, NB, LANES), F32),
        ),
        grid_spec=pltpu.PrefetchScalarGridSpec(
            num_scalar_prefetch=1,
            grid=(4,),
            in_specs=[
                pl.BlockSpec(select.shape, lambda i, place: (0, 0)),
                pl.BlockSpec(
                    (matrix.shape[0], 4 * LANES),
                    lambda i, place: (0, place[0] * 4 + (place[1] + i) % 4),
                ),
            ],
            out_specs=(
                pl.BlockSpec((4, 1, NB, LANES), lambda i, place: (0, i, 0, 0)),
                pl.BlockSpec((1, 4, NB, LANES), lambda i, place: (i, 0, 0, 0)),
            ),
        ),
        compiler_params=pltpu.CompilerParams(vmem_limit_bytes=VMEM_LIMIT),
        cost_estimate=pl.CostEstimate(
            flops=2 * 2 * 512 * 768 * 2048, bytes_accessed=10 << 20, transcendentals=0
        ),
        name="pick_rows",
    )(place, select, matrix)


def top_parts_kernel(matrix_ref, *refs):
    outs, sems = refs[:8], refs[8]
    copies = []
    for core in range(2):
        for y in range(4):
            for z in range(4):
                columns = pl.ds((core * 16 + y * 4 + z) * LANES, LANES)
                copies.append((matrix_ref.at[pl.ds(0, 128), columns], outs[z].at[y, core]))
                copies.append((matrix_ref.at[pl.ds(128, 128), columns], outs[4 + y].at[z, core]))
    copies = [
        pltpu.make_async_copy(source, target, sems.at[i])
        for i, (source, target) in enumerate(copies)
    ]
    for copy in copies:
        copy.start()
    for copy in copies:
        copy.wait()


def top_parts(matrix):
    return pl.pallas_call(
        top_parts_kernel,
        out_shape=tuple(jax.ShapeDtypeStruct((4, 2, 128, LANES), F32) for _ in range(8)),
        in_specs=[pl.BlockSpec(memory_space=pl.ANY)],
        out_specs=tuple(pl.BlockSpec(memory_space=pl.ANY) for _ in range(8)),
        scratch_shapes=[pltpu.SemaphoreType.DMA((64,))],
        cost_estimate=pl.CostEstimate(flops=0, bytes_accessed=8 << 20, transcendentals=0),
        name="top_parts",
    )(matrix)


def scatter_tops(matrix, y, z):
    parts = top_parts(matrix)
    at_root = (y == 0) & (z == 0)

    def send(value, target_y, target_z, source_y, source_z):
        pairs = [
            (rank_of(sy, sz, core), rank_of(ty, tz, core))
            for sy, sz, ty, tz in zip(source_y, source_z, target_y, target_z)
            for core in range(2)
        ]
        return lax.ppermute(value, "prow", pairs)

    got_a = [send(parts[d], [0], [d], [0], [0]) for d in (1, 3, 2)]
    got_b = [send(parts[4 + d], [d], [0], [0], [0]) for d in (1, 3, 2)]
    held_a = jnp.where(at_root, parts[0], got_a[0] + got_a[1] + got_a[2])
    held_b = jnp.where(at_root, parts[4], got_b[0] + got_b[1] + got_b[2])
    four = list(range(4))
    got_a = [send(held_a[d], [d] * 4, four, [0] * 4, four) for d in (1, 3, 2)]
    got_b = [send(held_b[d], four, [d] * 4, four, [0] * 4) for d in (1, 3, 2)]
    share_a = jnp.where(y == 0, held_a[0], got_a[0] + got_a[1] + got_a[2])
    share_b = jnp.where(z == 0, held_b[0], got_b[0] + got_b[1] + got_b[2])
    return jnp.concatenate([share_a, share_b], axis=1)


def solve_kernel(raw0_ref, raw1_ref, inverse_ref, lower_ref, out_ref):
    def dot(a, b):
        return jnp.dot(a, b, precision=HIGHEST, preferred_element_type=F32)

    upper0 = dot(inverse_ref[0], raw0_ref[...])
    raw1 = raw1_ref[...] - dot(lower_ref[...], upper0)
    out_ref[:NB] = upper0
    out_ref[NB:] = dot(inverse_ref[1], raw1)


def solve(raw0, raw1, inverses, lower):
    return pl.pallas_call(
        solve_kernel,
        out_shape=jax.ShapeDtypeStruct((2 * NB, LANES), F32),
        cost_estimate=pl.CostEstimate(
            flops=6 * 3 * 2 * 256 * 256 * 128, bytes_accessed=1 << 20, transcendentals=0
        ),
        name="solve",
    )(raw0, raw1, inverses, lower)


def update_kernel(rank_ref, left_ref, keep_ref, matrix_ref, upper_ref, top_ref, out_ref):
    upper = jnp.concatenate([upper_ref[0, 0], upper_ref[1, 0]], axis=1)
    tops = jnp.concatenate(
        [
            jnp.concatenate([top_ref[0, core, 0], top_ref[1, core, 0]], axis=1)
            for core in range(2)
        ],
        axis=0,
    )
    upper_high, upper_low = split_two(upper)
    top_high, top_low = split_two(tops)
    right = jnp.concatenate([upper_high, upper_low, upper_high, top_high, top_low], axis=0)
    total = jnp.dot(left_ref[...], right, preferred_element_type=F32)
    out_ref[...] = matrix_ref[...] * keep_ref[...] + total

    @pl.when(rank_ref[0] == 0)
    def _():
        out_ref[:NB] = upper[:NB]

    @pl.when(rank_ref[0] == 1)
    def _():
        out_ref[:NB] = upper[NB:]


def update(rank, left, keep, matrix, upper, tops):
    rows, columns = matrix.shape
    width = 2 * LANES
    return pl.pallas_call(
        update_kernel,
        out_shape=jax.ShapeDtypeStruct(matrix.shape, F32),
        grid_spec=pltpu.PrefetchScalarGridSpec(
            num_scalar_prefetch=1,
            grid=(columns // width,),
            in_specs=[
                pl.BlockSpec(left.shape, lambda i, rank: (0, 0)),
                pl.BlockSpec(keep.shape, lambda i, rank: (0, 0)),
                pl.BlockSpec((rows, width), lambda i, rank: (0, i)),
                pl.BlockSpec((2, 1, 2 * NB, LANES), lambda i, rank: (i % 8, i // 8, 0, 0)),
                pl.BlockSpec((2, 2, 1, NB, LANES), lambda i, rank: (i % 8, 0, i // 8, 0, 0)),
            ],
            out_specs=pl.BlockSpec((rows, width), lambda i, rank: (0, i)),
        ),
        compiler_params=pltpu.CompilerParams(vmem_limit_bytes=VMEM_LIMIT),
        cost_estimate=pl.CostEstimate(
            flops=2 * rows * columns * left.shape[1], bytes_accessed=40 << 20, transcendentals=0
        ),
        name="update",
    )(rank, left, keep, matrix, upper, tops)


def body(matrix, lower_panels, inverses, pivots):
    rank = lax.axis_index("prow")
    column_rank = lax.axis_index("pcol")
    y, z, core = rank // 8, rank // 2 % 4, rank % 2
    rows = matrix.shape[0]
    index = jnp.arange(NB, dtype=jnp.int32)

    pivot0, pivot1 = pivots[0], pivots[1]
    again = pivot1[:, None] == pivot0[None, :]
    from_top = jnp.any(again, axis=1)
    source1 = jnp.where(from_top, jnp.sum(jnp.where(again, index[None, :], 0), axis=1), pivot1)
    sources = jnp.concatenate([pivot0, source1])

    def local(matrix_row):
        blocks = matrix_row // NB
        place = blocks // 32 * NB + matrix_row % NB
        return jnp.where(blocks % 32 == rank, place, -1)

    local_row = jnp.arange(rows, dtype=jnp.int32)
    select = (local(sources)[:, None] == local_row[None, :]).astype(BF16)

    keep_place = jnp.stack([core, y, z]).astype(jnp.int32)
    send_place = jnp.stack([1 - core, y, z]).astype(jnp.int32)
    sent = pick_rows(send_place, select, matrix)
    other = [lax.ppermute(value, "prow", SWAP_CORES) for value in sent]
    kept = pick_rows(keep_place, select, matrix)
    part_a = [kept[0][d] + other[0][d] for d in range(4)]
    part_b = [kept[1][d] + other[1][d] for d in range(4)]

    def add_up(parts, axis):
        total = parts[0]
        for d in (1, 3, 2):
            total = total + shift(parts[d], **{axis: d})
        return total

    part_a = add_up(part_a, "dz")
    part_b = add_up(part_b, "dy")
    raw0 = add_up([part_a[d] for d in range(4)], "dy")
    raw1 = add_up([part_b[d] for d in range(4)], "dz")

    def panel_select(matrix_row):
        blocks = matrix_row // NB
        place = blocks // 32 * NB + matrix_row % NB
        piece = lower_panels.shape[1]
        mine = (blocks % 32 == rank) & (place // piece == column_rank)
        place = jnp.where(mine, place % piece, -1)
        return (place[:, None] == jnp.arange(piece, dtype=jnp.int32)[None, :]).astype(F32)

    panel_rows = jnp.concatenate([pivot1, NB + index])
    picked = jnp.dot(panel_select(panel_rows), lower_panels[0], precision=HIGHEST)
    picked = lax.psum(picked, ("prow", "pcol"))
    lower_pivot, lower_top = picked[:NB], picked[NB:]

    upper = solve(raw0, raw1, inverses, lower_pivot)
    upper = lax.all_gather(upper, "prow", axis=0).reshape(16, 2, 2 * NB, LANES)

    tops = scatter_tops(matrix, y, z)
    tops = lax.all_gather(tops, "prow", axis=0).reshape(16, 2, 2, NB, LANES)

    pieces = [lower_panels] + [
        lax.ppermute(lower_panels, "pcol", [(i, (i + d) % 4) for i in range(4)]) for d in (1, 2, 3)
    ]
    pieces = jnp.stack(pieces)
    order = (column_rank - jnp.arange(4, dtype=jnp.int32)) % 4
    pieces = pieces[order]
    lower0 = pieces[:, 0].reshape(rows, NB)
    lower1 = pieces[:, 1].reshape(rows, NB)

    takes0 = (pivot0 >= 2 * NB) & ~jnp.any(again, axis=0)
    place0 = jnp.where(takes0, local(pivot0), -1)
    place1 = local(pivot1)
    hit0 = local_row[:, None] == place0[None, :]
    hit1 = local_row[:, None] == place1[None, :]
    moved = (NB + index)[:, None] == pivot0[None, :]
    top1 = jnp.where(
        jnp.any(moved, axis=1),
        jnp.sum(jnp.where(moved, index[None, :], 0), axis=1),
        NB + index,
    )
    to_top = (top1[:, None] == jnp.arange(2 * NB, dtype=jnp.int32)[None, :]).astype(BF16)
    take = jnp.dot(hit1.astype(BF16), to_top, preferred_element_type=F32)
    take = take + jnp.concatenate([hit0, jnp.zeros_like(hit0)], axis=1).astype(F32)
    second = jnp.any(hit1, axis=1)[:, None]
    replaced = second | jnp.any(hit0, axis=1)[:, None]
    lower0 = jnp.where(second, jnp.dot(hit1.astype(F32), lower_top, precision=HIGHEST), lower0)
    lower = -jnp.concatenate([lower0, lower1], axis=1)
    high = lax.reduce_precision(lower, 8, 7)
    low = (lower - high).astype(BF16)
    high = high.astype(BF16)
    take = take.astype(BF16)
    left = jnp.concatenate([high, high, low, take, take], axis=1)
    keep = jnp.where(replaced, 0.0, 1.0).astype(F32)
    return update(rank.reshape(1).astype(jnp.int32), left, keep, matrix, upper, tops)


def solution(mesh):
    placed = (P("prow", "pcol"), P(None, ("prow", "pcol"), None), P(), P())
    return jax.shard_map(
        body, mesh=mesh, in_specs=placed, out_specs=P("prow", "pcol"), check_vma=False
    )
```

time: 630 us -> 446 us (0.71)
  waiting for transfers between devices: 390 us -> 183 us
  Pallas kernels: 0 us -> 176 us
  local copies, waits for them, and re-layouts: 142 us -> 5.48 us
  starting transfers between devices: 0.21 us -> 43.5 us
  matrix products: 38.1 us -> 3.16 us
  blocking collectives: 22.5 us -> 0 us
    pallas_call x0 -> x5, Pallas kernels: none -> 176 us  [the longest x1 129 us: top_parts(): pl.pallas_call(top_parts_kernel, out_shape=tuple((jax.ShapeDtypeStruct((4...]
    reduce_scatter x2 -> x0, waiting for transfers between devices: 150 us -> none  [body(): shared = lax.psum_scatter(picked, 'prow', scatter_dimension=1, tiled=True)]
    psum x2 -> x1, waiting for transfers between devices: 206 us -> 101 us  [body(): picked = lax.psum(picked, ('prow', 'pcol'))]
    scatter x6 -> x0, local copies, waits for them, and re-layouts: 78 us -> none  [the longest x4 52.8 us: body(): updated = updated.at[target].set(old_top, mode='drop')]
    ppermute x0 -> x29, waiting for transfers between devices: none -> 55.1 us  [the longest x12 22.5 us: shift(): return lax.ppermute(value, 'prow', shift_pairs(dy, dz))]
    ppermute x0 -> x29, starting transfers between devices: none -> 43.4 us  [the longest x12 21.2 us: send(): return lax.ppermute(value, 'prow', pairs)]
    dot_general x4 -> x3, matrix products: 38.1 us -> 3.16 us  [the longest x1 1.4 us: body(): take = jnp.dot(hit1.astype(BF16), to_top, preferred_element_type=F32)]
    gather x4 -> x1, local copies, waits for them, and re-layouts: 31.7 us -> 0.65 us  [body(): pieces = pieces[order]]
  transfers between devices with their start and end apart: 6 -> 32, of which waited for: 6 -> 15; matrix products, arithmetic and copies ran while one was open for 13% -> 6% of each run, Pallas kernels for 0% -> 5%
where the time goes in v1:
time: 446 us; the launch traced here: 444 us
  waiting for transfers between devices  183 us (41%)
  Pallas kernels  176 us (39%)
  starting transfers between devices  43.5 us (10%)
  other arithmetic  17.8 us (4%)
  between operations  15.3 us (3%)
  local copies, waits for them, and re-layouts  5.48 us (1%)
    pallas_call x1, Pallas kernels, top_parts(): pl.pallas_call(top_parts_kernel, out_shape=tuple((jax.ShapeDtypeStruct((4...  129 us
    psum x1, waiting for transfers between devices, body(): picked = lax.psum(picked, ('prow', 'pcol'))  101 us
    pallas_call x1, Pallas kernels, update(): pl.pallas_call(update_kernel, out_shape=jax.ShapeDtypeStruct(matrix.shape...  27.3 us
    all_gather x1, waiting for transfers between devices, body(): upper = lax.all_gather(upper, 'prow', axis=0).reshape(16, 2, 2 * NB, LANES)  26.9 us
    ppermute x12, waiting for transfers between devices, shift(): return lax.ppermute(value, 'prow', shift_pairs(dy, dz))  22.5 us
    ppermute x12, starting transfers between devices, send(): return lax.ppermute(value, 'prow', pairs)  21.2 us
    ppermute x12, waiting for transfers between devices, send(): return lax.ppermute(value, 'prow', pairs)  18.4 us
    pallas_call x2, Pallas kernels, pick_rows(): pl.pallas_call(pick_kernel, out_shape=(jax.ShapeDtypeStruct((4, 4, NB, LA...  16.7 us
  transfers between devices with their start and end apart: 32, of which 15 were waited for; matrix products, arithmetic and copies ran while one was open for 6% of the time, Pallas kernels for 5%

profile of v1, /device:TPU:1, one launch (start us, length us, event | category | flops | bytes accessed | tf_op | source)
XLA Modules:
  0.0 444.5 jit_solution(17235320081570948176)
XLA Ops:
  7.4 128.7 %top_parts.1 = (f32[4,2,128,128]{3,2,1,0:T(8,128)}, f32[4,2,128,128]{3,2,1,0:T(8,128)}, f32[4,2,128,128]{3,2,1,0:T(8,128)}, f32[4,2,128,128]{3,2,1,0:T(8,128)}, ...) custom-call(f32[768,4096]{1,0:T(8,128)} %matrix_ref.7), custom_call_target="tpu_custom_call" | custom-call | bytes 8388608 | tf_op jit(solution)/shard_map/top_parts/pallas_call | solution.py:104
  136.1 4.5 %collective-permute-start.17 = (f32[4,2,128,128]{3,2,1,0:T(8,128)}, f32[4,2,128,128]{3,2,1,0:T(8,128)S(1)}, u32[]{:S(2)}, u32[]{:S(2)}) collective-permute-start(f32[4,2,128,128]{3,2,1,0:T(8,128)} %get-tuple-element.22), channel_id=1, source_target_pairs={{0,8},{4,12},{1,9},{5,13},{2,10},{6,14},{3,11},{7,15}} | collective-permute-start | bytes 1572872 | tf_op jit(solution)/shard_map/ppermute | solution.py:125
  140.7 2.8 collective-permute-start.18
  143.5 1.3 collective-permute-start.19
  144.9 1.2 fusion.19
  146.2 1.3 collective-permute-start.23
  147.5 1.3 collective-permute-start.24
  148.9 2.7 collective-permute-done.17
  151.6 1.3 collective-permute-start.25
  152.9 1.6 collective-permute-done.18
  154.5 8.8 %collective-permute-done.19 = f32[4,2,128,128]{3,2,1,0:T(8,128)S(1)} collective-permute-done((f32[4,2,128,128]{3,2,1,0:T(8,128)}, f32[4,2,128,128]{3,2,1,0:T(8,128)S(1)}, u32[]{:S(2)}, u32[]{:S(2)}) %collective-permute-start.19) | collective-permute-done | bytes 524320 | tf_op jit(solution)/shard_map/ppermute | solution.py:125
  163.5 1.4 collective-permute-start.21
  164.9 1.3 collective-permute-start.22
  166.2 1.3 collective-permute-start.20
  167.5 2.9 collective-permute-done.25
  170.6 1.3 collective-permute-start.27
  171.9 2.0 collective-permute-start.28
  173.9 1.3 collective-permute-start.26
  175.2 0.9 collective-permute-done.20
  176.1 1.5 collective-permute-done.26
  177.7 0.7 pad_maximum_fusion.1
  178.5 0.8 compare_reduce_fusion
  179.3 0.8 fusion.23
  180.1 0.6 add_add_fusion
  180.8 1.1 fusion.1.select_ref
  181.9 8.3 %pick_rows.3 = (f32[4,4,256,128]{3,2,1,0:T(8,128)}, f32[4,4,256,128]{3,2,1,0:T(8,128)}) custom-call(s32[3]{0:T(128)} %get-tuple-element.64.place_ref, bf16[512,768]{1,0:T(8,128)(2,1)} %fusion.1.select_ref, f32[768,4096]{1,0:T(8,128)} %matrix_ref.7), custom_call_target="tpu_custom_call" | custom-call | flops 3221225472 | bytes 10485760 | tf_op jit(solution)/shard_map/pick_rows/pallas_call | solution.py:55
  190.2 2.7 collective-permute-start.3
  192.9 8.3 %pick_rows.2 = (f32[4,4,256,128]{3,2,1,0:T(8,128)}, f32[4,4,256,128]{3,2,1,0:T(8,128)}) custom-call(s32[3]{0:T(128)} %get-tuple-element.63.place_ref, bf16[512,768]{1,0:T(8,128)(2,1)} %fusion.1.select_ref, f32[768,4096]{1,0:T(8,128)} %matrix_ref.7), custom_call_target="tpu_custom_call" | custom-call | flops 3221225472 | bytes 10485760 | tf_op jit(solution)/shard_map/pick_rows/pallas_call | solution.py:55
  201.3 3.1 fusion.14
  204.4 2.2 collective-permute-start.4
  206.7 2.3 collective-permute-start.5
  209.0 101.1 %all-reduce.3.cloned.1.call-done = f32[512,256]{1,0:T(8,128)} async-done(((f32[512,256]{1,0:T(8,128)}), f32[512,256]{1,0:T(8,128)}) %all-reduce.3.cloned.1.call-update) | async-done | bytes 524304 | tf_op jit(solution)/shard_map/psum | solution.py:260
  310.1 1.7 slice.177.lower_ref
  311.8 1.5 fusion.7
  313.8 2.9 collective-permute-start.13
  316.7 0.8 collective-permute-start.12
  317.6 1.8 fusion.18
  319.4 0.7 collective-permute-start.7
  320.7 7.5 %collective-permute-done.11 = f32[4,256,128]{2,1,0:T(8,128)S(1)} collective-permute-done((f32[4,256,128]{2,1,0:T(8,128)S(1)}, f32[4,256,128]{2,1,0:T(8,128)S(1)}, u32[]{:S(2)}, u32[]{:S(2)}) %collective-permute-start.11) | collective-permute-done | bytes 524320 | tf_op jit(solution)/shard_map/ppermute | solution.py:33
  328.2 1.3 collective-permute-start.8
  329.4 11.0 %collective-permute-done.13 = f32[4,256,128]{2,1,0:T(8,128)S(1)} collective-permute-done((f32[4,256,128]{2,1,0:T(8,128)S(1)}, f32[4,256,128]{2,1,0:T(8,128)S(1)}, u32[]{:S(2)}, u32[]{:S(2)}) %collective-permute-start.13) | collective-permute-done | bytes 524320 | tf_op jit(solution)/shard_map/ppermute | solution.py:33
  340.4 1.2 fusion.11
  341.9 2.9 collective-permute-start.16
  345.2 0.8 collective-permute-done.9
  346.0 0.7 fusion.36.raw0_ref
  346.7 3.2 collective-permute-done.16
  350.0 0.7 fusion.33.raw1_ref
  350.6 3.4 solve.1
  354.0 2.5 collective-permute-start
  357.0 1.6 collective-permute-start.1
  358.6 0.9 fusion.37
  359.5 0.9 select_n.292.keep_ref
  360.5 3.4 collective-permute-done
  363.9 1.9 collective-permute-done.2
  365.8 8.9 %collective-permute-done.1 = f32[2,192,256]{2,1,0:T(8,128)S(1)} collective-permute-done((f32[2,192,256]{2,1,0:T(8,128)S(1)}, f32[2,192,256]{2,1,0:T(8,128)S(1)}, u32[]{:S(2)}, u32[]{:S(2)}) %collective-permute-start.1) | collective-permute-done | bytes 393248 | tf_op jit(solution)/shard_map/ppermute | solution.py:270
  374.8 0.7 gather_fusion
  375.6 0.9 copy-done.2
  377.0 1.1 constant_dynamic-update-slice_fusion.3
  378.2 1.1 constant_dynamic-update-slice_fusion.2
  379.3 1.1 fusion.2
  380.4 1.4 constant_dynamic-update-slice_fusion.1
  381.8 1.0 constant_dynamic-update-slice_fusion.left_ref
  382.9 26.9 %all-gather.5.cloned.1.call-done = f32[16384,128]{1,0:T(8,128)} async-done(((f32[512,128]{1,0:T(8,128)}), f32[16384,128]{1,0:T(8,128)}) %all-gather.5.cloned.1.call-update) | async-done | bytes 8388624 | tf_op jit(solution)/shard_map/all_gather | solution.py:264
  409.7 27.3 %update.1 = f32[768,4096]{1,0:T(8,128)} custom-call(s32[1]{0:T(128)} %bitcast.rank_ref, bf16[768,2560]{1,0:T(8,128)(2,1)} %constant_dynamic-update-slice_fusion.left_ref, f32[768,1]{1,0:T(8,128)} %select_n.292.keep_ref, f32[768,4096]{1,0:T(8,128)} %matrix_ref.7, f32[16,2,512,128]{3,2,1,0:T(8,128)} %bitcast.118, f32[16,2,2,256,128]{4,3,2,1,0:T(8,128)} %bitcast.117), custom_call_target="tpu_custom_call" | custom-call | flops 16106127360 | bytes 41943040 | tf_op jit(solution)/shard_map/update/pallas_call | solution.py:187
  (71 shorter events, 3.8 us)
Async XLA Ops:
  7.4 137.5 %copy-start.6 = (s32[2,256]{1,0:T(2,128)S(1)}, s32[2,256]{1,0:T(2,128)}, u32[]{:S(2)}) copy-start(s32[2,256]{1,0:T(2,128)} %param.7) | copy-start | bytes 6148
  7.4 137.5 %copy-start.1 = (f32[2,192,256]{2,1,0:T(8,128)S(1)}, f32[2,192,256]{2,1,0:T(8,128)}, u32[]{:S(2)}) copy-start(f32[2,192,256]{2,1,0:T(8,128)} %param.5) | copy-start | bytes 1179652
  7.4 302.7 %all-reduce.3.cloned.1.call-start = ((), (), s32[]{:S(2)}) async-start(), calls=%async_computation | async-start | bytes 1048576 | tf_op jit(solution)/shard_map/psum | solution.py:260
  136.1 27.2 %copy-start.4 = (f32[4,2,128,128]{3,2,1,0:T(8,128)S(1)}, f32[4,2,128,128]{3,2,1,0:T(8,128)}, u32[]{:S(2)}) copy-start(f32[4,2,128,128]{3,2,1,0:T(8,128)} %get-tuple-element.21) | copy-start | bytes 1572868
  136.1 15.5 %collective-permute-start.17 = (f32[4,2,128,128]{3,2,1,0:T(8,128)}, f32[4,2,128,128]{3,2,1,0:T(8,128)S(1)}, u32[]{:S(2)}, u32[]{:S(2)}) collective-permute-start(f32[4,2,128,128]{3,2,1,0:T(8,128)} %get-tuple-element.22), channel_id=1, source_target_pairs={{0,8},{4,12},{1,9},{5,13},{2,10},{6,14},{3,11},{7,15}} | collective-permute-start | bytes 1572872 | tf_op jit(solution)/shard_map/ppermute | solution.py:125
  140.7 13.8 %collective-permute-start.18 = (f32[4,2,128,128]{3,2,1,0:T(8,128)}, f32[4,2,128,128]{3,2,1,0:T(8,128)S(1)}, u32[]{:S(2)}, u32[]{:S(2)}) collective-permute-start(f32[4,2,128,128]{3,2,1,0:T(8,128)} %get-tuple-element.23), channel_id=1, source_target_pairs={{0,24},{4,28},{1,25},{5,29},{2,26},{6,30},{3,27},{7,31}} | collective-permute-start | bytes 1572872 | tf_op jit(solution)/shard_map/ppermute | solution.py:125
  143.5 19.8 %collective-permute-start.19 = (f32[4,2,128,128]{3,2,1,0:T(8,128)}, f32[4,2,128,128]{3,2,1,0:T(8,128)S(1)}, u32[]{:S(2)}, u32[]{:S(2)}) collective-permute-start(f32[4,2,128,128]{3,2,1,0:T(8,128)} %get-tuple-element.24), channel_id=1, source_target_pairs={{0,16},{4,20},{1,17},{5,21},{2,18},{6,22},{3,19},{7,23}} | collective-permute-start | bytes 1572872 | tf_op jit(solution)/shard_map/ppermute | solution.py:125
  146.2 236.7 %all-gather.7.cloned.1.call-start = ((), (), s32[]{:S(2)}) async-start(), calls=%async_computation.2 | async-start | bytes 8650752 | tf_op jit(solution)/shard_map/all_gather | solution.py:267
  146.2 20.0 %collective-permute-start.23 = (f32[4,2,128,128]{3,2,1,0:T(8,128)}, f32[4,2,128,128]{3,2,1,0:T(8,128)S(1)}, u32[]{:S(2)}, u32[]{:S(2)}) collective-permute-start(f32[4,2,128,128]{3,2,1,0:T(8,128)} %get-tuple-element.26), channel_id=1, source_target_pairs={{0,32},{4,36},{1,33},{5,37},{2,34},{6,38},{3,35},{7,39}} | collective-permute-start | bytes 1572872 | tf_op jit(solution)/shard_map/ppermute | solution.py:125
  147.5 20.0 %collective-permute-start.24 = (f32[4,2,128,128]{3,2,1,0:T(8,128)}, f32[4,2,128,128]{3,2,1,0:T(8,128)S(1)}, u32[]{:S(2)}, u32[]{:S(2)}) collective-permute-start(f32[4,2,128,128]{3,2,1,0:T(8,128)} %get-tuple-element.27), channel_id=1, source_target_pairs={{0,96},{4,100},{1,97},{5,101},{2,98},{6,102},{3,99},{7,103}} | collective-permute-start | bytes 1572872 | tf_op jit(solution)/shard_map/ppermute | solution.py:125
  151.6 18.8 %collective-permute-start.25 = (f32[4,2,128,128]{3,2,1,0:T(8,128)}, f32[4,2,128,128]{3,2,1,0:T(8,128)S(1)}, u32[]{:S(2)}, u32[]{:S(2)}) collective-permute-start(f32[4,2,128,128]{3,2,1,0:T(8,128)} %get-tuple-element.28), channel_id=1, source_target_pairs={{0,64},{4,68},{1,65},{5,69},{2,66},{6,70},{3,67},{7,71}} | collective-permute-start | bytes 1572872 | tf_op jit(solution)/shard_map/ppermute | solution.py:125
  163.3 7.1 %copy-start.3 = (f32[4,2,128,128]{3,2,1,0:T(8,128)S(1)}, f32[4,2,128,128]{3,2,1,0:T(8,128)}, u32[]{:S(2)}) copy-start(f32[4,2,128,128]{3,2,1,0:T(8,128)} %get-tuple-element.25) | copy-start | bytes 1572868
  163.5 10.4 %collective-permute-start.21 = (f32[2,128,128]{2,1,0:T(8,128)S(1)}, f32[2,128,128]{2,1,0:T(8,128)S(1)}, u32[]{:S(2)}, u32[]{:S(2)}) collective-permute-start(f32[2,128,128]{2,1,0:T(8,128)S(1)} %get-tuple-element.42), channel_id=1, source_target_pairs={{0,96},{4,100},{8,104},{12,108},{16,112},{20,116},{24,120},{28,124... | collective-permute-start | bytes 393224 | tf_op jit(solution)/shard_map/ppermute | solution.py:125
  164.9 10.3 %collective-permute-start.22 = (f32[2,128,128]{2,1,0:T(8,128)S(1)}, f32[2,128,128]{2,1,0:T(8,128)S(1)}, u32[]{:S(2)}, u32[]{:S(2)}) collective-permute-start(f32[2,128,128]{2,1,0:T(8,128)S(1)} %get-tuple-element.43), channel_id=1, source_target_pairs={{0,64},{4,68},{8,72},{12,76},{16,80},{20,84},{24,88},{28,92},{1,65... | collective-permute-start | bytes 393224 | tf_op jit(solution)/shard_map/ppermute | solution.py:125
  166.2 9.9 %collective-permute-start.20 = (f32[2,128,128]{2,1,0:T(8,128)S(1)}, f32[2,128,128]{2,1,0:T(8,128)S(1)}, u32[]{:S(2)}, u32[]{:S(2)}) collective-permute-start(f32[2,128,128]{2,1,0:T(8,128)S(1)} %get-tuple-element.44), channel_id=1, source_target_pairs={{0,32},{4,36},{8,40},{12,44},{16,48},{20,52},{24,56},{28,60},{1,33... | collective-permute-start | bytes 393224 | tf_op jit(solution)/shard_map/ppermute | solution.py:125
  170.6 5.5 %collective-permute-start.27 = (f32[2,128,128]{2,1,0:T(8,128)S(1)}, f32[2,128,128]{2,1,0:T(8,128)S(1)}, u32[]{:S(2)}, u32[]{:S(2)}) collective-permute-start(f32[2,128,128]{2,1,0:T(8,128)S(1)} %get-tuple-element.45), channel_id=1, source_target_pairs={{0,24},{4,28},{32,56},{36,60},{64,88},{68,92},{96,120},{100,124},{... | collective-permute-start | bytes 393224 | tf_op jit(solution)/shard_map/ppermute | solution.py:125
  171.9 4.2 collective-permute-start.28
  173.9 3.8 collective-permute-start.26
  178.4 231.3 %all-gather.5.cloned.1.call-start = ((), (), s32[]{:S(2)}) async-start(), calls=%async_computation.1 | async-start | bytes 8650752 | tf_op jit(solution)/shard_map/all_gather | solution.py:264
  190.2 11.1 %collective-permute-start.3 = (f32[4,4,256,128]{3,2,1,0:T(8,128)}, f32[4,4,256,128]{3,2,1,0:T(8,128)S(1)}, u32[]{:S(2)}, u32[]{:S(2)}) collective-permute-start(f32[4,4,256,128]{3,2,1,0:T(8,128)} %get-tuple-element.18), channel_id=1, source_target_pairs={{0,4},{4,0},{8,12},{12,8},{16,20},{20,16},{24,28},{28,24},{32,36},... | collective-permute-start | bytes 6291464 | tf_op jit(solution)/shard_map/ppermute | solution.py:234
  192.9 118.9 %collective-permute-start.10 = (f32[4,4,256,128]{3,2,1,0:T(8,128)}, f32[4,4,256,128]{3,2,1,0:T(8,128)S(1)}, u32[]{:S(2)}, u32[]{:S(2)}) collective-permute-start(f32[4,4,256,128]{3,2,1,0:T(8,128)} %get-tuple-element.20), channel_id=1, source_target_pairs={{0,4},{4,0},{8,12},{12,8},{16,20},{20,16},{24,28},{28,24},{32,36},... | collective-permute-start | bytes 6291464 | tf_op jit(solution)/shard_map/ppermute | solution.py:234
  201.3 3.1 copy-start
  204.4 112.4 %collective-permute-start.4 = (f32[4,256,128]{2,1,0:T(8,128)}, f32[4,256,128]{2,1,0:T(8,128)}, u32[]{:S(2)}, u32[]{:S(2)}) collective-permute-start(f32[4,256,128]{2,1,0:T(8,128)} %get-tuple-element.37), channel_id=1, source_target_pairs={{0,8},{4,12},{8,16},{12,20},{16,24},{20,28},{24,0},{28,4},{32,40},... | collective-permute-start | bytes 1572872 | tf_op jit(solution)/shard_map/ppermute | solution.py:33
  206.6 111.0 %collective-permute-start.6 = (f32[4,256,128]{2,1,0:T(8,128)S(1)}, f32[4,256,128]{2,1,0:T(8,128)}, u32[]{:S(2)}, u32[]{:S(2)}) collective-permute-start(f32[4,256,128]{2,1,0:T(8,128)S(1)} %get-tuple-element.38), channel_id=1, source_target_pairs={{0,16},{4,20},{8,24},{12,28},{16,0},{20,4},{24,8},{28,12},{32,48},... | collective-permute-start | bytes 1572872 | tf_op jit(solution)/shard_map/ppermute | solution.py:33
  206.7 110.9 %collective-permute-start.5 = (f32[4,256,128]{2,1,0:T(8,128)S(1)}, f32[4,256,128]{2,1,0:T(8,128)}, u32[]{:S(2)}, u32[]{:S(2)}) collective-permute-start(f32[4,256,128]{2,1,0:T(8,128)S(1)} %get-tuple-element.39), channel_id=1, source_target_pairs={{0,24},{4,28},{8,0},{12,4},{16,8},{20,12},{24,16},{28,20},{32,56},... | collective-permute-start | bytes 1572872 | tf_op jit(solution)/shard_map/ppermute | solution.py:33
  313.3 14.8 %collective-permute-start.11 = (f32[4,256,128]{2,1,0:T(8,128)S(1)}, f32[4,256,128]{2,1,0:T(8,128)S(1)}, u32[]{:S(2)}, u32[]{:S(2)}) collective-permute-start(f32[4,256,128]{2,1,0:T(8,128)S(1)} %get-tuple-element.34), channel_id=1, source_target_pairs={{0,32},{4,36},{8,40},{12,44},{16,48},{20,52},{24,56},{28,60},{32,6... | collective-permute-start | bytes 1572872 | tf_op jit(solution)/shard_map/ppermute | solution.py:33
  313.8 26.6 %collective-permute-start.13 = (f32[4,256,128]{2,1,0:T(8,128)S(1)}, f32[4,256,128]{2,1,0:T(8,128)S(1)}, u32[]{:S(2)}, u32[]{:S(2)}) collective-permute-start(f32[4,256,128]{2,1,0:T(8,128)S(1)} %get-tuple-element.35), channel_id=1, source_target_pairs={{0,64},{4,68},{8,72},{12,76},{16,80},{20,84},{24,88},{28,92},{32,9... | collective-permute-start | bytes 1572872 | tf_op jit(solution)/shard_map/ppermute | solution.py:33
  316.7 23.7 %collective-permute-start.12 = (f32[4,256,128]{2,1,0:T(8,128)S(1)}, f32[4,256,128]{2,1,0:T(8,128)S(1)}, u32[]{:S(2)}, u32[]{:S(2)}) collective-permute-start(f32[4,256,128]{2,1,0:T(8,128)S(1)} %get-tuple-element.36), channel_id=1, source_target_pairs={{0,96},{4,100},{8,104},{12,108},{16,112},{20,116},{24,120},{28,124... | collective-permute-start | bytes 1572872 | tf_op jit(solution)/shard_map/ppermute | solution.py:33
  319.4 25.4 %collective-permute-start.7 = (f32[256,128]{1,0:T(8,128)S(1)}, f32[256,128]{1,0:T(8,128)S(1)}, u32[]{:S(2)}, u32[]{:S(2)}) collective-permute-start(f32[256,128]{1,0:T(8,128)S(1)} %get-tuple-element.51), channel_id=1, source_target_pairs={{0,32},{4,36},{8,40},{12,44},{16,48},{20,52},{24,56},{28,60},{32,6... | collective-permute-start | bytes 393224 | tf_op jit(solution)/shard_map/ppermute | solution.py:33
  320.1 25.9 %collective-permute-start.9 = (f32[256,128]{1,0:T(8,128)S(1)}, f32[256,128]{1,0:T(8,128)S(1)}, u32[]{:S(2)}, u32[]{:S(2)}) collective-permute-start(f32[256,128]{1,0:T(8,128)S(1)} %get-tuple-element.52), channel_id=1, source_target_pairs={{0,64},{4,68},{8,72},{12,76},{16,80},{20,84},{24,88},{28,92},{32,9... | collective-permute-start | bytes 393224 | tf_op jit(solution)/shard_map/ppermute | solution.py:33
  328.2 17.9 %collective-permute-start.8 = (f32[256,128]{1,0:T(8,128)S(1)}, f32[256,128]{1,0:T(8,128)S(1)}, u32[]{:S(2)}, u32[]{:S(2)}) collective-permute-start(f32[256,128]{1,0:T(8,128)S(1)} %get-tuple-element.53), channel_id=1, source_target_pairs={{0,96},{4,100},{8,104},{12,108},{16,112},{20,116},{24,120},{28,124... | collective-permute-start | bytes 393224 | tf_op jit(solution)/shard_map/ppermute | solution.py:33
  341.6 17.0 %copy-start.9 = (pred[256]{0:T(512)(128)(4,1)S(1)}, pred[256]{0:T(512)(128)(4,1)}, u32[]{:S(2)}) copy-start(pred[256]{0:T(512)(128)(4,1)} %get-tuple-element.30) | copy-start | bytes 772
  341.6 5.1 %collective-permute-start.14 = (f32[256,128]{1,0:T(8,128)S(1)}, f32[256,128]{1,0:T(8,128)S(1)}, u32[]{:S(2)}, u32[]{:S(2)}) collective-permute-start(f32[256,128]{1,0:T(8,128)S(1)} %get-tuple-element.48), channel_id=1, source_target_pairs={{0,8},{4,12},{8,16},{12,20},{16,24},{20,28},{24,0},{28,4},{32,40},... | collective-permute-start | bytes 393224 | tf_op jit(solution)/shard_map/ppermute | solution.py:33
  341.9 8.1 %collective-permute-start.16 = (f32[256,128]{1,0:T(8,128)S(1)}, f32[256,128]{1,0:T(8,128)S(1)}, u32[]{:S(2)}, u32[]{:S(2)}) collective-permute-start(f32[256,128]{1,0:T(8,128)S(1)} %get-tuple-element.49), channel_id=1, source_target_pairs={{0,16},{4,20},{8,24},{12,28},{16,0},{20,4},{24,8},{28,12},{32,48},... | collective-permute-start | bytes 393224 | tf_op jit(solution)/shard_map/ppermute | solution.py:33
  344.8 5.2 %collective-permute-start.15 = (f32[256,128]{1,0:T(8,128)S(1)}, f32[256,128]{1,0:T(8,128)S(1)}, u32[]{:S(2)}, u32[]{:S(2)}) collective-permute-start(f32[256,128]{1,0:T(8,128)S(1)} %get-tuple-element.50), channel_id=1, source_target_pairs={{0,24},{4,28},{8,0},{12,4},{16,8},{20,12},{24,16},{28,20},{32,56},... | collective-permute-start | bytes 393224 | tf_op jit(solution)/shard_map/ppermute | solution.py:33
  346.7 13.7 %copy-start.7 = (s32[256]{0:T(256)S(1)}, s32[256]{0:T(256)}, u32[]{:S(2)}) copy-start(s32[256]{0:T(256)} %get-tuple-element.32) | copy-start | bytes 3076
  346.7 13.7 %copy-start.8 = (pred[256]{0:T(512)(128)(4,1)S(1)}, pred[256]{0:T(512)(128)(4,1)}, u32[]{:S(2)}) copy-start(pred[256]{0:T(512)(128)(4,1)} %get-tuple-element.33) | copy-start | bytes 772
  354.0 9.8 %collective-permute-start = (f32[2,192,256]{2,1,0:T(8,128)S(1)}, f32[2,192,256]{2,1,0:T(8,128)S(1)}, u32[]{:S(2)}, u32[]{:S(2)}) collective-permute-start(f32[2,192,256]{2,1,0:T(8,128)S(1)} %copy-done.1), channel_id=1, source_target_pairs={{0,1},{1,2},{2,3},{3,0},{4,5},{5,6},{6,7},{7,4},{8,9},{9,10},{10,1... | collective-permute-start | bytes 1179656 | tf_op jit(solution)/shard_map/ppermute | solution.py:270
  356.5 9.3 %collective-permute-start.2 = (f32[2,192,256]{2,1,0:T(8,128)S(1)}, f32[2,192,256]{2,1,0:T(8,128)S(1)}, u32[]{:S(2)}, u32[]{:S(2)}) collective-permute-start(f32[2,192,256]{2,1,0:T(8,128)S(1)} %copy-done.1), channel_id=1, source_target_pairs={{0,3},{1,0},{2,1},{3,2},{4,7},{5,4},{6,5},{7,6},{8,11},{9,8},{10,9... | collective-permute-start | bytes 1179656 | tf_op jit(solution)/shard_map/ppermute | solution.py:270
  357.0 17.7 %collective-permute-start.1 = (f32[2,192,256]{2,1,0:T(8,128)S(1)}, f32[2,192,256]{2,1,0:T(8,128)S(1)}, u32[]{:S(2)}, u32[]{:S(2)}) collective-permute-start(f32[2,192,256]{2,1,0:T(8,128)S(1)} %copy-done.1), channel_id=1, source_target_pairs={{0,2},{1,3},{2,0},{3,1},{4,6},{5,7},{6,4},{7,5},{8,10},{9,11},{10,... | collective-permute-start | bytes 1179656 | tf_op jit(solution)/shard_map/ppermute | solution.py:270
  375.4 1.1 copy-start.2
  379.3 1.2 copy-start.5
Sparse Core Ops, SparseCore 0:
  146.3 163.7 all-reduce.2
Sparse Core Ops, SparseCore 1:
  178.5 71.6 all-gather.6
  354.1 55.6 all-gather.4

commit v2 on v0

v2 whole, which is shorter than its diff:
```python
import jax
import jax.numpy as jnp
from jax import lax
from jax.experimental import pallas as pl
from jax.experimental.pallas import tpu as pltpu
from jax.sharding import PartitionSpec as P

F32 = jnp.float32
BF16 = jnp.bfloat16
HIGHEST = lax.Precision.HIGHEST
NB = 256
LANES = 128
SHARE = 2 * NB + 32
VMEM_LIMIT = 56 * 1024 * 1024


def rank_of(y, z, core):
    return ((y % 4) * 4 + z % 4) * 2 + core


def moved(y, z, core, one, two):
    return (y + two, z + one, core) if core == 0 else (y + one, z + two, core)


def send(value, one=0, two=0, only=lambda one, two: True):
    pairs = []
    for y in range(4):
        for z in range(4):
            for core in range(2):
                at = (z, y) if core == 0 else (y, z)
                if only(*at):
                    pairs.append((rank_of(y, z, core), rank_of(*moved(y, z, core, one, two))))
    return lax.ppermute(value, "prow", pairs)


def swap_cores(value):
    return lax.ppermute(value, "prow", [(rank, rank ^ 1) for rank in range(32)])


def split_two(value):
    high = value.astype(BF16)
    low = (value - high.astype(F32)).astype(BF16)
    return high, low


def exact_dot(a, b):
    return jnp.dot(a, b, precision=HIGHEST, preferred_element_type=F32)


def chip_at(place, one, two):
    by_z = (place[1] + two) % 4 * 4 + (place[2] + one) % 4
    by_y = (place[1] + one) % 4 * 4 + (place[2] + two) % 4
    return jnp.where(place[0] == 0, by_z, by_y)


def pick_kernel(place_ref, select_ref, *refs):
    extras, blocks, out_ref = refs[:4], refs[4:8], refs[8]
    high, low = split_two(jnp.concatenate([block[...] for block in blocks], axis=1))
    select = select_ref[...]
    rows = jnp.dot(select, high, preferred_element_type=F32)
    rows = rows + jnp.dot(select, low, preferred_element_type=F32)
    for two in range(4):
        out_ref[0, two, : 2 * NB] = rows[:, two * LANES : (two + 1) * LANES]
        out_ref[0, two, 2 * NB :] = extras[two][0]


def pick_rows(place, select, extra, matrix):
    def share(two):
        return lambda i, place: chip_at(place, i, two) * 2 + place[0]

    def columns(two):
        return pl.BlockSpec((matrix.shape[0], LANES), lambda i, place: (0, share(two)(i, place)))

    def extras(two):
        return pl.BlockSpec((1, 32, LANES), lambda i, place: (share(two)(i, place), 0, 0))

    return pl.pallas_call(
        pick_kernel,
        out_shape=jax.ShapeDtypeStruct((4, 4, SHARE, LANES), F32),
        grid_spec=pltpu.PrefetchScalarGridSpec(
            num_scalar_prefetch=1,
            grid=(4,),
            in_specs=[pl.BlockSpec(select.shape, lambda i, place: (0, 0))]
            + [extras(two) for two in range(4)]
            + [columns(two) for two in range(4)],
            out_specs=pl.BlockSpec((1, 4, SHARE, LANES), lambda i, place: (i, 0, 0, 0)),
        ),
        compiler_params=pltpu.CompilerParams(vmem_limit_bytes=VMEM_LIMIT),
        cost_estimate=pl.CostEstimate(
            flops=2 * 2 * 512 * 768 * 2048, bytes_accessed=10 << 20, transcendentals=0
        ),
        name="pick_rows",
    )(place, select, *([extra] * 4), *([matrix] * 4))


def cut_kernel(place_ref, *refs):
    blocks, outs = refs[:4], refs[4:]
    for one in range(4):

        @pl.when(pl.program_id(0) == one)
        def _(one=one):
            for two in range(4):
                outs[one][two] = blocks[two][...]


def cut_top(place, matrix):
    def block(two):
        return pl.BlockSpec((NB, 2 * LANES), lambda i, place: (0, chip_at(place, i, two)))

    return pl.pallas_call(
        cut_kernel,
        out_shape=tuple(jax.ShapeDtypeStruct((4, NB, 2 * LANES), F32) for _ in range(4)),
        grid_spec=pltpu.PrefetchScalarGridSpec(
            num_scalar_prefetch=1,
            grid=(4,),
            in_specs=[block(two) for two in range(4)],
            out_specs=tuple(
                pl.BlockSpec((4, NB, 2 * LANES), lambda i, place: (0, 0, 0)) for _ in range(4)
            ),
        ),
        compiler_params=pltpu.CompilerParams(vmem_limit_bytes=VMEM_LIMIT),
        cost_estimate=pl.CostEstimate(flops=0, bytes_accessed=8 << 20, transcendentals=0),
        name="cut_top",
    )(place, *([matrix] * 4))


def solve_kernel(raw_ref, inverse_ref, out_ref):
    out_ref[:NB] = exact_dot(inverse_ref[0], raw_ref[:NB])
    out_ref[NB : 2 * NB] = exact_dot(inverse_ref[1], raw_ref[NB : 2 * NB])
    out_ref[2 * NB :] = raw_ref[2 * NB :]


def solve(raw, inverses):
    return pl.pallas_call(
        solve_kernel,
        out_shape=jax.ShapeDtypeStruct((SHARE, LANES), F32),
        cost_estimate=pl.CostEstimate(
            flops=6 * 2 * 2 * 256 * 256 * 128, bytes_accessed=1 << 20, transcendentals=0
        ),
        name="solve",
    )(raw, inverses)


def update_kernel(
    place_ref, keep_ref, take_ref, hit_ref, lower_ref, inverse_ref,
    matrix_ref, top_ref, *refs,
):
    pieces, extras = refs[:16], refs[16:32]
    out_ref, left_ref, upper_ref, flat_ref = refs[32:]
    core, rank = place_ref[0], place_ref[3]
    step = pl.program_id(0)

    @pl.when(step == 0)
    def _():
        for side in range(2):
            for turn in range(4):
                for inner in range(4):
                    one, two = (turn, inner) if side == 0 else (inner, turn)
                    owner = chip_at(place_ref, one, two) * 2 + (core + side) % 2
                    start = pl.multiple_of(owner * 32, 32)
                    slot = side * 8 + turn * 2 + inner // 2
                    flat_ref[pl.ds(start, 32)] = extras[slot][inner % 2]
        pivot_rows = jnp.concatenate([flat_ref[:NB], flat_ref[2 * NB : 3 * NB]], axis=1)
        top_rows = jnp.concatenate([flat_ref[NB : 2 * NB], flat_ref[3 * NB :]], axis=1)
        weight = exact_dot(inverse_ref[1], pivot_rows)
        hit = hit_ref[...].astype(F32)
        swapped = jnp.max(hit, axis=1, keepdims=True) > 0.0
        lower0 = jnp.where(swapped, exact_dot(hit, top_rows), lower_ref[0])
        lower1 = lower_ref[1]
        lower0 = lower0 - exact_dot(lower1, weight)
        at_second = rank == 1
        lower0 = jnp.concatenate([jnp.where(at_second, weight, lower0[:NB]), lower0[NB:]], axis=0)
        lower1 = jnp.concatenate([jnp.where(at_second, 0.0, lower1[:NB]), lower1[NB:]], axis=0)
        high, low = split_two(-jnp.concatenate([lower0, lower1], axis=1))
        take = take_ref[...]
        for i, part in enumerate((high, high, low, take, take)):
            left_ref[:, i * 2 * NB : (i + 1) * 2 * NB] = part

    for side, turn, inner in ((0, step // 4, step % 4), (1, step % 4, step // 4)):
        lanes = pl.ds(pl.multiple_of((core + side) % 2 * LANES, LANES), LANES)
        for slot in range(8):

            @pl.when((turn == slot // 2) & (inner // 2 == slot % 2))
            def _(slot=slot, side=side, lanes=lanes):
                upper_ref[:, lanes] = pieces[side * 8 + slot][0, : 2 * NB]

    upper = upper_ref[...]
    tops = jnp.concatenate([top_ref[0, 0], top_ref[0, 1]], axis=0)
    upper_high, upper_low = split_two(upper)
    top_high, top_low = split_two(tops)
    right = jnp.concatenate([upper_high, upper_low, upper_high, top_high, top_low], axis=0)
    total = jnp.dot(left_ref[...], right, preferred_element_type=F32)
    out_ref[...] = matrix_ref[...] * keep_ref[...] + total

    @pl.when(rank == 0)
    def _():
        out_ref[:NB] = upper[:NB]

    @pl.when(rank == 1)
    def _():
        out_ref[:NB] = out_ref[:NB] + upper[NB:]


def update(place, keep, take, hit, lower, inverse, matrix, tops, pieces):
    rows, columns = matrix.shape
    width = 2 * LANES

    def whole(array):
        return pl.BlockSpec(array.shape, lambda i, place: (0,) * array.ndim)

    def chip(i, place):
        return chip_at(place, i // 4, i % 4)

    def piece_spec(side, slot):
        def own(i, place):
            return (jnp.clip(i - 2 * slot, 0, 1), 0, 0)

        def other(i, place):
            return (jnp.clip(i // 4 - slot % 2 * 2, 0, 1), 0, 0)

        return pl.BlockSpec((1, SHARE, LANES), other if side else own)

    extra_spec = pl.BlockSpec((2, 32, LANES), lambda i, place: (0, 16, 0))
    pieces = list(pieces)
    return pl.pallas_call(
        update_kernel,
        out_shape=jax.ShapeDtypeStruct(matrix.shape, F32),
        grid_spec=pltpu.PrefetchScalarGridSpec(
            num_scalar_prefetch=1,
            grid=(columns // width,),
            in_specs=[whole(a) for a in (keep, take, hit, lower, inverse)]
            + [
                pl.BlockSpec((rows, width), lambda i, place: (0, chip(i, place))),
                pl.BlockSpec((1, 2, NB, width), lambda i, place: (chip(i, place), 0, 0, 0)),
            ]
            + [piece_spec(side, slot) for side in range(2) for slot in range(8)]
            + [extra_spec] * 16,
            out_specs=pl.BlockSpec((rows, width), lambda i, place: (0, chip(i, place))),
            scratch_shapes=[
                pltpu.VMEM((rows, 10 * NB), BF16),
                pltpu.VMEM((2 * NB, width), F32),
                pltpu.VMEM((4 * NB, LANES), F32),
            ],
        ),
        compiler_params=pltpu.CompilerParams(vmem_limit_bytes=VMEM_LIMIT),
        cost_estimate=pl.CostEstimate(
            flops=2 * rows * columns * 10 * NB, bytes_accessed=40 << 20, transcendentals=0
        ),
        name="update",
    )(place, keep, take, hit, lower, inverse, matrix, tops, *pieces, *pieces)


def body(matrix, lower_panels, inverses, pivots):
    rank = lax.axis_index("prow")
    column_rank = lax.axis_index("pcol")
    y, z, core = rank // 8, rank // 2 % 4, rank % 2
    first = jnp.where(core == 0, z, y)
    second = jnp.where(core == 0, y, z)
    rows = matrix.shape[0]
    index = jnp.arange(NB, dtype=jnp.int32)
    place = jnp.stack([core, y, z, rank]).astype(jnp.int32)
    other_place = jnp.stack([1 - core, y, z, rank]).astype(jnp.int32)

    panel = lower_panels[0]
    far = [lax.ppermute(panel, "pcol", [(i, (i - d) % 4) for i in range(4)]) for d in (1, 2, 3)]
    panel = jnp.concatenate([panel] + far)

    top_parts = cut_top(place, matrix)
    top_got = [
        send(top_parts[d], one=d, only=lambda one, two: one == 0 and two == 0) for d in (2, 1, 3)
    ]

    pivot0, pivot1 = pivots[0], pivots[1]
    again = pivot1[:, None] == pivot0[None, :]
    from_top = jnp.any(again, axis=1)
    source1 = jnp.where(from_top, jnp.sum(jnp.where(again, index[None, :], 0), axis=1), pivot1)
    sources = jnp.concatenate([pivot0, source1])

    def local(matrix_row):
        blocks = matrix_row // NB
        where = blocks // 32 * NB + matrix_row % NB
        return jnp.where(blocks % 32 == rank, where, -1)

    local_row = jnp.arange(rows, dtype=jnp.int32)
    select = (local(sources)[:, None] == local_row[None, :]).astype(BF16)

    panel_rows = jnp.concatenate([pivot1, NB + index])
    piece = lower_panels.shape[1]
    where = local(panel_rows)
    away = (where // piece - column_rank) % 4 * piece + where % piece
    where = jnp.where(where >= 0, away, -1)
    extra = exact_dot((where[:, None] == local_row[None, :]).astype(F32), panel)
    extra = jnp.concatenate([extra[:, :LANES], extra[:, LANES:]], axis=0).reshape(32, 32, LANES)

    sent = pick_rows(other_place, select, extra, matrix)
    other = swap_cores(sent)
    own_place, _ = lax.optimization_barrier((place, sent))
    kept = pick_rows(own_place, select, extra, matrix)
    part = [kept[d] + other[d] for d in range(4)]
    ahead = send(part[2][:2], one=1)
    behind = send(part[2][2:], one=3)
    part[1] = jnp.concatenate([part[1][:2] + ahead, part[1][2:]])
    part[3] = jnp.concatenate([part[3][:2], part[3][2:] + behind])
    part = part[0] + send(part[1], one=1) + send(part[3], one=3)
    top_got, _ = lax.optimization_barrier((top_got, kept))
    top_held = jnp.where(first == 0, top_parts[0], top_got[0] + top_got[1] + top_got[2])
    top_got = [send(top_held[d], two=d, only=lambda one, two: two == 0) for d in (2, 1, 3)]
    top_share = jnp.where(second == 0, top_held[0], top_got[0] + top_got[1] + top_got[2])
    top_share, part = lax.optimization_barrier((top_share, part))
    tops = lax.all_gather(top_share, "prow", axis=0).reshape(16, 2, NB, 2 * LANES)

    lower = lax.all_gather(lower_panels, "pcol", axis=1, tiled=True)

    takes0 = (pivot0 >= 2 * NB) & ~jnp.any(again, axis=0)
    place0 = jnp.where(takes0, local(pivot0), -1)
    hit0 = local_row[:, None] == place0[None, :]
    hit1 = local_row[:, None] == local(pivot1)[None, :]
    shifted = (NB + index)[:, None] == pivot0[None, :]
    top1 = jnp.where(
        jnp.any(shifted, axis=1),
        jnp.sum(jnp.where(shifted, index[None, :], 0), axis=1),
        NB + index,
    )
    to_top = (top1[:, None] == jnp.arange(2 * NB, dtype=jnp.int32)[None, :]).astype(BF16)
    hit1 = hit1.astype(BF16)
    take = jnp.dot(hit1, to_top, preferred_element_type=F32)
    take = take + jnp.concatenate([hit0, jnp.zeros_like(hit0)], axis=1).astype(F32)
    replaced = jnp.any(hit1 > 0, axis=1) | jnp.any(hit0, axis=1)
    replaced = replaced | ((rank == 1) & (local_row < NB))
    keep = jnp.where(replaced, 0.0, 1.0).astype(F32)[:, None]
    take = take.astype(BF16)

    raw = part[0]
    for d in (2, 1, 3):
        raw = raw + send(part[d], two=d)

    raw, keep, take, hit1, lower = lax.optimization_barrier((raw, keep, take, hit1, lower))
    share = solve(raw, inverses)

    near = {d: send(share, two=4 - d) for d in (1, 2, 3)}
    low = jnp.stack([share, near[1]])
    high = jnp.stack([near[2], near[3]])
    low_before, high_after = send(low, one=1), send(high, one=3)
    high_before, low_after = send(high, one=1), send(low, one=3)
    low_across, high_across = send(low_before, one=1), send(high_after, one=3)
    pieces = [
        low, high, low_after, high_after, low_across, high_across, low_before, high_before
    ]
    pieces = pieces + [swap_cores(value) for value in pieces]
    return update(place, keep, take, hit1, lower, inverses, matrix, tops, pieces)


def solution(mesh):
    placed = (P("prow", "pcol"), P(None, ("prow", "pcol"), None), P(), P())
    return jax.shard_map(
        body, mesh=mesh, in_specs=placed, out_specs=P("prow", "pcol"), check_vma=False
    )
```

time: 630 us -> 220 us (0.35)
  waiting for transfers between devices: 390 us -> 56.9 us
  local copies, waits for them, and re-layouts: 142 us -> 5.9 us
  Pallas kernels: 0 us -> 63.4 us
  starting transfers between devices: 0.21 us -> 56.9 us
  matrix products: 38.1 us -> 2.32 us
  blocking collectives: 22.5 us -> 0 us
    psum x2 -> x0, waiting for transfers between devices: 206 us -> none  [from_root(): return lax.psum(kept, axis)]
    reduce_scatter x2 -> x0, waiting for transfers between devices: 150 us -> none  [body(): shared = lax.psum_scatter(picked, 'prow', scatter_dimension=1, tiled=True)]
    scatter x6 -> x0, local copies, waits for them, and re-layouts: 78 us -> none  [the longest x4 52.8 us: body(): updated = updated.at[target].set(old_top, mode='drop')]
    pallas_call x0 -> x5, Pallas kernels: none -> 63.4 us  [the longest x1 37.5 us: update(): pl.pallas_call(update_kernel, out_shape=jax.ShapeDtypeStruct(matrix.shape...]
    ppermute x0 -> x34, waiting for transfers between devices: none -> 56.9 us  [the longest x22 52.7 us: send(): return lax.ppermute(value, 'prow', pairs)]
    ppermute x0 -> x34, starting transfers between devices: none -> 56.8 us  [the longest x22 35.8 us: send(): return lax.ppermute(value, 'prow', pairs)]
    dot_general x4 -> x2, matrix products: 38.1 us -> 2.32 us  [the longest x1 1.38 us: body(): take = jnp.dot(hit1, to_top, preferred_element_type=F32)]
    all_gather x2, waiting for transfers between devices: 33.5 us -> 0.01 us  [the longest x1 0.01 us: body(): lower = lax.all_gather(lower_panels, 'pcol', axis=1, tiled=True)]
  transfers between devices with their start and end apart: 6 -> 36, of which waited for: 6 -> 15; matrix products, arithmetic and copies ran while one was open for 13% -> 11% of each run, Pallas kernels for 0% -> 8%
where the time goes in v2:
time: 220 us; the launch traced here: 219 us
  Pallas kernels  63.4 us (29%)
  starting transfers between devices  56.9 us (26%)
  waiting for transfers between devices  56.9 us (26%)
  other arithmetic  19.8 us (9%)
  between operations  13.8 us (6%)
  local copies, waits for them, and re-layouts  5.9 us (3%)
  matrix products  2.32 us (1%)
    ppermute x22, waiting for transfers between devices, send(): return lax.ppermute(value, 'prow', pairs)  52.7 us
    pallas_call x1, Pallas kernels, update(): pl.pallas_call(update_kernel, out_shape=jax.ShapeDtypeStruct(matrix.shape...  37.5 us
    ppermute x22, starting transfers between devices, send(): return lax.ppermute(value, 'prow', pairs)  35.8 us
    pallas_call x2, Pallas kernels, pick_rows(): pl.pallas_call(pick_kernel, out_shape=jax.ShapeDtypeStruct((4, 4, SHARE,...  17.6 us
    ppermute x9, starting transfers between devices, swap_cores(): return lax.ppermute(value, 'prow', [(rank, rank ^ 1) for rank in range(32)])  15.3 us
    pallas_call x1, Pallas kernels, cut_top(): pl.pallas_call(cut_kernel, out_shape=tuple((jax.ShapeDtypeStruct((4, NB,...  5.91 us
    ppermute x3, starting transfers between devices, body(): lax.ppermute(panel, 'pcol', [(i, (i - d) % 4) for i in range(4)])  5.71 us
  transfers between devices with their start and end apart: 36, of which 15 were waited for; matrix products, arithmetic and copies ran while one was open for 11% of the time, Pallas kernels for 8%

profile of v2, /device:TPU:1, one launch (start us, length us, event | category | flops | bytes accessed | tf_op | source)
XLA Modules:
  0.0 219.1 jit_solution(9862045984019690014)
XLA Ops:
  6.5 0.9 slice_bitcast_fusion.13
  7.5 2.1 collective-permute-start.5
  9.6 2.5 %collective-permute-start.4 = (f32[192,256]{1,0:T(8,128)S(1)}, f32[192,256]{1,0:T(8,128)S(1)}, u32[]{:S(2)}, u32[]{:S(2)}) collective-permute-start(f32[192,256]{1,0:T(8,128)S(1)} %slice_bitcast_fusion.13), channel_id=1, source_target_pairs={{0,2},{1,3},{2,0},{3,1},{4,6},{5,7},{6,4},{7,5},{8,10},{9,11},{10,... | collective-permute-start | bytes 589832 | tf_op jit(solution)/shard_map/ppermute | solution.py:265
  12.0 1.2 collective-permute-start.3
  13.2 0.8 fusion.51
  15.2 1.1 fusion.select_ref
  16.4 4.2 %collective-permute-done.4 = f32[192,256]{1,0:T(8,128)S(1)} collective-permute-done((f32[192,256]{1,0:T(8,128)S(1)}, f32[192,256]{1,0:T(8,128)S(1)}, u32[]{:S(2)}, u32[]{:S(2)}) %collective-permute-start.4) | collective-permute-done | bytes 196640 | tf_op jit(solution)/shard_map/ppermute | solution.py:265
  20.6 0.9 fusion.1
  21.6 0.8 pad_maximum_fusion.4
  22.4 8.8 %pick_rows.2 = f32[4,4,544,128]{3,2,1,0:T(8,128)} custom-call(s32[4]{0:T(128)} %add_add_fusion.1.place_ref, bf16[512,768]{1,0:T(8,128)(2,1)} %fusion.select_ref, f32[32,32,128]{2,1,0:T(8,128)} %bitcast.61, f32[32,32,128]{2,1,0:T(8,128)} %bitcast.62, f32[32,32,128]{2,1,0:T(8,128)} %bitcast.63, f32[32,32,128]{2,1,0:T(8,128)} %bitcast.64, ...), custom_call_target="tpu_custom_call" | custom-call | flops 3221225472 | bytes 10485760 | tf_op jit(solution)/shard_map/pick_rows/pallas_call | solution.py:77
  31.2 1.5 collective-permute-start.9
  33.3 5.9 %cut_top.1 = (f32[4,256,256]{2,1,0:T(8,128)}, f32[4,256,256]{2,1,0:T(8,128)}, f32[4,256,256]{2,1,0:T(8,128)}, f32[4,256,256]{2,1,0:T(8,128)}) custom-call(s32[4]{0:T(128)} %add_add_fusion.place_ref, f32[768,4096]{1,0:T(8,128)} %matrix_ref.1, f32[768,4096]{1,0:T(8,128)} %matrix_ref.1, f32[768,4096]{1,0:T(8,128)} %matrix_ref.1, f32[768,4096]{1,0:T(8,128)} %matrix_ref.1), custom_call_target="tpu_custom_call" | custom-call | bytes 8388608 | tf_op jit(solution)/shard_map/cut_top/pallas_call | solution.py:110
  39.2 4.9 %collective-permute-start = (f32[4,256,256]{2,1,0:T(8,128)}, f32[4,256,256]{2,1,0:T(8,128)S(1)}, u32[]{:S(2)}, u32[]{:S(2)}) collective-permute-start(f32[4,256,256]{2,1,0:T(8,128)} %get-tuple-element.21), channel_id=1, source_target_pairs={{0,16},{4,68},{1,17},{5,69},{2,18},{6,70},{3,19},{7,71}} | collective-permute-start | bytes 3145736 | tf_op jit(solution)/shard_map/ppermute | solution.py:33
  44.1 2.3 %collective-permute-start.1 = (f32[4,256,256]{2,1,0:T(8,128)}, f32[4,256,256]{2,1,0:T(8,128)}, u32[]{:S(2)}, u32[]{:S(2)}) collective-permute-start(f32[4,256,256]{2,1,0:T(8,128)} %get-tuple-element.22), channel_id=1, source_target_pairs={{0,8},{4,36},{1,9},{5,37},{2,10},{6,38},{3,11},{7,39}} | collective-permute-start | bytes 3145736 | tf_op jit(solution)/shard_map/ppermute | solution.py:33
  46.4 2.3 %collective-permute-start.2 = (f32[4,256,256]{2,1,0:T(8,128)}, f32[4,256,256]{2,1,0:T(8,128)}, u32[]{:S(2)}, u32[]{:S(2)}) collective-permute-start(f32[4,256,256]{2,1,0:T(8,128)} %get-tuple-element.23), channel_id=1, source_target_pairs={{0,24},{4,100},{1,25},{5,101},{2,26},{6,102},{3,27},{7,103}} | collective-permute-start | bytes 3145736 | tf_op jit(solution)/shard_map/ppermute | solution.py:33
  48.7 8.8 %pick_rows.3 = f32[4,4,544,128]{3,2,1,0:T(8,128)} custom-call(s32[4]{0:T(128)} %add_add_fusion.place_ref, bf16[512,768]{1,0:T(8,128)(2,1)} %fusion.select_ref, f32[32,32,128]{2,1,0:T(8,128)} %bitcast.65, f32[32,32,128]{2,1,0:T(8,128)} %bitcast.66, f32[32,32,128]{2,1,0:T(8,128)} %bitcast.67, f32[32,32,128]{2,1,0:T(8,128)} %bitcast.68, ...), custom_call_target="tpu_custom_call" | custom-call | flops 3221225472 | bytes 10485760 | tf_op jit(solution)/shard_map/pick_rows/pallas_call | solution.py:77
  57.5 3.9 %slice_add_fusion.2 = (f32[1,4,544,128]{3,2,1,0:T(8,128)S(1)}, f32[1,4,544,128]{3,2,1,0:T(8,128)S(1)}, f32[1,4,544,128]{3,2,1,0:T(8,128)S(1)}) fusion(f32[4,4,544,128]{3,2,1,0:T(8,128)S(1)} %collective-permute-done.9, f32[4,4,544,128]{3,2,1,0:T(8,128)} %pick_rows.3), kind=kLoop, calls=%fused_computation.7 | loop fusion | flops 835584 | bytes 10027008 | tf_op jit(solution)/shard_map/add | solution.py:299
  61.4 1.1 slice_bitcast_fusion.4
  62.6 4.7 %collective-permute-done.1 = f32[4,256,256]{2,1,0:T(8,128)} collective-permute-done((f32[4,256,256]{2,1,0:T(8,128)}, f32[4,256,256]{2,1,0:T(8,128)}, u32[]{:S(2)}, u32[]{:S(2)}) %collective-permute-start.1) | collective-permute-done | bytes 1048608 | tf_op jit(solution)/shard_map/ppermute | solution.py:33
  67.3 2.1 collective-permute-start.10
  69.5 2.0 collective-permute-done.12
  71.5 1.1 fusion.14
  72.7 1.2 collective-permute-start.13
  73.9 3.7 %collective-permute-done.10 = f32[2,544,128]{2,1,0:T(8,128)S(1)} collective-permute-done((f32[2,544,128]{2,1,0:T(8,128)}, f32[2,544,128]{2,1,0:T(8,128)S(1)}, u32[]{:S(2)}, u32[]{:S(2)}) %collective-permute-start.10) | collective-permute-done | bytes 557088 | tf_op jit(solution)/shard_map/ppermute | solution.py:33
  77.6 1.1 pad_maximum_fusion
  78.7 0.9 collective-permute-start.11
  79.6 1.9 add_select_fusion
  81.5 1.0 slice_bitcast_fusion.10
  82.5 2.0 collective-permute-start.7
  84.5 2.0 collective-permute-start.8
  86.5 2.0 collective-permute-start.6
  88.4 1.8 collective-permute-done.7
  90.2 1.1 collective-permute-done.8
  91.3 4.5 %collective-permute-done.6 = f32[256,256]{1,0:T(8,128)} collective-permute-done((f32[256,256]{1,0:T(8,128)}, f32[256,256]{1,0:T(8,128)}, u32[]{:S(2)}, u32[]{:S(2)}) %collective-permute-start.6) | collective-permute-done | bytes 262176 | tf_op jit(solution)/shard_map/ppermute | solution.py:33
  95.9 1.9 fusion.24
  97.8 2.1 fusion.4
  100.2 0.9 fusion.12
  101.2 3.5 %collective-permute-start.14 = (f32[544,128]{1,0:T(8,128)S(1)}, f32[544,128]{1,0:T(8,128)S(1)}, u32[]{:S(2)}, u32[]{:S(2)}) collective-permute-start(f32[544,128]{1,0:T(8,128)S(1)} %get-tuple-element.43), channel_id=1, source_target_pairs={{0,64},{4,20},{8,72},{12,28},{16,80},{20,4},{24,88},{28,12},{32,96... | collective-permute-start | bytes 835592 | tf_op jit(solution)/shard_map/ppermute | solution.py:33
  104.7 1.5 collective-permute-start.15
  106.1 0.9 fusion.19.keep_ref
  107.1 1.4 add_convert_fusion.take_ref
  108.6 1.7 collective-permute-done.16
  110.4 1.5 collective-permute-done.15
  111.9 0.8 fusion.21.raw_ref
  112.6 2.4 %solve.1 = f32[544,128]{1,0:T(8,128)} custom-call(f32[544,128]{1,0:T(8,128)} %fusion.21.raw_ref, f32[2,256,256]{2,1,0:T(8,128)} %inverse_ref.3), custom_call_target="tpu_custom_call" | custom-call | flops 201326592 | bytes 1048576 | tf_op jit(solution)/shard_map/solve/pallas_call | solution.py:134
  115.4 1.2 collective-permute-start.19
  116.6 2.9 %collective-permute-start.18 = (f32[544,128]{1,0:T(8,128)}, f32[544,128]{1,0:T(8,128)S(1)}, u32[]{:S(2)}, u32[]{:S(2)}) collective-permute-start(f32[544,128]{1,0:T(8,128)} %solve.1), channel_id=1, source_target_pairs={{0,64},{4,20},{8,72},{12,28},{16,80},{20,4},{24,88},{28,12},{32,96... | collective-permute-start | bytes 835592 | tf_op jit(solution)/shard_map/ppermute | solution.py:33
  119.4 3.4 %collective-permute-done.17 = f32[544,128]{1,0:T(8,128)S(1)} collective-permute-done((f32[544,128]{1,0:T(8,128)}, f32[544,128]{1,0:T(8,128)S(1)}, u32[]{:S(2)}, u32[]{:S(2)}) %collective-permute-start.17) | collective-permute-done | bytes 278560 | tf_op jit(solution)/shard_map/ppermute | solution.py:33
  122.9 1.0 pad_maximum_fusion.2.refs_0_.refs_16_
  123.9 4.4 %collective-permute-start.26 = (f32[2,544,128]{2,1,0:T(8,128)S(1)}, f32[2,544,128]{2,1,0:T(8,128)S(1)}, u32[]{:S(2)}, u32[]{:S(2)}) collective-permute-start(f32[2,544,128]{2,1,0:T(8,128)S(1)} %pad_maximum_fusion.2.refs_0_.refs_16_), channel_id=1, source_target_pairs={{0,4},{4,0},{8,12},{12,8},{16,20},{20,16},{24,28},{28,24},{32,36},... | collective-permute-start | bytes 1671176 | tf_op jit(solution)/shard_map/ppermute | solution.py:37
  128.3 1.4 collective-permute-start.22
  129.7 1.3 collective-permute-start.20
  131.7 2.4 %collective-permute-start.27 = (f32[2,544,128]{2,1,0:T(8,128)S(1)}, f32[2,544,128]{2,1,0:T(8,128)S(1)}, u32[]{:S(2)}, u32[]{:S(2)}) collective-permute-start(f32[2,544,128]{2,1,0:T(8,128)S(1)} %pad_maximum_fusion.3.refs_1_.refs_17_), channel_id=1, source_target_pairs={{0,4},{4,0},{8,12},{12,8},{16,20},{20,16},{24,28},{28,24},{32,36},... | collective-permute-start | bytes 1671176 | tf_op jit(solution)/shard_map/ppermute | solution.py:37
  134.1 6.8 %collective-permute-done.22.refs_6_.refs_22_ = f32[2,544,128]{2,1,0:T(8,128)S(1)} collective-permute-done((f32[2,544,128]{2,1,0:T(8,128)S(1)}, f32[2,544,128]{2,1,0:T(8,128)S(1)}, u32[]{:S(2)}, u32[]{:S(2)}) %collective-permute-start.22) | collective-permute-done | bytes 557088 | tf_op jit(solution)/shard_map/ppermute | solution.py:33
  140.9 2.4 %collective-permute-start.32 = (f32[2,544,128]{2,1,0:T(8,128)S(1)}, f32[2,544,128]{2,1,0:T(8,128)S(1)}, u32[]{:S(2)}, u32[]{:S(2)}) collective-permute-start(f32[2,544,128]{2,1,0:T(8,128)S(1)} %collective-permute-done.22.refs_6_.refs_22_), channel_id=1, source_target_pairs={{0,4},{4,0},{8,12},{12,8},{16,20},{20,16},{24,28},{28,24},{32,36},... | collective-permute-start | bytes 1671176 | tf_op jit(solution)/shard_map/ppermute | solution.py:37
  143.2 17.1 %collective-permute-done.21.refs_3_.refs_19_ = f32[2,544,128]{2,1,0:T(8,128)S(1)} collective-permute-done((f32[2,544,128]{2,1,0:T(8,128)S(1)}, f32[2,544,128]{2,1,0:T(8,128)S(1)}, u32[]{:S(2)}, u32[]{:S(2)}) %collective-permute-start.21) | collective-permute-done | bytes 557088 | tf_op jit(solution)/shard_map/ppermute | solution.py:33
  160.3 3.5 %collective-permute-start.24 = (f32[2,544,128]{2,1,0:T(8,128)S(1)}, f32[2,544,128]{2,1,0:T(8,128)S(1)}, u32[]{:S(2)}, u32[]{:S(2)}) collective-permute-start(f32[2,544,128]{2,1,0:T(8,128)S(1)} %collective-permute-done.21.refs_3_.refs_19_), channel_id=1, source_target_pairs={{0,24},{4,100},{8,0},{12,108},{16,8},{20,116},{24,16},{28,124},{32... | collective-permute-start | bytes 1671176 | tf_op jit(solution)/shard_map/ppermute | solution.py:33
  163.8 1.4 collective-permute-start.29
  165.7 1.8 collective-permute-done.23.refs_4_.refs_20_
  167.9 2.4 %collective-permute-done.24.refs_5_.refs_21_ = f32[2,544,128]{2,1,0:T(8,128)S(1)} collective-permute-done((f32[2,544,128]{2,1,0:T(8,128)S(1)}, f32[2,544,128]{2,1,0:T(8,128)S(1)}, u32[]{:S(2)}, u32[]{:S(2)}) %collective-permute-start.24) | collective-permute-done | bytes 557088 | tf_op jit(solution)/shard_map/ppermute | solution.py:33
  170.2 2.4 %collective-permute-start.31 = (f32[2,544,128]{2,1,0:T(8,128)S(1)}, f32[2,544,128]{2,1,0:T(8,128)}, u32[]{:S(2)}, u32[]{:S(2)}) collective-permute-start(f32[2,544,128]{2,1,0:T(8,128)S(1)} %collective-permute-done.24.refs_5_.refs_21_), channel_id=1, source_target_pairs={{0,4},{4,0},{8,12},{12,8},{16,20},{20,16},{24,28},{28,24},{32,36},... | collective-permute-start | bytes 1671176 | tf_op jit(solution)/shard_map/ppermute | solution.py:37
  172.8 0.7 copy-done.17
  173.8 0.8 copy-done.19
  174.7 37.5 %update.1 = f32[768,4096]{1,0:T(8,128)} custom-call(s32[4]{0:T(128)} %add_add_fusion.place_ref, f32[768,1]{1,0:T(8,128)} %fusion.19.keep_ref, bf16[768,512]{1,0:T(8,128)(2,1)} %add_convert_fusion.take_ref, bf16[768,256]{1,0:T(8,128)(2,1)} %get-tuple-element.31.hit_ref, f32[2,768,256]{2,1,0:T(8,128)} %all-gather.4.cloned.1.call-done.lower_ref, ...), custom_call_target="tpu_custom_call" | custom-call | flops 16106127360 | bytes 41943040 | tf_op jit(solution)/shard_map/update/pallas_call | solution.py:225
  (93 shorter events, 5.1 us)
Async XLA Ops:
  6.5 106.1 %all-gather.4.cloned.1.call-start = ((), (), s32[]{:S(2)}) async-start(), calls=%async_computation | async-start | bytes 1966080 | tf_op jit(solution)/shard_map/all_gather | solution.py:312
  7.5 8.9 %collective-permute-start.5 = (f32[192,256]{1,0:T(8,128)S(1)}, f32[192,256]{1,0:T(8,128)S(1)}, u32[]{:S(2)}, u32[]{:S(2)}) collective-permute-start(f32[192,256]{1,0:T(8,128)S(1)} %slice_bitcast_fusion.13), channel_id=1, source_target_pairs={{0,1},{1,2},{2,3},{3,0},{4,5},{5,6},{6,7},{7,4},{8,9},{9,10},{10,1... | collective-permute-start | bytes 589832 | tf_op jit(solution)/shard_map/ppermute | solution.py:265
  9.6 11.0 %collective-permute-start.4 = (f32[192,256]{1,0:T(8,128)S(1)}, f32[192,256]{1,0:T(8,128)S(1)}, u32[]{:S(2)}, u32[]{:S(2)}) collective-permute-start(f32[192,256]{1,0:T(8,128)S(1)} %slice_bitcast_fusion.13), channel_id=1, source_target_pairs={{0,2},{1,3},{2,0},{3,1},{4,6},{5,7},{6,4},{7,5},{8,10},{9,11},{10,... | collective-permute-start | bytes 589832 | tf_op jit(solution)/shard_map/ppermute | solution.py:265
  12.0 8.5 %collective-permute-start.3 = (f32[192,256]{1,0:T(8,128)S(1)}, f32[192,256]{1,0:T(8,128)S(1)}, u32[]{:S(2)}, u32[]{:S(2)}) collective-permute-start(f32[192,256]{1,0:T(8,128)S(1)} %slice_bitcast_fusion.13), channel_id=1, source_target_pairs={{0,3},{1,0},{2,1},{3,2},{4,7},{5,4},{6,5},{7,6},{8,11},{9,8},{10,9... | collective-permute-start | bytes 589832 | tf_op jit(solution)/shard_map/ppermute | solution.py:265
  31.2 26.3 %collective-permute-start.9 = (f32[4,4,544,128]{3,2,1,0:T(8,128)}, f32[4,4,544,128]{3,2,1,0:T(8,128)S(1)}, u32[]{:S(2)}, u32[]{:S(2)}) collective-permute-start(f32[4,4,544,128]{3,2,1,0:T(8,128)} %pick_rows.2), channel_id=1, source_target_pairs={{0,4},{4,0},{8,12},{12,8},{16,20},{20,16},{24,28},{28,24},{32,36},... | collective-permute-start | bytes 13369352 | tf_op jit(solution)/shard_map/ppermute | solution.py:37
  39.2 23.3 %collective-permute-start = (f32[4,256,256]{2,1,0:T(8,128)}, f32[4,256,256]{2,1,0:T(8,128)S(1)}, u32[]{:S(2)}, u32[]{:S(2)}) collective-permute-start(f32[4,256,256]{2,1,0:T(8,128)} %get-tuple-element.21), channel_id=1, source_target_pairs={{0,16},{4,68},{1,17},{5,69},{2,18},{6,70},{3,19},{7,71}} | collective-permute-start | bytes 3145736 | tf_op jit(solution)/shard_map/ppermute | solution.py:33
  44.1 23.2 %collective-permute-start.1 = (f32[4,256,256]{2,1,0:T(8,128)}, f32[4,256,256]{2,1,0:T(8,128)}, u32[]{:S(2)}, u32[]{:S(2)}) collective-permute-start(f32[4,256,256]{2,1,0:T(8,128)} %get-tuple-element.22), channel_id=1, source_target_pairs={{0,8},{4,36},{1,9},{5,37},{2,10},{6,38},{3,11},{7,39}} | collective-permute-start | bytes 3145736 | tf_op jit(solution)/shard_map/ppermute | solution.py:33
  46.4 20.9 %collective-permute-start.2 = (f32[4,256,256]{2,1,0:T(8,128)}, f32[4,256,256]{2,1,0:T(8,128)}, u32[]{:S(2)}, u32[]{:S(2)}) collective-permute-start(f32[4,256,256]{2,1,0:T(8,128)} %get-tuple-element.23), channel_id=1, source_target_pairs={{0,24},{4,100},{1,25},{5,101},{2,26},{6,102},{3,27},{7,103}} | collective-permute-start | bytes 3145736 | tf_op jit(solution)/shard_map/ppermute | solution.py:33
  57.5 3.9 %copy-start = (f32[4,4,544,128]{3,2,1,0:T(8,128)}, f32[4,4,544,128]{3,2,1,0:T(8,128)S(1)}, u32[]{:S(2)}) copy-start(f32[4,4,544,128]{3,2,1,0:T(8,128)S(1)} %collective-permute-done.9) | copy-start | bytes 13369348
  62.5 9.0 %collective-permute-start.12 = (f32[2,544,128]{2,1,0:T(8,128)}, f32[2,544,128]{2,1,0:T(8,128)}, u32[]{:S(2)}, u32[]{:S(2)}) collective-permute-start(f32[2,544,128]{2,1,0:T(8,128)} %get-tuple-element.47), channel_id=1, source_target_pairs={{0,24},{4,100},{8,0},{12,108},{16,8},{20,116},{24,16},{28,124},{32... | collective-permute-start | bytes 1671176 | tf_op jit(solution)/shard_map/ppermute | solution.py:33
  62.5 112.1 %all-gather.6.cloned.1.call-start = ((), (), s32[]{:S(2)}) async-start(), calls=%async_computation.1 | async-start | bytes 8650752 | tf_op jit(solution)/shard_map/all_gather | solution.py:310
  62.6 6.9 %copy-start.2 = (f32[4,256,256]{2,1,0:T(8,128)}, f32[4,256,256]{2,1,0:T(8,128)S(1)}, u32[]{:S(2)}) copy-start(f32[4,256,256]{2,1,0:T(8,128)S(1)} %collective-permute-done) | copy-start | bytes 3145732
  67.3 10.2 %collective-permute-start.10 = (f32[2,544,128]{2,1,0:T(8,128)}, f32[2,544,128]{2,1,0:T(8,128)S(1)}, u32[]{:S(2)}, u32[]{:S(2)}) collective-permute-start(f32[2,544,128]{2,1,0:T(8,128)} %get-tuple-element.46), channel_id=1, source_target_pairs={{0,8},{4,36},{8,16},{12,44},{16,24},{20,52},{24,0},{28,60},{32,40}... | collective-permute-start | bytes 1671176 | tf_op jit(solution)/shard_map/ppermute | solution.py:33
  72.7 25.1 %collective-permute-start.13 = (f32[4,544,128]{2,1,0:T(8,128)S(1)}, f32[4,544,128]{2,1,0:T(8,128)S(1)}, u32[]{:S(2)}, u32[]{:S(2)}) collective-permute-start(f32[4,544,128]{2,1,0:T(8,128)S(1)} %pad_maximum_fusion.1), channel_id=1, source_target_pairs={{0,24},{4,100},{8,0},{12,108},{16,8},{20,116},{24,16},{28,124},{32... | collective-permute-start | bytes 3342344 | tf_op jit(solution)/shard_map/ppermute | solution.py:33
  77.6 2.0 copy-start.1
  77.6 2.0 copy-start.3
  78.7 19.0 %collective-permute-start.11 = (f32[4,544,128]{2,1,0:T(8,128)}, f32[4,544,128]{2,1,0:T(8,128)}, u32[]{:S(2)}, u32[]{:S(2)}) collective-permute-start(f32[4,544,128]{2,1,0:T(8,128)} %pad_maximum_fusion), channel_id=1, source_target_pairs={{0,8},{4,36},{8,16},{12,44},{16,24},{20,52},{24,0},{28,60},{32,40}... | collective-permute-start | bytes 3342344 | tf_op jit(solution)/shard_map/ppermute | solution.py:33
  82.5 7.8 %collective-permute-start.7 = (f32[256,256]{1,0:T(8,128)}, f32[256,256]{1,0:T(8,128)}, u32[]{:S(2)}, u32[]{:S(2)}) collective-permute-start(f32[256,256]{1,0:T(8,128)} %get-tuple-element.48), channel_id=1, source_target_pairs={{0,32},{4,12},{8,40},{16,48},{24,56},{36,44},{68,76},{100,108},{1,... | collective-permute-start | bytes 786440 | tf_op jit(solution)/shard_map/ppermute | solution.py:33
  84.5 6.8 %collective-permute-start.8 = (f32[256,256]{1,0:T(8,128)}, f32[256,256]{1,0:T(8,128)}, u32[]{:S(2)}, u32[]{:S(2)}) collective-permute-start(f32[256,256]{1,0:T(8,128)} %get-tuple-element.49), channel_id=1, source_target_pairs={{0,96},{4,28},{8,104},{16,112},{24,120},{36,60},{68,92},{100,124},... | collective-permute-start | bytes 786440 | tf_op jit(solution)/shard_map/ppermute | solution.py:33
  86.5 9.4 %collective-permute-start.6 = (f32[256,256]{1,0:T(8,128)}, f32[256,256]{1,0:T(8,128)}, u32[]{:S(2)}, u32[]{:S(2)}) collective-permute-start(f32[256,256]{1,0:T(8,128)} %get-tuple-element.50), channel_id=1, source_target_pairs={{0,64},{4,20},{8,72},{16,80},{24,88},{36,52},{68,84},{100,116},{1,... | collective-permute-start | bytes 786440 | tf_op jit(solution)/shard_map/ppermute | solution.py:33
  97.7 2.2 copy-start.6
  101.2 7.5 %collective-permute-start.14 = (f32[544,128]{1,0:T(8,128)S(1)}, f32[544,128]{1,0:T(8,128)S(1)}, u32[]{:S(2)}, u32[]{:S(2)}) collective-permute-start(f32[544,128]{1,0:T(8,128)S(1)} %get-tuple-element.43), channel_id=1, source_target_pairs={{0,64},{4,20},{8,72},{12,28},{16,80},{20,4},{24,88},{28,12},{32,96... | collective-permute-start | bytes 835592 | tf_op jit(solution)/shard_map/ppermute | solution.py:33
  104.7 5.7 %collective-permute-start.16 = (f32[544,128]{1,0:T(8,128)S(1)}, f32[544,128]{1,0:T(8,128)S(1)}, u32[]{:S(2)}, u32[]{:S(2)}) collective-permute-start(f32[544,128]{1,0:T(8,128)S(1)} %get-tuple-element.44), channel_id=1, source_target_pairs={{0,96},{4,28},{8,104},{12,4},{16,112},{20,12},{24,120},{28,20},{32... | collective-permute-start | bytes 835592 | tf_op jit(solution)/shard_map/ppermute | solution.py:33
  104.7 7.2 %collective-permute-start.15 = (f32[544,128]{1,0:T(8,128)S(1)}, f32[544,128]{1,0:T(8,128)S(1)}, u32[]{:S(2)}, u32[]{:S(2)}) collective-permute-start(f32[544,128]{1,0:T(8,128)S(1)} %get-tuple-element.45), channel_id=1, source_target_pairs={{0,32},{4,12},{8,40},{12,20},{16,48},{20,28},{24,56},{28,4},{32,64... | collective-permute-start | bytes 835592 | tf_op jit(solution)/shard_map/ppermute | solution.py:33
  115.1 7.8 %collective-permute-start.17 = (f32[544,128]{1,0:T(8,128)}, f32[544,128]{1,0:T(8,128)S(1)}, u32[]{:S(2)}, u32[]{:S(2)}) collective-permute-start(f32[544,128]{1,0:T(8,128)} %solve.1), channel_id=1, source_target_pairs={{0,96},{4,28},{8,104},{12,4},{16,112},{20,12},{24,120},{28,20},{32... | collective-permute-start | bytes 835592 | tf_op jit(solution)/shard_map/ppermute | solution.py:33
  115.4 15.6 %collective-permute-start.19 = (f32[544,128]{1,0:T(8,128)}, f32[544,128]{1,0:T(8,128)S(1)}, u32[]{:S(2)}, u32[]{:S(2)}) collective-permute-start(f32[544,128]{1,0:T(8,128)} %solve.1), channel_id=1, source_target_pairs={{0,32},{4,12},{8,40},{12,20},{16,48},{20,28},{24,56},{28,4},{32,64... | collective-permute-start | bytes 835592 | tf_op jit(solution)/shard_map/ppermute | solution.py:33
  116.6 14.4 %collective-permute-start.18 = (f32[544,128]{1,0:T(8,128)}, f32[544,128]{1,0:T(8,128)S(1)}, u32[]{:S(2)}, u32[]{:S(2)}) collective-permute-start(f32[544,128]{1,0:T(8,128)} %solve.1), channel_id=1, source_target_pairs={{0,64},{4,20},{8,72},{12,28},{16,80},{20,4},{24,88},{28,12},{32,96... | collective-permute-start | bytes 835592 | tf_op jit(solution)/shard_map/ppermute | solution.py:33
  123.9 50.8 %copy-start.4 = (f32[2,544,128]{2,1,0:T(8,128)}, f32[2,544,128]{2,1,0:T(8,128)S(1)}, u32[]{:S(2)}) copy-start(f32[2,544,128]{2,1,0:T(8,128)S(1)} %pad_maximum_fusion.2.refs_0_.refs_16_) | copy-start | bytes 1671172
  123.9 10.2 %collective-permute-start.26 = (f32[2,544,128]{2,1,0:T(8,128)S(1)}, f32[2,544,128]{2,1,0:T(8,128)S(1)}, u32[]{:S(2)}, u32[]{:S(2)}) collective-permute-start(f32[2,544,128]{2,1,0:T(8,128)S(1)} %pad_maximum_fusion.2.refs_0_.refs_16_), channel_id=1, source_target_pairs={{0,4},{4,0},{8,12},{12,8},{16,20},{20,16},{24,28},{28,24},{32,36},... | collective-permute-start | bytes 1671176 | tf_op jit(solution)/shard_map/ppermute | solution.py:37
  128.3 12.6 %collective-permute-start.22 = (f32[2,544,128]{2,1,0:T(8,128)S(1)}, f32[2,544,128]{2,1,0:T(8,128)S(1)}, u32[]{:S(2)}, u32[]{:S(2)}) collective-permute-start(f32[2,544,128]{2,1,0:T(8,128)S(1)} %pad_maximum_fusion.2.refs_0_.refs_16_), channel_id=1, source_target_pairs={{0,8},{4,36},{8,16},{12,44},{16,24},{20,52},{24,0},{28,60},{32,40}... | collective-permute-start | bytes 1671176 | tf_op jit(solution)/shard_map/ppermute | solution.py:33
  129.7 13.6 %collective-permute-start.20 = (f32[2,544,128]{2,1,0:T(8,128)S(1)}, f32[2,544,128]{2,1,0:T(8,128)S(1)}, u32[]{:S(2)}, u32[]{:S(2)}) collective-permute-start(f32[2,544,128]{2,1,0:T(8,128)S(1)} %pad_maximum_fusion.2.refs_0_.refs_16_), channel_id=1, source_target_pairs={{0,24},{4,100},{8,0},{12,108},{16,8},{20,116},{24,16},{28,124},{32... | collective-permute-start | bytes 1671176 | tf_op jit(solution)/shard_map/ppermute | solution.py:33
  131.0 43.7 %copy-start.5 = (f32[2,544,128]{2,1,0:T(8,128)}, f32[2,544,128]{2,1,0:T(8,128)S(1)}, u32[]{:S(2)}) copy-start(f32[2,544,128]{2,1,0:T(8,128)S(1)} %pad_maximum_fusion.3.refs_1_.refs_17_) | copy-start | bytes 1671172
  131.0 29.3 %collective-permute-start.21 = (f32[2,544,128]{2,1,0:T(8,128)S(1)}, f32[2,544,128]{2,1,0:T(8,128)S(1)}, u32[]{:S(2)}, u32[]{:S(2)}) collective-permute-start(f32[2,544,128]{2,1,0:T(8,128)S(1)} %pad_maximum_fusion.3.refs_1_.refs_17_), channel_id=1, source_target_pairs={{0,24},{4,100},{8,0},{12,108},{16,8},{20,116},{24,16},{28,124},{32... | collective-permute-start | bytes 1671176 | tf_op jit(solution)/shard_map/ppermute | solution.py:33
  131.7 32.1 %collective-permute-start.27 = (f32[2,544,128]{2,1,0:T(8,128)S(1)}, f32[2,544,128]{2,1,0:T(8,128)S(1)}, u32[]{:S(2)}, u32[]{:S(2)}) collective-permute-start(f32[2,544,128]{2,1,0:T(8,128)S(1)} %pad_maximum_fusion.3.refs_1_.refs_17_), channel_id=1, source_target_pairs={{0,4},{4,0},{8,12},{12,8},{16,20},{20,16},{24,28},{28,24},{32,36},... | collective-permute-start | bytes 1671176 | tf_op jit(solution)/shard_map/ppermute | solution.py:37
  134.1 40.6 %copy-start.7 = (f32[2,544,128]{2,1,0:T(8,128)}, f32[2,544,128]{2,1,0:T(8,128)S(1)}, u32[]{:S(2)}) copy-start(f32[2,544,128]{2,1,0:T(8,128)S(1)} %collective-permute-done.26.refs_8_.refs_24_) | copy-start | bytes 1671172
  134.1 31.1 %collective-permute-start.25 = (f32[2,544,128]{2,1,0:T(8,128)S(1)}, f32[2,544,128]{2,1,0:T(8,128)S(1)}, u32[]{:S(2)}, u32[]{:S(2)}) collective-permute-start(f32[2,544,128]{2,1,0:T(8,128)S(1)} %pad_maximum_fusion.3.refs_1_.refs_17_), channel_id=1, source_target_pairs={{0,8},{4,36},{8,16},{12,44},{16,24},{20,52},{24,0},{28,60},{32,40}... | collective-permute-start | bytes 1671176 | tf_op jit(solution)/shard_map/ppermute | solution.py:33
  140.9 33.8 %copy-start.8 = (f32[2,544,128]{2,1,0:T(8,128)}, f32[2,544,128]{2,1,0:T(8,128)S(1)}, u32[]{:S(2)}) copy-start(f32[2,544,128]{2,1,0:T(8,128)S(1)} %collective-permute-done.22.refs_6_.refs_22_) | copy-start | bytes 1671172
  140.9 24.4 %collective-permute-start.32 = (f32[2,544,128]{2,1,0:T(8,128)S(1)}, f32[2,544,128]{2,1,0:T(8,128)S(1)}, u32[]{:S(2)}, u32[]{:S(2)}) collective-permute-start(f32[2,544,128]{2,1,0:T(8,128)S(1)} %collective-permute-done.22.refs_6_.refs_22_), channel_id=1, source_target_pairs={{0,4},{4,0},{8,12},{12,8},{16,20},{20,16},{24,28},{28,24},{32,36},... | collective-permute-start | bytes 1671176 | tf_op jit(solution)/shard_map/ppermute | solution.py:37
  143.2 31.5 %copy-start.9 = (f32[2,544,128]{2,1,0:T(8,128)}, f32[2,544,128]{2,1,0:T(8,128)S(1)}, u32[]{:S(2)}) copy-start(f32[2,544,128]{2,1,0:T(8,128)S(1)} %collective-permute-done.20.refs_2_.refs_18_) | copy-start | bytes 1671172
  143.2 24.3 %collective-permute-start.23 = (f32[2,544,128]{2,1,0:T(8,128)S(1)}, f32[2,544,128]{2,1,0:T(8,128)S(1)}, u32[]{:S(2)}, u32[]{:S(2)}) collective-permute-start(f32[2,544,128]{2,1,0:T(8,128)S(1)} %collective-permute-done.22.refs_6_.refs_22_), channel_id=1, source_target_pairs={{0,8},{4,36},{8,16},{12,44},{16,24},{20,52},{24,0},{28,60},{32,40}... | collective-permute-start | bytes 1671176 | tf_op jit(solution)/shard_map/ppermute | solution.py:33
  160.3 14.4 %copy-start.10 = (f32[2,544,128]{2,1,0:T(8,128)}, f32[2,544,128]{2,1,0:T(8,128)S(1)}, u32[]{:S(2)}) copy-start(f32[2,544,128]{2,1,0:T(8,128)S(1)} %collective-permute-done.21.refs_3_.refs_19_) | copy-start | bytes 1671172
  160.3 10.0 %collective-permute-start.24 = (f32[2,544,128]{2,1,0:T(8,128)S(1)}, f32[2,544,128]{2,1,0:T(8,128)S(1)}, u32[]{:S(2)}, u32[]{:S(2)}) collective-permute-start(f32[2,544,128]{2,1,0:T(8,128)S(1)} %collective-permute-done.21.refs_3_.refs_19_), channel_id=1, source_target_pairs={{0,24},{4,100},{8,0},{12,108},{16,8},{20,116},{24,16},{28,124},{32... | collective-permute-start | bytes 1671176 | tf_op jit(solution)/shard_map/ppermute | solution.py:33
  163.8 8.9 %copy-start.11 = (f32[2,544,128]{2,1,0:T(8,128)}, f32[2,544,128]{2,1,0:T(8,128)S(1)}, u32[]{:S(2)}) copy-start(f32[2,544,128]{2,1,0:T(8,128)S(1)} %collective-permute-done.27.refs_9_.refs_25_) | copy-start | bytes 1671172
  163.8 8.9 %collective-permute-start.29 = (f32[2,544,128]{2,1,0:T(8,128)S(1)}, f32[2,544,128]{2,1,0:T(8,128)S(1)}, u32[]{:S(2)}, u32[]{:S(2)}) collective-permute-start(f32[2,544,128]{2,1,0:T(8,128)S(1)} %collective-permute-done.21.refs_3_.refs_19_), channel_id=1, source_target_pairs={{0,4},{4,0},{8,12},{12,8},{16,20},{20,16},{24,28},{28,24},{32,36},... | collective-permute-start | bytes 1671176 | tf_op jit(solution)/shard_map/ppermute | solution.py:37
  165.2 7.6 %copy-start.12 = (f32[2,544,128]{2,1,0:T(8,128)}, f32[2,544,128]{2,1,0:T(8,128)S(1)}, u32[]{:S(2)}) copy-start(f32[2,544,128]{2,1,0:T(8,128)S(1)} %collective-permute-done.25.refs_7_.refs_23_) | copy-start | bytes 1671172
  165.2 7.5 %collective-permute-start.28 = (f32[2,544,128]{2,1,0:T(8,128)S(1)}, f32[2,544,128]{2,1,0:T(8,128)S(1)}, u32[]{:S(2)}, u32[]{:S(2)}) collective-permute-start(f32[2,544,128]{2,1,0:T(8,128)S(1)} %collective-permute-done.20.refs_2_.refs_18_), channel_id=1, source_target_pairs={{0,4},{4,0},{8,12},{12,8},{16,20},{20,16},{24,28},{28,24},{32,36},... | collective-permute-start | bytes 1671176 | tf_op jit(solution)/shard_map/ppermute | solution.py:37
  165.3 7.5 %copy-start.13 = (f32[2,544,128]{2,1,0:T(8,128)}, f32[2,544,128]{2,1,0:T(8,128)S(1)}, u32[]{:S(2)}) copy-start(f32[2,544,128]{2,1,0:T(8,128)S(1)} %collective-permute-done.32.refs_14_.refs_30_) | copy-start | bytes 1671172
  165.3 7.4 %collective-permute-start.33 = (f32[2,544,128]{2,1,0:T(8,128)S(1)}, f32[2,544,128]{2,1,0:T(8,128)S(1)}, u32[]{:S(2)}, u32[]{:S(2)}) collective-permute-start(f32[2,544,128]{2,1,0:T(8,128)S(1)} %collective-permute-done.25.refs_7_.refs_23_), channel_id=1, source_target_pairs={{0,4},{4,0},{8,12},{12,8},{16,20},{20,16},{24,28},{28,24},{32,36},... | collective-permute-start | bytes 1671176 | tf_op jit(solution)/shard_map/ppermute | solution.py:37
  167.5 5.2 %copy-start.14 = (f32[2,544,128]{2,1,0:T(8,128)}, f32[2,544,128]{2,1,0:T(8,128)S(1)}, u32[]{:S(2)}) copy-start(f32[2,544,128]{2,1,0:T(8,128)S(1)} %collective-permute-done.23.refs_4_.refs_20_) | copy-start | bytes 1671172
  167.5 5.2 %collective-permute-start.30 = (f32[2,544,128]{2,1,0:T(8,128)S(1)}, f32[2,544,128]{2,1,0:T(8,128)S(1)}, u32[]{:S(2)}, u32[]{:S(2)}) collective-permute-start(f32[2,544,128]{2,1,0:T(8,128)S(1)} %collective-permute-done.23.refs_4_.refs_20_), channel_id=1, source_target_pairs={{0,4},{4,0},{8,12},{12,8},{16,20},{20,16},{24,28},{28,24},{32,36},... | collective-permute-start | bytes 1671176 | tf_op jit(solution)/shard_map/ppermute | solution.py:37
  170.2 2.5 %copy-start.15 = (f32[2,544,128]{2,1,0:T(8,128)}, f32[2,544,128]{2,1,0:T(8,128)S(1)}, u32[]{:S(2)}) copy-start(f32[2,544,128]{2,1,0:T(8,128)S(1)} %collective-permute-done.24.refs_5_.refs_21_) | copy-start | bytes 1671172
  170.2 4.4 %collective-permute-start.31 = (f32[2,544,128]{2,1,0:T(8,128)S(1)}, f32[2,544,128]{2,1,0:T(8,128)}, u32[]{:S(2)}, u32[]{:S(2)}) collective-permute-start(f32[2,544,128]{2,1,0:T(8,128)S(1)} %collective-permute-done.24.refs_5_.refs_21_), channel_id=1, source_target_pairs={{0,4},{4,0},{8,12},{12,8},{16,20},{20,16},{24,28},{28,24},{32,36},... | collective-permute-start | bytes 1671176 | tf_op jit(solution)/shard_map/ppermute | solution.py:37
  172.7 0.8 copy-start.17
  172.7 1.0 copy-start.18
  172.7 1.1 copy-start.16
  173.8 0.8 copy-start.19
Sparse Core Ops, SparseCore 0:
  62.6 24.1 all-gather.3
  100.0 65.5 all-gather.5

commit v3 on v0

v3 whole, which is shorter than its diff:
```python
import jax
import jax.numpy as jnp
from jax import lax
from jax.experimental import pallas as pl
from jax.experimental.pallas import tpu as pltpu
from jax.sharding import PartitionSpec as P

F32 = jnp.float32
BF16 = jnp.bfloat16
HIGHEST = lax.Precision.HIGHEST
NB = 256
LANES = 128
EXTRA = 32
SHARE = 2 * NB + EXTRA
VMEM_LIMIT = 56 * 1024 * 1024


def rank_of(y, z, core):
    return ((y % 4) * 4 + z % 4) * 2 + core


def moved(y, z, core, one, two):
    return (y + two, z + one, core) if core == 0 else (y + one, z + two, core)


def send(value, one=0, two=0, only=lambda one, two: True):
    pairs = []
    for y in range(4):
        for z in range(4):
            for core in range(2):
                at = (z, y) if core == 0 else (y, z)
                if only(*at):
                    pairs.append((rank_of(y, z, core), rank_of(*moved(y, z, core, one, two))))
    return lax.ppermute(value, "prow", pairs)


def swap_cores(value):
    return lax.ppermute(value, "prow", [(rank, rank ^ 1) for rank in range(32)])


def split_two(value):
    high = value.astype(BF16)
    low = (value - high.astype(F32)).astype(BF16)
    return high, low


def exact_dot(a, b):
    return jnp.dot(a, b, precision=HIGHEST, preferred_element_type=F32)


def chip_at(place, one, two):
    by_z = (place[1] + two) % 4 * 4 + (place[2] + one) % 4
    by_y = (place[1] + one) % 4 * 4 + (place[2] + two) % 4
    return jnp.where(place[0] == 0, by_z, by_y)


def pick_kernel(place_ref, matrix_ref, select_ref, out_ref, left_ref, blocks_ref, rows_ref, in_sems, out_sems):
    def fetches(one):
        return [
            pltpu.make_async_copy(
                matrix_ref.at[:, pl.ds(pl.multiple_of(share * LANES, LANES), LANES)],
                blocks_ref.at[one, :, pl.ds(two * LANES, LANES)],
                in_sems.at[one, two],
            )
            for two in range(4)
            for share in [chip_at(place_ref, one, two) * 2 + place_ref[0]]
        ]

    def store(one):
        return pltpu.make_async_copy(rows_ref.at[one], out_ref.at[one], out_sems.at[one])

    for one in range(4):
        for copy in fetches(one):
            copy.start()
    for part in range(2):
        left_ref[:, part * select_ref.shape[1] : (part + 1) * select_ref.shape[1]] = select_ref[...]

    @pl.loop(0, 4)
    def _(one):
        for copy in fetches(one):
            copy.wait()
        right = jnp.concatenate(split_two(blocks_ref[one]), axis=0)
        rows = jnp.dot(left_ref[...], right, preferred_element_type=F32)
        for two in range(4):
            rows_ref[one, two] = rows[:, two * LANES : (two + 1) * LANES]
        store(one).start()

    for one in range(4):
        store(one).wait()


def pick_rows(place, select, matrix):
    rows = matrix.shape[0]
    hbm = pl.BlockSpec(memory_space=pl.ANY)
    shape = (4, 4, 2 * NB, LANES)
    return pl.pallas_call(
        pick_kernel,
        out_shape=jax.ShapeDtypeStruct(shape, F32),
        in_specs=[
            pl.BlockSpec(memory_space=pltpu.SMEM), hbm, pl.BlockSpec(memory_space=pltpu.VMEM)
        ],
        out_specs=hbm,
        scratch_shapes=[
            pltpu.VMEM((2 * NB, 2 * rows), BF16),
            pltpu.VMEM((4, rows, 4 * LANES), F32),
            pltpu.VMEM(shape, F32),
            pltpu.SemaphoreType.DMA((4, 4)),
            pltpu.SemaphoreType.DMA((4,)),
        ],
        compiler_params=pltpu.CompilerParams(vmem_limit_bytes=52 << 20),
        cost_estimate=pl.CostEstimate(
            flops=2 * 2 * 512 * 768 * 2048, bytes_accessed=10 << 20, transcendentals=0
        ),
        name="pick_rows",
    )(place, matrix, select)


def extra_kernel(place_ref, select_ref, own_ref, other_ref, out_ref, flat_ref):
    total = None
    for part, lower_ref in enumerate((own_ref, other_ref)):
        lower = lower_ref[...]
        high, rest = split_two(lower)
        middle, low = split_two(lower - high.astype(F32))
        select = select_ref[part]
        for piece in (high, middle, low):
            rows = jnp.dot(select, piece, preferred_element_type=F32)
            total = rows if total is None else total + rows
    flat_ref[: 2 * NB] = total[:, :LANES]
    flat_ref[2 * NB :] = total[:, LANES:]
    for one in range(4):
        for two in range(4):
            share = chip_at(place_ref, one, two) * 2 + place_ref[0]
            start = pl.multiple_of(share * EXTRA, EXTRA)
            out_ref[one, two] = flat_ref[pl.ds(start, EXTRA)]


def pick_extra(place, select, own, other):
    return pl.pallas_call(
        extra_kernel,
        out_shape=jax.ShapeDtypeStruct((4, 4, EXTRA, LANES), F32),
        in_specs=[pl.BlockSpec(memory_space=pltpu.SMEM)]
        + [pl.BlockSpec(memory_space=pltpu.VMEM)] * 3,
        scratch_shapes=[pltpu.VMEM((4 * NB, LANES), F32)],
        compiler_params=pltpu.CompilerParams(vmem_limit_bytes=16 << 20),
        cost_estimate=pl.CostEstimate(
            flops=2 * 3 * 512 * 1536 * 256, bytes_accessed=4 << 20, transcendentals=0
        ),
        name="pick_extra",
    )(place, select, own, other)


def solve_kernel(raw_ref, inverse_ref, out_ref):
    out_ref[:NB] = exact_dot(inverse_ref[0], raw_ref[:NB])
    out_ref[NB : 2 * NB] = exact_dot(inverse_ref[1], raw_ref[NB : 2 * NB])
    out_ref[2 * NB :] = raw_ref[2 * NB :]


def solve(raw, inverses):
    return pl.pallas_call(
        solve_kernel,
        out_shape=jax.ShapeDtypeStruct((SHARE, LANES), F32),
        cost_estimate=pl.CostEstimate(
            flops=6 * 2 * 2 * 256 * 256 * 128, bytes_accessed=1 << 20, transcendentals=0
        ),
        name="solve",
    )(raw, inverses)


def tops_kernel(
    matrix_ref, top_ref, take_ref, out_ref, left_ref, tops_ref, blocks_ref, in_sems, out_sems
):
    width = 2 * LANES

    def lanes(step):
        return pl.ds(pl.multiple_of(step * width, width), width)

    def fetches(step):
        return (
            pltpu.make_async_copy(top_ref.at[:, lanes(step)], tops_ref.at[step], in_sems.at[0, step]),
            pltpu.make_async_copy(
                matrix_ref.at[:, lanes(step)], blocks_ref.at[step], in_sems.at[1, step]
            ),
        )

    def store(step):
        return pltpu.make_async_copy(
            blocks_ref.at[step], out_ref.at[:, lanes(step)], out_sems.at[step]
        )

    @pl.loop(0, 16)
    def _(step):
        for copy in fetches(step):
            copy.start()

    left_ref[:, : 2 * NB] = take_ref[...]
    left_ref[:, 2 * NB :] = take_ref[...]

    @pl.loop(0, 16)
    def _(step):
        for copy in fetches(step):
            copy.wait()
        high, low = split_two(tops_ref[step])
        right = jnp.concatenate([high, low], axis=0)
        total = jnp.dot(left_ref[...], right, preferred_element_type=F32)
        blocks_ref[step] = blocks_ref[step] + total
        store(step).start()

    @pl.loop(0, 16)
    def _(step):
        store(step).wait()


def put_tops(matrix, tops, take):
    rows = matrix.shape[0]
    hbm = pl.BlockSpec(memory_space=pl.ANY)
    vmem = pl.BlockSpec(memory_space=pltpu.VMEM)
    return pl.pallas_call(
        tops_kernel,
        out_shape=jax.ShapeDtypeStruct(matrix.shape, F32),
        in_specs=[hbm, hbm, vmem],
        out_specs=hbm,
        input_output_aliases={0: 0},
        scratch_shapes=[
            pltpu.VMEM((rows, 4 * NB), BF16),
            pltpu.VMEM((16, 2 * NB, 2 * LANES), F32),
            pltpu.VMEM((16, rows, 2 * LANES), F32),
            pltpu.SemaphoreType.DMA((2, 16)),
            pltpu.SemaphoreType.DMA((16,)),
        ],
        compiler_params=pltpu.CompilerParams(vmem_limit_bytes=52 << 20),
        cost_estimate=pl.CostEstimate(
            flops=2 * rows * 4096 * 4 * NB, bytes_accessed=32 << 20, transcendentals=0
        ),
        name="put_tops",
    )(matrix, tops, take)


def update_kernel(place_ref, source_ref, keep_ref, hit_ref, lower_ref, inverse_ref, *refs):
    pieces = refs[:16]
    out_ref, left_ref, held_ref, flat_ref, blocks_ref, piece_sems, in_sems, out_sems = refs[16:]
    core, rank = place_ref[0], place_ref[3]
    width = 2 * LANES
    copies = [
        pltpu.make_async_copy(
            pieces[side * 8 + slot],
            held_ref.at[side, slot // 2, pl.ds(slot % 2 * 2, 2)],
            piece_sems.at[side * 8 + slot],
        )
        for side in range(2)
        for slot in range(8)
    ]
    for copy in copies:
        copy.start()

    def lanes(step):
        chip = chip_at(place_ref, step // 4, step % 4)
        return pl.ds(pl.multiple_of(chip * width, width), width)

    def fetch(step):
        return pltpu.make_async_copy(
            source_ref.at[:, lanes(step)], blocks_ref.at[step], in_sems.at[step]
        )

    def store(step):
        return pltpu.make_async_copy(
            blocks_ref.at[step], out_ref.at[:, lanes(step)], out_sems.at[step]
        )

    @pl.loop(0, 16)
    def _(step):
        fetch(step).start()

    for copy in copies:
        copy.wait()
    for side in range(2):
        for turn in range(4):
            for inner in range(4):
                one, two = (turn, inner) if side == 0 else (inner, turn)
                owner = chip_at(place_ref, one, two) * 2 + (core + side) % 2
                start = pl.multiple_of(owner * EXTRA, EXTRA)
                flat_ref[pl.ds(start, EXTRA)] = held_ref[side, turn, inner, 2 * NB :]
    pivot_rows = jnp.concatenate([flat_ref[:NB], flat_ref[2 * NB : 3 * NB]], axis=1)
    top_rows = jnp.concatenate([flat_ref[NB : 2 * NB], flat_ref[3 * NB :]], axis=1)
    weight = exact_dot(inverse_ref[1], pivot_rows)
    hit = hit_ref[...].astype(F32)
    swapped = jnp.max(hit, axis=1, keepdims=True) > 0.0
    lower0 = jnp.where(swapped, exact_dot(hit, top_rows), lower_ref[0])
    lower1 = lower_ref[1]
    lower0 = lower0 - exact_dot(lower1, weight)
    at_second = rank == 1
    lower0 = jnp.concatenate([jnp.where(at_second, weight, lower0[:NB]), lower0[NB:]], axis=0)
    lower1 = jnp.concatenate([jnp.where(at_second, 0.0, lower1[:NB]), lower1[NB:]], axis=0)
    high, low = split_two(-jnp.concatenate([lower0, lower1], axis=1))
    for i, part in enumerate((high, high, low)):
        left_ref[:, i * 2 * NB : (i + 1) * 2 * NB] = part

    @pl.loop(0, 16)
    def _(step):
        own = held_ref[0, step // 4, step % 4, : 2 * NB]
        other = held_ref[1, step % 4, step // 4, : 2 * NB]
        upper = jnp.concatenate(
            [jnp.where(core == 0, own, other), jnp.where(core == 0, other, own)], axis=1
        )
        fetch(step).wait()
        high, low = split_two(upper)
        right = jnp.concatenate([high, low, high], axis=0)
        total = jnp.dot(left_ref[...], right, preferred_element_type=F32)
        total = blocks_ref[step] * keep_ref[...] + total
        start = jnp.where(at_second, total[:NB] + upper[NB:], total[:NB])
        blocks_ref[step, :NB] = jnp.where(rank == 0, upper[:NB], start)
        blocks_ref[step, NB:] = total[NB:]
        store(step).start()

    @pl.loop(0, 16)
    def _(step):
        store(step).wait()


def update(place, source, keep, hit, lower, inverse, pieces):
    rows, columns = source.shape
    hbm = pl.BlockSpec(memory_space=pl.ANY)
    vmem = pl.BlockSpec(memory_space=pltpu.VMEM)
    return pl.pallas_call(
        update_kernel,
        out_shape=jax.ShapeDtypeStruct(source.shape, F32),
        in_specs=[pl.BlockSpec(memory_space=pltpu.SMEM), hbm] + [vmem] * 4 + [hbm] * 16,
        out_specs=hbm,
        scratch_shapes=[
            pltpu.VMEM((rows, 6 * NB), BF16),
            pltpu.VMEM((2, 4, 4, SHARE, LANES), F32),
            pltpu.VMEM((4 * NB, LANES), F32),
            pltpu.VMEM((16, rows, 2 * LANES), F32),
            pltpu.SemaphoreType.DMA((16,)),
            pltpu.SemaphoreType.DMA((16,)),
            pltpu.SemaphoreType.DMA((16,)),
        ],
        compiler_params=pltpu.CompilerParams(vmem_limit_bytes=52 << 20),
        cost_estimate=pl.CostEstimate(
            flops=2 * rows * columns * 6 * NB, bytes_accessed=33 << 20, transcendentals=0
        ),
        name="update",
    )(place, source, keep, hit, lower, inverse, *pieces)


def own_tops_kernel(place_ref, matrix_ref, out_ref, zero_ref, held_ref, sems, zero_sems):
    rank = place_ref[3]
    zero_ref[...] = jnp.zeros_like(zero_ref)
    width = zero_ref.shape[1]

    def blanks(panel):
        return [
            pltpu.make_async_copy(
                zero_ref,
                out_ref.at[pl.ds(panel * NB, NB), pl.ds(i * width, width)],
                zero_sems.at[panel, i],
            )
            for i in range(4)
        ]

    for panel in range(2):

        @pl.when(rank != panel)
        def _(panel=panel):
            for copy in blanks(panel):
                copy.start()

    for panel in range(2):

        @pl.when(rank == panel)
        def _(panel=panel):
            load = pltpu.make_async_copy(matrix_ref.at[pl.ds(0, NB)], held_ref, sems.at[0])
            load.start()
            load.wait()
            store = pltpu.make_async_copy(
                held_ref, out_ref.at[pl.ds(panel * NB, NB)], sems.at[1]
            )
            store.start()
            store.wait()

    for panel in range(2):

        @pl.when(rank != panel)
        def _(panel=panel):
            for copy in blanks(panel):
                copy.wait()


def own_tops(place, matrix):
    columns = matrix.shape[1]
    hbm = pl.BlockSpec(memory_space=pl.ANY)
    return pl.pallas_call(
        own_tops_kernel,
        out_shape=jax.ShapeDtypeStruct((2 * NB, columns), F32),
        in_specs=[pl.BlockSpec(memory_space=pltpu.SMEM), hbm],
        out_specs=hbm,
        scratch_shapes=[
            pltpu.VMEM((NB, columns // 4), F32),
            pltpu.VMEM((NB, columns), F32),
            pltpu.SemaphoreType.DMA((2,)),
            pltpu.SemaphoreType.DMA((2, 4)),
        ],
        compiler_params=pltpu.CompilerParams(vmem_limit_bytes=VMEM_LIMIT),
        cost_estimate=pl.CostEstimate(flops=0, bytes_accessed=8 << 20, transcendentals=0),
        name="own_tops",
    )(place, matrix)


def body(matrix, lower_panels, inverses, pivots):
    rank = lax.axis_index("prow")
    column_rank = lax.axis_index("pcol")
    y, z, core = rank // 8, rank // 2 % 4, rank % 2
    first = jnp.where(core == 0, z, y)
    second = jnp.where(core == 0, y, z)
    rows = matrix.shape[0]
    index = jnp.arange(NB, dtype=jnp.int32)
    place = jnp.stack([core, y, z, rank]).astype(jnp.int32)
    other_place = jnp.stack([1 - core, y, z, rank]).astype(jnp.int32)

    tops = lax.psum(own_tops(place, matrix), "prow")

    lower = lax.all_gather(lower_panels, "pcol", axis=1, tiled=True)
    lower_own = lower_panels[0]
    far = [lax.ppermute(lower_own, "pcol", [(i, (i - d) % 4) for i in range(4)]) for d in (1, 2, 3)]
    lower_own = jnp.concatenate([lower_own] + far)


    pivot0, pivot1 = pivots[0], pivots[1]
    again = pivot1[:, None] == pivot0[None, :]
    from_top = jnp.any(again, axis=1)
    source1 = jnp.where(from_top, jnp.sum(jnp.where(again, index[None, :], 0), axis=1), pivot1)
    sources = jnp.concatenate([pivot0, source1])

    def local(matrix_row, owner=rank):
        blocks = matrix_row // NB
        where = blocks // 32 * NB + matrix_row % NB
        return jnp.where(blocks % 32 == owner, where, -1)

    local_row = jnp.arange(rows, dtype=jnp.int32)
    select = (local(sources)[:, None] == local_row[None, :]).astype(BF16)

    panel_rows = jnp.concatenate([pivot1, NB + index])
    want = jnp.stack([local(panel_rows), local(panel_rows, rank ^ 1)])
    piece = lower_panels.shape[1]
    away = (want // piece - column_rank) % 4 * piece + want % piece
    want = jnp.where(want >= 0, away, -1)
    want = (want[:, :, None] == local_row[None, None, :]).astype(BF16)

    def exchange(turn, share):
        lower_other = swap_cores(jnp.where(turn == 0, lower_own, 0.0))
        sent = pick_rows(other_place + turn, select, matrix)
        own_place, sent = lax.optimization_barrier((place + turn, sent))
        other = swap_cores(sent)

        kept = pick_rows(own_place, select, matrix)
        extra = pick_extra(place, want, lower_own, lower_other)
        part = [jnp.concatenate([kept[d] + other[d], extra[d]], axis=1) for d in range(4)]
        ahead = send(part[2][:2], one=1)
        behind = send(part[2][2:], one=3)
        part[1] = jnp.concatenate([part[1][:2] + ahead, part[1][2:]])
        part[3] = jnp.concatenate([part[3][:2], part[3][2:] + behind])
        part = part[0] + send(part[1], one=1) + send(part[3], one=3)

        raw = part[0]
        for d in (2, 1, 3):
            raw = raw + send(part[d], two=d)

        return solve(raw, inverses)

    rounds = jnp.minimum(pivots[0, 0] + 1, 1)
    share = lax.fori_loop(0, rounds, exchange, jnp.zeros((SHARE, LANES), F32))

    near = {d: send(share, two=4 - d) for d in (1, 2, 3)}
    low = jnp.stack([share, near[1]])
    high = jnp.stack([near[2], near[3]])

    pivots, high = lax.optimization_barrier((pivots, high))
    pivot0, pivot1 = pivots[0], pivots[1]
    again = pivot1[:, None] == pivot0[None, :]
    takes0 = (pivot0 >= 2 * NB) & ~jnp.any(again, axis=0)
    place0 = jnp.where(takes0, local(pivot0), -1)
    hit0 = local_row[:, None] == place0[None, :]
    hit1 = local_row[:, None] == local(pivot1)[None, :]
    shifted = (NB + index)[:, None] == pivot0[None, :]
    top1 = jnp.where(
        jnp.any(shifted, axis=1),
        jnp.sum(jnp.where(shifted, index[None, :], 0), axis=1),
        NB + index,
    )
    to_top = (top1[:, None] == jnp.arange(2 * NB, dtype=jnp.int32)[None, :]).astype(BF16)
    hit1 = hit1.astype(BF16)
    take = jnp.dot(hit1, to_top, preferred_element_type=F32)
    take = take + jnp.concatenate([hit0, jnp.zeros_like(hit0)], axis=1).astype(F32)
    replaced = jnp.any(hit1 > 0, axis=1) | jnp.any(hit0, axis=1)
    replaced = replaced | ((rank == 1) & (local_row < NB))
    keep = jnp.where(replaced, 0.0, 1.0).astype(F32)[:, None]
    take = take.astype(BF16)


    low_before, high_after = send(low, one=1), send(high, one=3)
    high_before, low_after = send(high, one=1), send(low, one=3)
    low_across, high_across = send(low_before, one=1), send(high_after, one=3)
    pieces = [
        low, high, low_after, high_after, low_across, high_across, low_before, high_before
    ]
    pieces = pieces + [swap_cores(value) for value in pieces]
    result = update(place, matrix, keep, hit1, lower, inverses, pieces)
    return put_tops(result, tops, take)


def solution(mesh):
    placed = (P("prow", "pcol"), P(None, ("prow", "pcol"), None), P(), P())
    return jax.shard_map(
        body, mesh=mesh, in_specs=placed, out_specs=P("prow", "pcol"), check_vma=False
    )
```

time: 630 us -> 195 us (0.31)
  waiting for transfers between devices: 390 us -> 60.1 us
  local copies, waits for them, and re-layouts: 142 us -> 5.09 us
  Pallas kernels: 0 us -> 58.9 us
  starting transfers between devices: 0.21 us -> 45.6 us
  matrix products: 38.1 us -> 0.49 us
  blocking collectives: 22.5 us -> 0 us
  other arithmetic: 22.1 us -> 8.49 us
    psum x2 -> x1, waiting for transfers between devices: 206 us -> 0.03 us  [body(): tops = lax.psum(own_tops(place, matrix), 'prow')]
    reduce_scatter x2 -> x0, waiting for transfers between devices: 150 us -> none  [body(): shared = lax.psum_scatter(picked, 'prow', scatter_dimension=1, tiled=True)]
    scatter x6 -> x0, local copies, waits for them, and re-layouts: 78 us -> none  [the longest x4 52.8 us: body(): updated = updated.at[target].set(old_top, mode='drop')]
    ppermute x0 -> x29, waiting for transfers between devices: none -> 59.3 us  [the longest x16 59.3 us: send(): return lax.ppermute(value, 'prow', pairs)]
    pallas_call x0 -> x7, Pallas kernels: none -> 58.9 us  [the longest x1 21.5 us: update(): pl.pallas_call(update_kernel, out_shape=jax.ShapeDtypeStruct(source.shape...]
    ppermute x0 -> x29, starting transfers between devices: none -> 45.5 us  [the longest x16 22.1 us: send(): return lax.ppermute(value, 'prow', pairs)]
    dot_general x4 -> x1, matrix products: 38.1 us -> 0.49 us  [body(): take = jnp.dot(hit1, to_top, preferred_element_type=F32)]
    all_gather x2 -> x1, waiting for transfers between devices: 33.5 us -> 0.01 us  [body(): lower = lax.all_gather(lower_panels, 'pcol', axis=1, tiled=True)]
  transfers between devices with their start and end apart: 6 -> 31, of which waited for: 6 -> 9; matrix products, arithmetic and copies ran while one was open for 13% -> 6% of each run, Pallas kernels for 0% -> 24%
where the time goes in v3:
time: 195 us
  waiting for transfers between devices  60.1 us (31%)
  Pallas kernels  58.9 us (30%)
  starting transfers between devices  45.6 us (23%)
  between operations  15.9 us (8%)
  other arithmetic  8.49 us (4%)
  local copies, waits for them, and re-layouts  5.09 us (3%)
    ppermute x16, waiting for transfers between devices, send(): return lax.ppermute(value, 'prow', pairs)  59.3 us
    ppermute x16, starting transfers between devices, send(): return lax.ppermute(value, 'prow', pairs)  22.1 us
    pallas_call x1, Pallas kernels, update(): pl.pallas_call(update_kernel, out_shape=jax.ShapeDtypeStruct(source.shape...  21.5 us
    ppermute x10, starting transfers between devices, swap_cores(): return lax.ppermute(value, 'prow', [(rank, rank ^ 1) for rank in range(32)])  17.7 us
    pallas_call x2, Pallas kernels, pick_rows(): pl.pallas_call(pick_kernel, out_shape=jax.ShapeDtypeStruct(shape, F32), i...  14.2 us
    pallas_call x1, Pallas kernels, put_tops(): pl.pallas_call(tops_kernel, out_shape=jax.ShapeDtypeStruct(matrix.shape,...  12.6 us
    pallas_call x1, Pallas kernels, own_tops(): pl.pallas_call(own_tops_kernel, out_shape=jax.ShapeDtypeStruct((2 * NB, c...  6.34 us
    ppermute x3, starting transfers between devices, body(): lax.ppermute(lower_own, 'pcol', [(i, (i - d) % 4) for i in range(4)])  5.71 us
  transfers between devices with their start and end apart: 31, of which 9 were waited for; matrix products, arithmetic and copies ran while one was open for 6% of the time, Pallas kernels for 24%

profile of v3, /device:TPU:1, one launch (start us, length us, event | category | flops | bytes accessed | tf_op | source)
XLA Modules:
  0.0 194.6 jit_solution(13643909108844280950)
XLA Ops:
  7.4 0.7 all-gather.2.cloned.1.call-update
  8.1 0.9 slice_bitcast_fusion.8
  9.1 2.1 %collective-permute-start.11 = (f32[192,256]{1,0:T(8,128)S(1)}, f32[192,256]{1,0:T(8,128)S(1)}, u32[]{:S(2)}, u32[]{:S(2)}) collective-permute-start(f32[192,256]{1,0:T(8,128)S(1)} %slice_bitcast_fusion.8), channel_id=1, source_target_pairs={{0,1},{1,2},{2,3},{3,0},{4,5},{5,6},{6,7},{7,4},{8,9},{9,10},{10,1... | collective-permute-start | bytes 589832 | tf_op jit(solution)/shard_map/ppermute | solution.py:423
  11.2 2.5 %collective-permute-start.10 = (f32[192,256]{1,0:T(8,128)S(1)}, f32[192,256]{1,0:T(8,128)S(1)}, u32[]{:S(2)}, u32[]{:S(2)}) collective-permute-start(f32[192,256]{1,0:T(8,128)S(1)} %slice_bitcast_fusion.8), channel_id=1, source_target_pairs={{0,2},{1,3},{2,0},{3,1},{4,6},{5,7},{6,4},{7,5},{8,10},{9,11},{10,... | collective-permute-start | bytes 589832 | tf_op jit(solution)/shard_map/ppermute | solution.py:423
  13.6 1.2 collective-permute-start.9
  14.9 6.3 %own_tops.1 = f32[512,4096]{1,0:T(8,128)} custom-call(s32[4]{0:T(128)S(1)} %add_add_fusion.place_ref, f32[768,4096]{1,0:T(8,128)} %matrix_ref.1), custom_call_target="tpu_custom_call" | custom-call | bytes 8388608 | tf_op jit(solution)/shard_map/own_tops/pallas_call | solution.py:391
  21.3 0.6 copy-done.15
  21.9 0.5 slice.84
  22.4 0.2 compare_reduce_fusion.2
  22.6 0.2 fusion.26
  23.8 0.7 broadcast_in_dim.58
  24.5 73.8 %while.11 = (s32[]{:T(128)}, f32[544,128]{1,0:T(8,128)}, s32[]{:T(128)}, s32[4]{0:T(128)S(1)}, s32[4]{0:T(128)S(1)}, /*index=5*/f32[768,4096]{1,0:T(8,128)}, f32...) while((s32[]{:T(128)}, f32[544,128]{1,0:T(8,128)}, ...), condition=%wide.region_3.4_spmd.clone, body=%wide.region_2.3_spmd.clone.sunk | while | flops 7859032064 | bytes 116447808 | solution.py:470
  24.5 0.2 fusion.56.select_ref
  24.7 7.0 %pick_rows.2 = f32[4,4,512,128]{3,2,1,0:T(8,128)} custom-call(s32[4]{0:T(128)S(1)} %get-tuple-element.225.place_ref, f32[768,4096]{1,0:T(8,128)} %get-tuple-element.272.matrix_ref, bf16[512,768]{1,0:T(8,128)(2,1)S(1)} %fusion.56.select_ref), custom_call_target="tpu_custom_call" | custom-call | flops 3221225472 | bytes 10485760 | tf_op jit(solution)/shard_map/while/body/pick_rows/pallas_call | solution.py:96
  31.8 1.7 collective-permute-start
  33.6 0.3 fusion.58.select_ref
  33.9 7.2 %pick_rows.3 = f32[4,4,512,128]{3,2,1,0:T(8,128)} custom-call(s32[4]{0:T(128)S(1)} %get-tuple-element.227.place_ref, f32[768,4096]{1,0:T(8,128)} %get-tuple-element.272.matrix_ref, bf16[512,768]{1,0:T(8,128)(2,1)S(1)} %fusion.56.select_ref), custom_call_target="tpu_custom_call" | custom-call | flops 3221225472 | bytes 10485760 | tf_op jit(solution)/shard_map/while/body/pick_rows/pallas_call | solution.py:96
  41.2 2.0 %pick_extra.1 = f32[4,4,32,128]{3,2,1,0:T(8,128)S(1)} custom-call(s32[4]{0:T(128)S(1)} %get-tuple-element.270.place_ref, bf16[2,512,768]{2,1,0:T(8,128)(2,1)S(1)} %fusion.58.select_ref, f32[768,256]{1,0:T(8,128)S(1)} %get-tuple-element.273.own_ref, f32[768,256]{1,0:T(8,128)S(1)} %collective-permute-done.1.other_ref), custom_call_target="tpu_custom_call" | custom-call | flops 1207959552 | bytes 4194304 | tf_op jit(solution)/shard_map/while/body/pick_extra/pallas_call | solution.py:138
  43.2 0.2 copy-done
  43.3 2.7 %fusion.57 = (f32[4,512,128]{2,1,0:T(8,128)S(1)}, f32[4,512,128]{2,1,0:T(8,128)S(1)}, f32[4,512,128]{2,1,0:T(8,128)S(1)}, f32[4,512,128]{2,1,0:T(8,128)S(1)}) fusion(f32[4,4,512,128]{3,2,1,0:T(8,128)} %collective-permute-done, f32[4,4,512,128]{3,2,1,0:T(8,128)S(1)} %copy-done), kind=kLoop, calls=%fused_computation.26.clone.1 | loop fusion | flops 1048576 | bytes 12582912 | tf_op jit(solution)/shard_map/while/body/add | solution.py:456
  46.1 0.8 collective-permute-start.4
  46.9 2.0 %collective-permute-start.2 = (f32[2,544,128]{2,1,0:T(8,128)S(1)}, f32[2,544,128]{2,1,0:T(8,128)S(1)}, u32[]{:S(2)}, u32[]{:S(2)}) collective-permute-start(f32[2,544,128]{2,1,0:T(8,128)S(1)} %get-tuple-element.232), channel_id=1, source_target_pairs={{0,24},{4,100},{8,0},{12,108},{16,8},{20,116},{24,16},{28,124},{32... | collective-permute-start | bytes 1671176 | tf_op jit(solution)/shard_map/while/body/ppermute | solution.py:34
  48.8 12.1 %collective-permute-done.4 = f32[2,544,128]{2,1,0:T(8,128)S(1)} collective-permute-done((f32[2,544,128]{2,1,0:T(8,128)S(1)}, f32[2,544,128]{2,1,0:T(8,128)S(1)}, u32[]{:S(2)}, u32[]{:S(2)}) %collective-permute-start.4) | collective-permute-done | bytes 557088 | tf_op jit(solution)/shard_map/while/body/ppermute | solution.py:34
  61.2 0.6 collective-permute-start.5
  61.8 0.1 fusion.60
  62.0 2.8 %collective-permute-start.3 = (f32[4,544,128]{2,1,0:T(8,128)S(1)}, f32[4,544,128]{2,1,0:T(8,128)S(1)}, u32[]{:S(2)}, u32[]{:S(2)}) collective-permute-start(f32[4,544,128]{2,1,0:T(8,128)S(1)} %pad_maximum_fusion.7), channel_id=1, source_target_pairs={{0,24},{4,100},{8,0},{12,108},{16,8},{20,116},{24,16},{28,124},{32... | collective-permute-start | bytes 3342344 | tf_op jit(solution)/shard_map/while/body/ppermute | solution.py:34
  64.8 14.2 %collective-permute-done.5 = f32[4,544,128]{2,1,0:T(8,128)S(1)} collective-permute-done((f32[4,544,128]{2,1,0:T(8,128)S(1)}, f32[4,544,128]{2,1,0:T(8,128)S(1)}, u32[]{:S(2)}, u32[]{:S(2)}) %collective-permute-start.5) | collective-permute-done | bytes 1114144 | tf_op jit(solution)/shard_map/while/body/ppermute | solution.py:34
  79.1 0.2 fusion.63
  79.3 4.8 %collective-permute-start.6 = (f32[544,128]{1,0:T(8,128)S(1)}, f32[544,128]{1,0:T(8,128)}, u32[]{:S(2)}, u32[]{:S(2)}) collective-permute-start(f32[544,128]{1,0:T(8,128)S(1)} %get-tuple-element.240), channel_id=1, source_target_pairs={{0,96},{4,28},{8,104},{12,4},{16,112},{20,12},{24,120},{28,20},{32... | collective-permute-start | bytes 835592 | tf_op jit(solution)/shard_map/while/body/ppermute | solution.py:34
  84.1 1.3 collective-permute-start.8
  85.4 5.6 %collective-permute-done.6 = f32[544,128]{1,0:T(8,128)} collective-permute-done((f32[544,128]{1,0:T(8,128)S(1)}, f32[544,128]{1,0:T(8,128)}, u32[]{:S(2)}, u32[]{:S(2)}) %collective-permute-start.6) | collective-permute-done | bytes 278560 | tf_op jit(solution)/shard_map/while/body/ppermute | solution.py:34
  90.9 3.2 %collective-permute-done.7 = f32[544,128]{1,0:T(8,128)} collective-permute-done((f32[544,128]{1,0:T(8,128)S(1)}, f32[544,128]{1,0:T(8,128)}, u32[]{:S(2)}, u32[]{:S(2)}) %collective-permute-start.7) | collective-permute-done | bytes 278560 | tf_op jit(solution)/shard_map/while/body/ppermute | solution.py:34
  94.1 1.9 fusion.64.raw_ref
  96.0 2.3 %solve.1 = f32[544,128]{1,0:T(8,128)} custom-call(f32[544,128]{1,0:T(8,128)} %fusion.64.raw_ref, f32[2,256,256]{2,1,0:T(8,128)S(1)} %get-tuple-element.274.inverse_ref), custom_call_target="tpu_custom_call" | custom-call | flops 201326592 | bytes 1048576 | tf_op jit(solution)/shard_map/while/body/solve/pallas_call | solution.py:159
  98.3 1.4 collective-permute-start.13
  99.8 0.6 collective-permute-start.12
  100.4 5.6 %collective-permute-done.14 = f32[544,128]{1,0:T(8,128)S(1)} collective-permute-done((f32[544,128]{1,0:T(8,128)}, f32[544,128]{1,0:T(8,128)S(1)}, u32[]{:S(2)}, u32[]{:S(2)}) %collective-permute-start.14) | collective-permute-done | bytes 278560 | tf_op jit(solution)/shard_map/ppermute | solution.py:34
  106.0 1.0 pad_maximum_fusion.5.refs_0_
  107.0 4.9 %collective-permute-start.21 = (f32[2,544,128]{2,1,0:T(8,128)S(1)}, f32[2,544,128]{2,1,0:T(8,128)S(1)}, u32[]{:S(2)}, u32[]{:S(2)}) collective-permute-start(f32[2,544,128]{2,1,0:T(8,128)S(1)} %pad_maximum_fusion.5.refs_0_), channel_id=1, source_target_pairs={{0,4},{4,0},{8,12},{12,8},{16,20},{20,16},{24,28},{28,24},{32,36},... | collective-permute-start | bytes 1671176 | tf_op jit(solution)/shard_map/ppermute | solution.py:38
  111.9 2.7 %collective-permute-start.15 = (f32[2,544,128]{2,1,0:T(8,128)S(1)}, f32[2,544,128]{2,1,0:T(8,128)S(1)}, u32[]{:S(2)}, u32[]{:S(2)}) collective-permute-start(f32[2,544,128]{2,1,0:T(8,128)S(1)} %pad_maximum_fusion.5.refs_0_), channel_id=1, source_target_pairs={{0,24},{4,100},{8,0},{12,108},{16,8},{20,116},{24,16},{28,124},{32... | collective-permute-start | bytes 1671176 | tf_op jit(solution)/shard_map/ppermute | solution.py:34
  114.6 0.9 collective-permute-start.22
  115.5 1.5 collective-permute-start.16
  117.0 0.2 compare_reduce_fusion.1
  117.4 4.4 %collective-permute-done.17.refs_6_ = f32[2,544,128]{2,1,0:T(8,128)S(1)} collective-permute-done((f32[2,544,128]{2,1,0:T(8,128)S(1)}, f32[2,544,128]{2,1,0:T(8,128)S(1)}, u32[]{:S(2)}, u32[]{:S(2)}) %collective-permute-start.17) | collective-permute-done | bytes 557088 | tf_op jit(solution)/shard_map/ppermute | solution.py:34
  121.8 1.1 collective-permute-start.27
  122.9 8.7 %collective-permute-done.16.refs_3_ = f32[2,544,128]{2,1,0:T(8,128)S(1)} collective-permute-done((f32[2,544,128]{2,1,0:T(8,128)S(1)}, f32[2,544,128]{2,1,0:T(8,128)S(1)}, u32[]{:S(2)}, u32[]{:S(2)}) %collective-permute-start.16) | collective-permute-done | bytes 557088 | tf_op jit(solution)/shard_map/ppermute | solution.py:34
  131.6 3.5 %collective-permute-start.19 = (f32[2,544,128]{2,1,0:T(8,128)S(1)}, f32[2,544,128]{2,1,0:T(8,128)S(1)}, u32[]{:S(2)}, u32[]{:S(2)}) collective-permute-start(f32[2,544,128]{2,1,0:T(8,128)S(1)} %collective-permute-done.16.refs_3_), channel_id=1, source_target_pairs={{0,24},{4,100},{8,0},{12,108},{16,8},{20,116},{24,16},{28,124},{32... | collective-permute-start | bytes 1671176 | tf_op jit(solution)/shard_map/ppermute | solution.py:34
  135.1 0.2 iota_compare_fusion.3
  135.3 0.2 fusion.21
  135.6 0.2 fusion.25.keep_ref
  135.8 2.3 %collective-permute-start.24 = (f32[2,544,128]{2,1,0:T(8,128)S(1)}, f32[2,544,128]{2,1,0:T(8,128)S(1)}, u32[]{:S(2)}, u32[]{:S(2)}) collective-permute-start(f32[2,544,128]{2,1,0:T(8,128)S(1)} %collective-permute-done.16.refs_3_), channel_id=1, source_target_pairs={{0,4},{4,0},{8,12},{12,8},{16,20},{20,16},{24,28},{28,24},{32,36},... | collective-permute-start | bytes 1671176 | tf_op jit(solution)/shard_map/ppermute | solution.py:38
  138.2 0.4 collective-permute-start.28
  138.6 3.8 %collective-permute-done.18.refs_4_ = f32[2,544,128]{2,1,0:T(8,128)S(1)} collective-permute-done((f32[2,544,128]{2,1,0:T(8,128)S(1)}, f32[2,544,128]{2,1,0:T(8,128)S(1)}, u32[]{:S(2)}, u32[]{:S(2)}) %collective-permute-start.18) | collective-permute-done | bytes 557088 | tf_op jit(solution)/shard_map/ppermute | solution.py:34
  142.3 2.9 %collective-permute-start.25 = (f32[2,544,128]{2,1,0:T(8,128)S(1)}, f32[2,544,128]{2,1,0:T(8,128)S(1)}, u32[]{:S(2)}, u32[]{:S(2)}) collective-permute-start(f32[2,544,128]{2,1,0:T(8,128)S(1)} %collective-permute-done.18.refs_4_), channel_id=1, source_target_pairs={{0,4},{4,0},{8,12},{12,8},{16,20},{20,16},{24,28},{28,24},{32,36},... | collective-permute-start | bytes 1671176 | tf_op jit(solution)/shard_map/ppermute | solution.py:38
  145.2 1.6 collective-permute-done.19.refs_5_
  146.9 3.3 %collective-permute-start.26 = (f32[2,544,128]{2,1,0:T(8,128)S(1)}, f32[2,544,128]{2,1,0:T(8,128)}, u32[]{:S(2)}, u32[]{:S(2)}) collective-permute-start(f32[2,544,128]{2,1,0:T(8,128)S(1)} %collective-permute-done.19.refs_5_), channel_id=1, source_target_pairs={{0,4},{4,0},{8,12},{12,8},{16,20},{20,16},{24,28},{28,24},{32,36},... | collective-permute-start | bytes 1671176 | tf_op jit(solution)/shard_map/ppermute | solution.py:38
  150.2 0.2 fusion.27
  150.4 0.5 add_convert_fusion.take_ref
  151.0 0.7 copy-done.12
  151.7 0.3 copy-done.13
  152.0 0.2 copy-done.11
  152.2 0.8 copy-done.14
  153.0 21.5 %update.1.matrix_ref = f32[768,4096]{1,0:T(8,128)} custom-call(s32[4]{0:T(128)S(1)} %get-tuple-element.342, f32[768,4096]{1,0:T(8,128)} %get-tuple-element.288, f32[768,1]{1,0:T(8,128)S(1)} %fusion.25.keep_ref, bf16[768,256]{1,0:T(8,128)(2,1)S(1)} %get-tuple-element.143.hit_ref, f32[2,768,256]{2,1,0:T(8,128)} %all-gather.2.cloned.1.call-done.lower_ref, ...), custom_call_target="tpu_custom_call" | custom-call | flops 9663676416 | bytes 34603008 | tf_op jit(solution)/shard_map/update/pallas_call | solution.py:323
  174.5 12.6 %put_tops.1 = f32[768,4096]{1,0:T(8,128)} custom-call(f32[768,4096]{1,0:T(8,128)} %update.1.matrix_ref, f32[512,4096]{1,0:T(8,128)} %all-reduce.3.cloned.1.call-done.top_ref, bf16[768,512]{1,0:T(8,128)(2,1)S(1)} %add_convert_fusion.take_ref), custom_call_target="tpu_custom_call", output_to_operand_aliasing={{}: (0, {})} | custom-call | flops 6442450944 | bytes 33554432 | tf_op jit(solution)/shard_map/put_tops/pallas_call | solution.py:217
  (83 shorter events, 1.4 us)
Async XLA Ops:
  7.4 145.6 %all-gather.2.cloned.1.call-start = ((), (), s32[]{:S(2)}) async-start(), calls=%async_computation | async-start | bytes 1966080 | tf_op jit(solution)/shard_map/all_gather | solution.py:421
  8.1 166.4 %all-reduce.3.cloned.1.call-start = ((), (), s32[]{:S(2)}) async-start(), calls=%async_computation.1 | async-start | bytes 16777216 | tf_op jit(solution)/shard_map/psum | solution.py:419
  9.1 14.6 %collective-permute-start.11 = (f32[192,256]{1,0:T(8,128)S(1)}, f32[192,256]{1,0:T(8,128)S(1)}, u32[]{:S(2)}, u32[]{:S(2)}) collective-permute-start(f32[192,256]{1,0:T(8,128)S(1)} %slice_bitcast_fusion.8), channel_id=1, source_target_pairs={{0,1},{1,2},{2,3},{3,0},{4,5},{5,6},{6,7},{7,4},{8,9},{9,10},{10,1... | collective-permute-start | bytes 589832 | tf_op jit(solution)/shard_map/ppermute | solution.py:423
  11.2 12.5 %collective-permute-start.10 = (f32[192,256]{1,0:T(8,128)S(1)}, f32[192,256]{1,0:T(8,128)S(1)}, u32[]{:S(2)}, u32[]{:S(2)}) collective-permute-start(f32[192,256]{1,0:T(8,128)S(1)} %slice_bitcast_fusion.8), channel_id=1, source_target_pairs={{0,2},{1,3},{2,0},{3,1},{4,6},{5,7},{6,4},{7,5},{8,10},{9,11},{10,... | collective-permute-start | bytes 589832 | tf_op jit(solution)/shard_map/ppermute | solution.py:423
  13.6 10.1 %collective-permute-start.9 = (f32[192,256]{1,0:T(8,128)S(1)}, f32[192,256]{1,0:T(8,128)S(1)}, u32[]{:S(2)}, u32[]{:S(2)}) collective-permute-start(f32[192,256]{1,0:T(8,128)S(1)} %slice_bitcast_fusion.8), channel_id=1, source_target_pairs={{0,3},{1,0},{2,1},{3,2},{4,7},{5,4},{6,5},{7,6},{8,11},{9,8},{10,9... | collective-permute-start | bytes 589832 | tf_op jit(solution)/shard_map/ppermute | solution.py:423
  21.2 0.7 copy-start.15
  21.3 3.3 %copy-start.1 = (f32[2,256,256]{2,1,0:T(8,128)S(1)}, f32[2,256,256]{2,1,0:T(8,128)}, u32[]{:S(2)}) copy-start(f32[2,256,256]{2,1,0:T(8,128)} %inverse_ref.1) | copy-start | bytes 1572868
  31.8 11.4 %collective-permute-start = (f32[4,4,512,128]{3,2,1,0:T(8,128)}, f32[4,4,512,128]{3,2,1,0:T(8,128)}, u32[]{:S(2)}, u32[]{:S(2)}) collective-permute-start(f32[4,4,512,128]{3,2,1,0:T(8,128)} %pick_rows.2), channel_id=1, source_target_pairs={{0,4},{4,0},{8,12},{12,8},{16,20},{20,16},{24,28},{28,24},{32,36},... | collective-permute-start | bytes 12582920 | tf_op jit(solution)/shard_map/while/body/ppermute | solution.py:38
  33.5 7.6 %collective-permute-start.1 = (f32[768,256]{1,0:T(8,128)S(1)}, f32[768,256]{1,0:T(8,128)S(1)}, u32[]{:S(2)}, u32[]{:S(2)}) collective-permute-start(f32[768,256]{1,0:T(8,128)S(1)} %broadcast_select_fusion.2), channel_id=1, source_target_pairs={{0,4},{4,0},{8,12},{12,8},{16,20},{20,16},{24,28},{28,24},{32,36},... | collective-permute-start | bytes 2359304 | tf_op jit(solution)/shard_map/while/body/ppermute | solution.py:38
  41.2 2.2 %copy-start = (f32[4,4,512,128]{3,2,1,0:T(8,128)S(1)}, f32[4,4,512,128]{3,2,1,0:T(8,128)}, u32[]{:S(2)}) copy-start(f32[4,4,512,128]{3,2,1,0:T(8,128)} %pick_rows.3) | copy-start | bytes 12582916 | tf_op jit(solution)/shard_map/while
  46.1 14.9 %collective-permute-start.4 = (f32[2,544,128]{2,1,0:T(8,128)S(1)}, f32[2,544,128]{2,1,0:T(8,128)S(1)}, u32[]{:S(2)}, u32[]{:S(2)}) collective-permute-start(f32[2,544,128]{2,1,0:T(8,128)S(1)} %get-tuple-element.236), channel_id=1, source_target_pairs={{0,8},{4,36},{8,16},{12,44},{16,24},{20,52},{24,0},{28,60},{32,40}... | collective-permute-start | bytes 1671176 | tf_op jit(solution)/shard_map/while/body/ppermute | solution.py:34
  46.9 14.9 %collective-permute-start.2 = (f32[2,544,128]{2,1,0:T(8,128)S(1)}, f32[2,544,128]{2,1,0:T(8,128)S(1)}, u32[]{:S(2)}, u32[]{:S(2)}) collective-permute-start(f32[2,544,128]{2,1,0:T(8,128)S(1)} %get-tuple-element.232), channel_id=1, source_target_pairs={{0,24},{4,100},{8,0},{12,108},{16,8},{20,116},{24,16},{28,124},{32... | collective-permute-start | bytes 1671176 | tf_op jit(solution)/shard_map/while/body/ppermute | solution.py:34
  61.2 17.9 %collective-permute-start.5 = (f32[4,544,128]{2,1,0:T(8,128)S(1)}, f32[4,544,128]{2,1,0:T(8,128)S(1)}, u32[]{:S(2)}, u32[]{:S(2)}) collective-permute-start(f32[4,544,128]{2,1,0:T(8,128)S(1)} %fusion.62), channel_id=1, source_target_pairs={{0,8},{4,36},{8,16},{12,44},{16,24},{20,52},{24,0},{28,60},{32,40}... | collective-permute-start | bytes 3342344 | tf_op jit(solution)/shard_map/while/body/ppermute | solution.py:34
  62.0 17.1 %collective-permute-start.3 = (f32[4,544,128]{2,1,0:T(8,128)S(1)}, f32[4,544,128]{2,1,0:T(8,128)S(1)}, u32[]{:S(2)}, u32[]{:S(2)}) collective-permute-start(f32[4,544,128]{2,1,0:T(8,128)S(1)} %pad_maximum_fusion.7), channel_id=1, source_target_pairs={{0,24},{4,100},{8,0},{12,108},{16,8},{20,116},{24,16},{28,124},{32... | collective-permute-start | bytes 3342344 | tf_op jit(solution)/shard_map/while/body/ppermute | solution.py:34
  79.3 11.6 %collective-permute-start.6 = (f32[544,128]{1,0:T(8,128)S(1)}, f32[544,128]{1,0:T(8,128)}, u32[]{:S(2)}, u32[]{:S(2)}) collective-permute-start(f32[544,128]{1,0:T(8,128)S(1)} %get-tuple-element.240), channel_id=1, source_target_pairs={{0,96},{4,28},{8,104},{12,4},{16,112},{20,12},{24,120},{28,20},{32... | collective-permute-start | bytes 835592 | tf_op jit(solution)/shard_map/while/body/ppermute | solution.py:34
  84.1 10.0 %collective-permute-start.7 = (f32[544,128]{1,0:T(8,128)S(1)}, f32[544,128]{1,0:T(8,128)}, u32[]{:S(2)}, u32[]{:S(2)}) collective-permute-start(f32[544,128]{1,0:T(8,128)S(1)} %get-tuple-element.241), channel_id=1, source_target_pairs={{0,32},{4,12},{8,40},{12,20},{16,48},{20,28},{24,56},{28,4},{32,64... | collective-permute-start | bytes 835592 | tf_op jit(solution)/shard_map/while/body/ppermute | solution.py:34
  84.1 10.0 %collective-permute-start.8 = (f32[544,128]{1,0:T(8,128)S(1)}, f32[544,128]{1,0:T(8,128)}, u32[]{:S(2)}, u32[]{:S(2)}) collective-permute-start(f32[544,128]{1,0:T(8,128)S(1)} %get-tuple-element.242), channel_id=1, source_target_pairs={{0,64},{4,20},{8,72},{12,28},{16,80},{20,4},{24,88},{28,12},{32,96... | collective-permute-start | bytes 835592 | tf_op jit(solution)/shard_map/while/body/ppermute | solution.py:34
  98.3 7.7 %collective-permute-start.14 = (f32[544,128]{1,0:T(8,128)}, f32[544,128]{1,0:T(8,128)S(1)}, u32[]{:S(2)}, u32[]{:S(2)}) collective-permute-start(f32[544,128]{1,0:T(8,128)} %get-tuple-element.61), channel_id=1, source_target_pairs={{0,96},{4,28},{8,104},{12,4},{16,112},{20,12},{24,120},{28,20},{32... | collective-permute-start | bytes 835592 | tf_op jit(solution)/shard_map/ppermute | solution.py:34
  98.3 16.2 %collective-permute-start.13 = (f32[544,128]{1,0:T(8,128)}, f32[544,128]{1,0:T(8,128)S(1)}, u32[]{:S(2)}, u32[]{:S(2)}) collective-permute-start(f32[544,128]{1,0:T(8,128)} %get-tuple-element.61), channel_id=1, source_target_pairs={{0,32},{4,12},{8,40},{12,20},{16,48},{20,28},{24,56},{28,4},{32,64... | collective-permute-start | bytes 835592 | tf_op jit(solution)/shard_map/ppermute | solution.py:34
  99.8 14.8 %collective-permute-start.12 = (f32[544,128]{1,0:T(8,128)}, f32[544,128]{1,0:T(8,128)S(1)}, u32[]{:S(2)}, u32[]{:S(2)}) collective-permute-start(f32[544,128]{1,0:T(8,128)} %get-tuple-element.61), channel_id=1, source_target_pairs={{0,64},{4,20},{8,72},{12,28},{16,80},{20,4},{24,88},{28,12},{32,96... | collective-permute-start | bytes 835592 | tf_op jit(solution)/shard_map/ppermute | solution.py:34
  107.0 10.3 %collective-permute-start.21 = (f32[2,544,128]{2,1,0:T(8,128)S(1)}, f32[2,544,128]{2,1,0:T(8,128)S(1)}, u32[]{:S(2)}, u32[]{:S(2)}) collective-permute-start(f32[2,544,128]{2,1,0:T(8,128)S(1)} %pad_maximum_fusion.5.refs_0_), channel_id=1, source_target_pairs={{0,4},{4,0},{8,12},{12,8},{16,20},{20,16},{24,28},{28,24},{32,36},... | collective-permute-start | bytes 1671176 | tf_op jit(solution)/shard_map/ppermute | solution.py:38
  111.9 9.9 %collective-permute-start.17 = (f32[2,544,128]{2,1,0:T(8,128)S(1)}, f32[2,544,128]{2,1,0:T(8,128)S(1)}, u32[]{:S(2)}, u32[]{:S(2)}) collective-permute-start(f32[2,544,128]{2,1,0:T(8,128)S(1)} %pad_maximum_fusion.5.refs_0_), channel_id=1, source_target_pairs={{0,8},{4,36},{8,16},{12,44},{16,24},{20,52},{24,0},{28,60},{32,40}... | collective-permute-start | bytes 1671176 | tf_op jit(solution)/shard_map/ppermute | solution.py:34
  111.9 11.0 %collective-permute-start.15 = (f32[2,544,128]{2,1,0:T(8,128)S(1)}, f32[2,544,128]{2,1,0:T(8,128)S(1)}, u32[]{:S(2)}, u32[]{:S(2)}) collective-permute-start(f32[2,544,128]{2,1,0:T(8,128)S(1)} %pad_maximum_fusion.5.refs_0_), channel_id=1, source_target_pairs={{0,24},{4,100},{8,0},{12,108},{16,8},{20,116},{24,16},{28,124},{32... | collective-permute-start | bytes 1671176 | tf_op jit(solution)/shard_map/ppermute | solution.py:34
  114.6 21.1 %collective-permute-start.22 = (f32[2,544,128]{2,1,0:T(8,128)S(1)}, f32[2,544,128]{2,1,0:T(8,128)S(1)}, u32[]{:S(2)}, u32[]{:S(2)}) collective-permute-start(f32[2,544,128]{2,1,0:T(8,128)S(1)} %pad_maximum_fusion.4.refs_1_), channel_id=1, source_target_pairs={{0,4},{4,0},{8,12},{12,8},{16,20},{20,16},{24,28},{28,24},{32,36},... | collective-permute-start | bytes 1671176 | tf_op jit(solution)/shard_map/ppermute | solution.py:38
  115.5 16.1 %collective-permute-start.16 = (f32[2,544,128]{2,1,0:T(8,128)S(1)}, f32[2,544,128]{2,1,0:T(8,128)S(1)}, u32[]{:S(2)}, u32[]{:S(2)}) collective-permute-start(f32[2,544,128]{2,1,0:T(8,128)S(1)} %pad_maximum_fusion.4.refs_1_), channel_id=1, source_target_pairs={{0,24},{4,100},{8,0},{12,108},{16,8},{20,116},{24,16},{28,124},{32... | collective-permute-start | bytes 1671176 | tf_op jit(solution)/shard_map/ppermute | solution.py:34
  117.3 18.1 %copy-start.2 = (f32[2,544,128]{2,1,0:T(8,128)}, f32[2,544,128]{2,1,0:T(8,128)S(1)}, u32[]{:S(2)}) copy-start(f32[2,544,128]{2,1,0:T(8,128)S(1)} %collective-permute-done.21.refs_8_) | copy-start | bytes 1671172
  117.3 20.8 %collective-permute-start.20 = (f32[2,544,128]{2,1,0:T(8,128)S(1)}, f32[2,544,128]{2,1,0:T(8,128)S(1)}, u32[]{:S(2)}, u32[]{:S(2)}) collective-permute-start(f32[2,544,128]{2,1,0:T(8,128)S(1)} %pad_maximum_fusion.4.refs_1_), channel_id=1, source_target_pairs={{0,8},{4,36},{8,16},{12,44},{16,24},{20,52},{24,0},{28,60},{32,40}... | collective-permute-start | bytes 1671176 | tf_op jit(solution)/shard_map/ppermute | solution.py:34
  121.8 28.6 %copy-start.3 = (f32[2,544,128]{2,1,0:T(8,128)}, f32[2,544,128]{2,1,0:T(8,128)S(1)}, u32[]{:S(2)}) copy-start(f32[2,544,128]{2,1,0:T(8,128)S(1)} %collective-permute-done.17.refs_6_) | copy-start | bytes 1671172
  121.8 16.4 %collective-permute-start.27 = (f32[2,544,128]{2,1,0:T(8,128)S(1)}, f32[2,544,128]{2,1,0:T(8,128)S(1)}, u32[]{:S(2)}, u32[]{:S(2)}) collective-permute-start(f32[2,544,128]{2,1,0:T(8,128)S(1)} %collective-permute-done.17.refs_6_), channel_id=1, source_target_pairs={{0,4},{4,0},{8,12},{12,8},{16,20},{20,16},{24,28},{28,24},{32,36},... | collective-permute-start | bytes 1671176 | tf_op jit(solution)/shard_map/ppermute | solution.py:38
  122.9 28.0 %copy-start.4 = (f32[2,544,128]{2,1,0:T(8,128)}, f32[2,544,128]{2,1,0:T(8,128)S(1)}, u32[]{:S(2)}) copy-start(f32[2,544,128]{2,1,0:T(8,128)S(1)} %collective-permute-done.15.refs_2_) | copy-start | bytes 1671172
  122.9 19.4 %collective-permute-start.18 = (f32[2,544,128]{2,1,0:T(8,128)S(1)}, f32[2,544,128]{2,1,0:T(8,128)S(1)}, u32[]{:S(2)}, u32[]{:S(2)}) collective-permute-start(f32[2,544,128]{2,1,0:T(8,128)S(1)} %collective-permute-done.17.refs_6_), channel_id=1, source_target_pairs={{0,8},{4,36},{8,16},{12,44},{16,24},{20,52},{24,0},{28,60},{32,40}... | collective-permute-start | bytes 1671176 | tf_op jit(solution)/shard_map/ppermute | solution.py:34
  131.6 19.3 %copy-start.6 = (f32[2,544,128]{2,1,0:T(8,128)}, f32[2,544,128]{2,1,0:T(8,128)S(1)}, u32[]{:S(2)}) copy-start(f32[2,544,128]{2,1,0:T(8,128)S(1)} %collective-permute-done.16.refs_3_) | copy-start | bytes 1671172
  131.6 15.3 %collective-permute-start.19 = (f32[2,544,128]{2,1,0:T(8,128)S(1)}, f32[2,544,128]{2,1,0:T(8,128)S(1)}, u32[]{:S(2)}, u32[]{:S(2)}) collective-permute-start(f32[2,544,128]{2,1,0:T(8,128)S(1)} %collective-permute-done.16.refs_3_), channel_id=1, source_target_pairs={{0,24},{4,100},{8,0},{12,108},{16,8},{20,116},{24,16},{28,124},{32... | collective-permute-start | bytes 1671176 | tf_op jit(solution)/shard_map/ppermute | solution.py:34
  135.7 14.6 %copy-start.5 = (f32[2,544,128]{2,1,0:T(8,128)}, f32[2,544,128]{2,1,0:T(8,128)S(1)}, u32[]{:S(2)}) copy-start(f32[2,544,128]{2,1,0:T(8,128)S(1)} %collective-permute-done.22.refs_9_) | copy-start | bytes 1671172
  135.8 15.2 %collective-permute-start.24 = (f32[2,544,128]{2,1,0:T(8,128)S(1)}, f32[2,544,128]{2,1,0:T(8,128)S(1)}, u32[]{:S(2)}, u32[]{:S(2)}) collective-permute-start(f32[2,544,128]{2,1,0:T(8,128)S(1)} %collective-permute-done.16.refs_3_), channel_id=1, source_target_pairs={{0,4},{4,0},{8,12},{12,8},{16,20},{20,16},{24,28},{28,24},{32,36},... | collective-permute-start | bytes 1671176 | tf_op jit(solution)/shard_map/ppermute | solution.py:38
  138.1 12.9 %copy-start.7 = (f32[2,544,128]{2,1,0:T(8,128)}, f32[2,544,128]{2,1,0:T(8,128)S(1)}, u32[]{:S(2)}) copy-start(f32[2,544,128]{2,1,0:T(8,128)S(1)} %collective-permute-done.20.refs_7_) | copy-start | bytes 1671172
  138.1 12.8 %collective-permute-start.23 = (f32[2,544,128]{2,1,0:T(8,128)S(1)}, f32[2,544,128]{2,1,0:T(8,128)S(1)}, u32[]{:S(2)}, u32[]{:S(2)}) collective-permute-start(f32[2,544,128]{2,1,0:T(8,128)S(1)} %collective-permute-done.15.refs_2_), channel_id=1, source_target_pairs={{0,4},{4,0},{8,12},{12,8},{16,20},{20,16},{24,28},{28,24},{32,36},... | collective-permute-start | bytes 1671176 | tf_op jit(solution)/shard_map/ppermute | solution.py:38
  138.2 12.2 %copy-start.8 = (f32[2,544,128]{2,1,0:T(8,128)}, f32[2,544,128]{2,1,0:T(8,128)S(1)}, u32[]{:S(2)}) copy-start(f32[2,544,128]{2,1,0:T(8,128)S(1)} %collective-permute-done.27.refs_14_) | copy-start | bytes 1671172
  138.2 12.8 %collective-permute-start.28 = (f32[2,544,128]{2,1,0:T(8,128)S(1)}, f32[2,544,128]{2,1,0:T(8,128)S(1)}, u32[]{:S(2)}, u32[]{:S(2)}) collective-permute-start(f32[2,544,128]{2,1,0:T(8,128)S(1)} %collective-permute-done.20.refs_7_), channel_id=1, source_target_pairs={{0,4},{4,0},{8,12},{12,8},{16,20},{20,16},{24,28},{28,24},{32,36},... | collective-permute-start | bytes 1671176 | tf_op jit(solution)/shard_map/ppermute | solution.py:38
  142.3 8.6 %copy-start.9 = (f32[2,544,128]{2,1,0:T(8,128)}, f32[2,544,128]{2,1,0:T(8,128)S(1)}, u32[]{:S(2)}) copy-start(f32[2,544,128]{2,1,0:T(8,128)S(1)} %collective-permute-done.18.refs_4_) | copy-start | bytes 1671172
  142.3 8.6 %collective-permute-start.25 = (f32[2,544,128]{2,1,0:T(8,128)S(1)}, f32[2,544,128]{2,1,0:T(8,128)S(1)}, u32[]{:S(2)}, u32[]{:S(2)}) collective-permute-start(f32[2,544,128]{2,1,0:T(8,128)S(1)} %collective-permute-done.18.refs_4_), channel_id=1, source_target_pairs={{0,4},{4,0},{8,12},{12,8},{16,20},{20,16},{24,28},{28,24},{32,36},... | collective-permute-start | bytes 1671176 | tf_op jit(solution)/shard_map/ppermute | solution.py:38
  146.9 4.1 %copy-start.10 = (f32[2,544,128]{2,1,0:T(8,128)}, f32[2,544,128]{2,1,0:T(8,128)S(1)}, u32[]{:S(2)}) copy-start(f32[2,544,128]{2,1,0:T(8,128)S(1)} %collective-permute-done.19.refs_5_) | copy-start | bytes 1671172
  146.9 6.1 %collective-permute-start.26 = (f32[2,544,128]{2,1,0:T(8,128)S(1)}, f32[2,544,128]{2,1,0:T(8,128)}, u32[]{:S(2)}, u32[]{:S(2)}) collective-permute-start(f32[2,544,128]{2,1,0:T(8,128)S(1)} %collective-permute-done.19.refs_5_), channel_id=1, source_target_pairs={{0,4},{4,0},{8,12},{12,8},{16,20},{20,16},{24,28},{28,24},{32,36},... | collective-permute-start | bytes 1671176 | tf_op jit(solution)/shard_map/ppermute | solution.py:38
  150.9 0.8 copy-start.12
  150.9 1.0 copy-start.13
  151.0 1.2 copy-start.11
  152.2 0.8 copy-start.14
Sparse Core Ops, SparseCore 0:
  9.8 29.6 all-gather.1
Sparse Core Ops, SparseCore 1:
  21.3 135.9 all-reduce.2

commit v4 on v3

--- a/solution.py
+++ b/solution.py
@@ -167,7 +167,8 @@
 
 
 def tops_kernel(
-    matrix_ref, top_ref, take_ref, out_ref, left_ref, tops_ref, blocks_ref, in_sems, out_sems
+    place_ref, matrix_ref, top_ref, other_ref, take_ref, out_ref, left_ref, tops_ref, blocks_ref,
+    in_sems, out_sems,
 ):
     width = 2 * LANES
 
@@ -175,10 +176,16 @@
         return pl.ds(pl.multiple_of(step * width, width), width)
 
     def fetches(step):
+        core = place_ref[0]
         return (
-            pltpu.make_async_copy(top_ref.at[:, lanes(step)], tops_ref.at[step], in_sems.at[0, step]),
             pltpu.make_async_copy(
-                matrix_ref.at[:, lanes(step)], blocks_ref.at[step], in_sems.at[1, step]
+                top_ref.at[:, lanes(step)], tops_ref.at[step, core], in_sems.at[0, step]
+            ),
+            pltpu.make_async_copy(
+                other_ref.at[:, lanes(step)], tops_ref.at[step, 1 - core], in_sems.at[1, step]
+            ),
+            pltpu.make_async_copy(
+                matrix_ref.at[:, lanes(step)], blocks_ref.at[step], in_sems.at[2, step]
             ),
         )
 
@@ -199,7 +206,7 @@
     def _(step):
         for copy in fetches(step):
             copy.wait()
-        high, low = split_two(tops_ref[step])
+        high, low = split_two(jnp.concatenate([tops_ref[step, 0], tops_ref[step, 1]], axis=0))
         right = jnp.concatenate([high, low], axis=0)
         total = jnp.dot(left_ref[...], right, preferred_element_type=F32)
         blocks_ref[step] = blocks_ref[step] + total
@@ -210,21 +217,21 @@
         store(step).wait()
 
 
-def put_tops(matrix, tops, take):
+def put_tops(place, matrix, tops, other_tops, take):
     rows = matrix.shape[0]
     hbm = pl.BlockSpec(memory_space=pl.ANY)
     vmem = pl.BlockSpec(memory_space=pltpu.VMEM)
     return pl.pallas_call(
         tops_kernel,
         out_shape=jax.ShapeDtypeStruct(matrix.shape, F32),
-        in_specs=[hbm, hbm, vmem],
+        in_specs=[pl.BlockSpec(memory_space=pltpu.SMEM), hbm, hbm, hbm, vmem],
         out_specs=hbm,
-        input_output_aliases={0: 0},
+        input_output_aliases={1: 0},
         scratch_shapes=[
             pltpu.VMEM((rows, 4 * NB), BF16),
-            pltpu.VMEM((16, 2 * NB, 2 * LANES), F32),
+            pltpu.VMEM((16, 2, NB, 2 * LANES), F32),
             pltpu.VMEM((16, rows, 2 * LANES), F32),
-            pltpu.SemaphoreType.DMA((2, 16)),
+            pltpu.SemaphoreType.DMA((3, 16)),
             pltpu.SemaphoreType.DMA((16,)),
         ],
         compiler_params=pltpu.CompilerParams(vmem_limit_bytes=52 << 20),
@@ -232,24 +239,35 @@
             flops=2 * rows * 4096 * 4 * NB, bytes_accessed=32 << 20, transcendentals=0
         ),
         name="put_tops",
-    )(matrix, tops, take)
-
-
-def update_kernel(place_ref, source_ref, keep_ref, hit_ref, lower_ref, inverse_ref, *refs):
+    )(place, matrix, tops, other_tops, take)
+
+
+def update_kernel(
+    place_ref, source_ref, keep_ref, hit_ref, lower0_ref, lower1_ref, inverse_ref, *refs
+):
     pieces = refs[:16]
     out_ref, left_ref, held_ref, flat_ref, blocks_ref, piece_sems, in_sems, out_sems = refs[16:]
     core, rank = place_ref[0], place_ref[3]
     width = 2 * LANES
-    copies = [
-        pltpu.make_async_copy(
-            pieces[side * 8 + slot],
-            held_ref.at[side, slot // 2, pl.ds(slot % 2 * 2, 2)],
-            piece_sems.at[side * 8 + slot],
-        )
-        for side in range(2)
-        for slot in range(8)
-    ]
-    for copy in copies:
+
+    def copies_of(first, count, part):
+        return [
+            pltpu.make_async_copy(
+                pieces[side * 8 + slot].at[:, pl.ds(first, count)],
+                held_ref.at[side, slot // 2, pl.ds(slot % 2 * 2, 2), pl.ds(first, count)],
+                piece_sems.at[part, side * 8 + slot],
+            )
+            for side in range(2)
+            for slot in range(8)
+        ]
+
+    def in_order(lower_ref):
+        piece = lower_ref.shape[0] // 4
+        starts = [(i + 4 - place_ref[4]) % 4 * piece for i in range(4)]
+        return jnp.concatenate([lower_ref[pl.ds(pl.multiple_of(i, 8), piece)] for i in starts])
+
+    extras, copies = copies_of(2 * NB, EXTRA, 0), copies_of(0, 2 * NB, 1)
+    for copy in extras + copies:
         copy.start()
 
     def lanes(step):
@@ -270,7 +288,7 @@
     def _(step):
         fetch(step).start()
 
-    for copy in copies:
+    for copy in extras:
         copy.wait()
     for side in range(2):
         for turn in range(4):
@@ -284,8 +302,8 @@
     weight = exact_dot(inverse_ref[1], pivot_rows)
     hit = hit_ref[...].astype(F32)
     swapped = jnp.max(hit, axis=1, keepdims=True) > 0.0
-    lower0 = jnp.where(swapped, exact_dot(hit, top_rows), lower_ref[0])
-    lower1 = lower_ref[1]
+    lower0 = jnp.where(swapped, exact_dot(hit, top_rows), in_order(lower0_ref))
+    lower1 = in_order(lower1_ref)
     lower0 = lower0 - exact_dot(lower1, weight)
     at_second = rank == 1
     lower0 = jnp.concatenate([jnp.where(at_second, weight, lower0[:NB]), lower0[NB:]], axis=0)
@@ -293,6 +311,8 @@
     high, low = split_two(-jnp.concatenate([lower0, lower1], axis=1))
     for i, part in enumerate((high, high, low)):
         left_ref[:, i * 2 * NB : (i + 1) * 2 * NB] = part
+    for copy in copies:
+        copy.wait()
 
     @pl.loop(0, 16)
     def _(step):
@@ -316,21 +336,21 @@
         store(step).wait()
 
 
-def update(place, source, keep, hit, lower, inverse, pieces):
+def update(place, source, keep, hit, lower0, lower1, inverse, pieces):
     rows, columns = source.shape
     hbm = pl.BlockSpec(memory_space=pl.ANY)
     vmem = pl.BlockSpec(memory_space=pltpu.VMEM)
     return pl.pallas_call(
         update_kernel,
         out_shape=jax.ShapeDtypeStruct(source.shape, F32),
-        in_specs=[pl.BlockSpec(memory_space=pltpu.SMEM), hbm] + [vmem] * 4 + [hbm] * 16,
+        in_specs=[pl.BlockSpec(memory_space=pltpu.SMEM), hbm] + [vmem] * 5 + [hbm] * 16,
         out_specs=hbm,
         scratch_shapes=[
             pltpu.VMEM((rows, 6 * NB), BF16),
             pltpu.VMEM((2, 4, 4, SHARE, LANES), F32),
             pltpu.VMEM((4 * NB, LANES), F32),
             pltpu.VMEM((16, rows, 2 * LANES), F32),
-            pltpu.SemaphoreType.DMA((16,)),
+            pltpu.SemaphoreType.DMA((2, 16)),
             pltpu.SemaphoreType.DMA((16,)),
             pltpu.SemaphoreType.DMA((16,)),
         ],
@@ -339,50 +359,38 @@
             flops=2 * rows * columns * 6 * NB, bytes_accessed=33 << 20, transcendentals=0
         ),
         name="update",
-    )(place, source, keep, hit, lower, inverse, *pieces)
-
-
-def own_tops_kernel(place_ref, matrix_ref, out_ref, zero_ref, held_ref, sems, zero_sems):
-    rank = place_ref[3]
-    zero_ref[...] = jnp.zeros_like(zero_ref)
-    width = zero_ref.shape[1]
-
-    def blanks(panel):
-        return [
-            pltpu.make_async_copy(
-                zero_ref,
-                out_ref.at[pl.ds(panel * NB, NB), pl.ds(i * width, width)],
-                zero_sems.at[panel, i],
-            )
-            for i in range(4)
-        ]
-
-    for panel in range(2):
-
-        @pl.when(rank != panel)
-        def _(panel=panel):
-            for copy in blanks(panel):
-                copy.start()
-
-    for panel in range(2):
-
-        @pl.when(rank == panel)
-        def _(panel=panel):
-            load = pltpu.make_async_copy(matrix_ref.at[pl.ds(0, NB)], held_ref, sems.at[0])
+    )(place, source, keep, hit, lower0, lower1, inverse, *pieces)
+
+
+def own_tops_kernel(place_ref, matrix_ref, out_ref, held_ref, sems):
+    at_root = place_ref[3] < 2
+    part = NB // 4
+    chunks = [pl.ds(i * part, part) for i in range(4)]
+    loads = [
+        pltpu.make_async_copy(matrix_ref.at[rows], held_ref.at[rows], sems.at[0, i])
+        for i, rows in enumerate(chunks)
+    ]
+    stores = [
+        pltpu.make_async_copy(held_ref.at[rows], out_ref.at[rows], sems.at[1, i])
+        for i, rows in enumerate(chunks)
+    ]
+
+    @pl.when(at_root)
+    def _():
+        for load in loads:
             load.start()
+        for load, store in zip(loads, stores):
             load.wait()
-            store = pltpu.make_async_copy(
-                held_ref, out_ref.at[pl.ds(panel * NB, NB)], sems.at[1]
-            )
             store.start()
-            store.wait()
-
-    for panel in range(2):
-
-        @pl.when(rank != panel)
-        def _(panel=panel):
-            for copy in blanks(panel):
-                copy.wait()
+
+    @pl.when(jnp.logical_not(at_root))
+    def _():
+        held_ref[...] = jnp.zeros_like(held_ref)
+        for store in stores:
+            store.start()
+
+    for store in stores:
+        store.wait()
 
 
 def own_tops(place, matrix):
@@ -390,17 +398,12 @@
     hbm = pl.BlockSpec(memory_space=pl.ANY)
     return pl.pallas_call(
         own_tops_kernel,
-        out_shape=jax.ShapeDtypeStruct((2 * NB, columns), F32),
+        out_shape=jax.ShapeDtypeStruct((NB, columns), F32),
         in_specs=[pl.BlockSpec(memory_space=pltpu.SMEM), hbm],
         out_specs=hbm,
-        scratch_shapes=[
-            pltpu.VMEM((NB, columns // 4), F32),
-            pltpu.VMEM((NB, columns), F32),
-            pltpu.SemaphoreType.DMA((2,)),
-            pltpu.SemaphoreType.DMA((2, 4)),
-        ],
+        scratch_shapes=[pltpu.VMEM((NB, columns), F32), pltpu.SemaphoreType.DMA((2, 4))],
         compiler_params=pltpu.CompilerParams(vmem_limit_bytes=VMEM_LIMIT),
-        cost_estimate=pl.CostEstimate(flops=0, bytes_accessed=8 << 20, transcendentals=0),
+        cost_estimate=pl.CostEstimate(flops=0, bytes_accessed=4 << 20, transcendentals=0),
         name="own_tops",
     )(place, matrix)
 
@@ -413,15 +416,15 @@
     second = jnp.where(core == 0, y, z)
     rows = matrix.shape[0]
     index = jnp.arange(NB, dtype=jnp.int32)
-    place = jnp.stack([core, y, z, rank]).astype(jnp.int32)
+    place = jnp.stack([core, y, z, rank, column_rank]).astype(jnp.int32)
     other_place = jnp.stack([1 - core, y, z, rank]).astype(jnp.int32)
 
-    tops = lax.psum(own_tops(place, matrix), "prow")
-
-    lower = lax.all_gather(lower_panels, "pcol", axis=1, tiled=True)
-    lower_own = lower_panels[0]
-    far = [lax.ppermute(lower_own, "pcol", [(i, (i - d) % 4) for i in range(4)]) for d in (1, 2, 3)]
-    lower_own = jnp.concatenate([lower_own] + far)
+    same_core = [[rank_of(y, z, core) for y in range(4) for z in range(4)] for core in range(2)]
+    tops = lax.psum(own_tops(place, matrix), "prow", axis_index_groups=same_core)
+
+    pairs = [[(i, (i - d) % 4) for i in range(4)] for d in (1, 2, 3)]
+    lower = [lower_panels] + [lax.ppermute(lower_panels, "pcol", pair) for pair in pairs]
+    lower_own, lower_last = (jnp.concatenate([part[panel] for part in lower]) for panel in range(2))
 
 
     pivot0, pivot1 = pivots[0], pivots[1]
@@ -445,66 +448,70 @@
     want = jnp.where(want >= 0, away, -1)
     want = (want[:, :, None] == local_row[None, None, :]).astype(BF16)
 
-    def exchange(turn, share):
-        lower_other = swap_cores(jnp.where(turn == 0, lower_own, 0.0))
-        sent = pick_rows(other_place + turn, select, matrix)
-        own_place, sent = lax.optimization_barrier((place + turn, sent))
-        other = swap_cores(sent)
-
-        kept = pick_rows(own_place, select, matrix)
+    lower_other = swap_cores(lower_own)
+    sent = pick_rows(other_place, select, matrix)
+    own_place, sent = lax.optimization_barrier((place, sent))
+    other = swap_cores(sent)
+
+    kept = pick_rows(own_place, select, matrix)
+
+    def exchange():
         extra = pick_extra(place, want, lower_own, lower_other)
         part = [jnp.concatenate([kept[d] + other[d], extra[d]], axis=1) for d in range(4)]
         ahead = send(part[2][:2], one=1)
         behind = send(part[2][2:], one=3)
-        part[1] = jnp.concatenate([part[1][:2] + ahead, part[1][2:]])
-        part[3] = jnp.concatenate([part[3][:2], part[3][2:] + behind])
-        part = part[0] + send(part[1], one=1) + send(part[3], one=3)
-
-        raw = part[0]
-        for d in (2, 1, 3):
-            raw = raw + send(part[d], two=d)
-
-        return solve(raw, inverses)
-
-    rounds = jnp.minimum(pivots[0, 0] + 1, 1)
-    share = lax.fori_loop(0, rounds, exchange, jnp.zeros((SHARE, LANES), F32))
-
-    near = {d: send(share, two=4 - d) for d in (1, 2, 3)}
-    low = jnp.stack([share, near[1]])
-    high = jnp.stack([near[2], near[3]])
-
-    pivots, high = lax.optimization_barrier((pivots, high))
-    pivot0, pivot1 = pivots[0], pivots[1]
-    again = pivot1[:, None] == pivot0[None, :]
-    takes0 = (pivot0 >= 2 * NB) & ~jnp.any(again, axis=0)
-    place0 = jnp.where(takes0, local(pivot0), -1)
-    hit0 = local_row[:, None] == place0[None, :]
-    hit1 = local_row[:, None] == local(pivot1)[None, :]
-    shifted = (NB + index)[:, None] == pivot0[None, :]
-    top1 = jnp.where(
-        jnp.any(shifted, axis=1),
-        jnp.sum(jnp.where(shifted, index[None, :], 0), axis=1),
-        NB + index,
-    )
-    to_top = (top1[:, None] == jnp.arange(2 * NB, dtype=jnp.int32)[None, :]).astype(BF16)
-    hit1 = hit1.astype(BF16)
-    take = jnp.dot(hit1, to_top, preferred_element_type=F32)
-    take = take + jnp.concatenate([hit0, jnp.zeros_like(hit0)], axis=1).astype(F32)
-    replaced = jnp.any(hit1 > 0, axis=1) | jnp.any(hit0, axis=1)
-    replaced = replaced | ((rank == 1) & (local_row < NB))
-    keep = jnp.where(replaced, 0.0, 1.0).astype(F32)[:, None]
-    take = take.astype(BF16)
-
-
-    low_before, high_after = send(low, one=1), send(high, one=3)
-    high_before, low_after = send(high, one=1), send(low, one=3)
-    low_across, high_across = send(low_before, one=1), send(high_after, one=3)
-    pieces = [
-        low, high, low_after, high_after, low_across, high_across, low_before, high_before
-    ]
-    pieces = pieces + [swap_cores(value) for value in pieces]
-    result = update(place, matrix, keep, hit1, lower, inverses, pieces)
-    return put_tops(result, tops, take)
+        high = part[0][2:] + send(part[1][2:], one=1)
+        low = part[0][:2] + send(part[3][:2], one=3)
+        low = low + send(part[1][:2] + ahead, one=1)
+        high = high + send(part[3][2:] + behind, one=3)
+        raw = low[0] + send(high[0], two=2) + send(low[1], two=1) + send(high[1], two=3)
+
+        share = solve(raw, inverses)
+
+        near = {d: send(share, two=4 - d) for d in (1, 2, 3)}
+        low = jnp.stack([share, near[1]])
+        high = jnp.stack([near[2], near[3]])
+
+        late, high = lax.optimization_barrier((pivots, high))
+        pivot0, pivot1 = late[0], late[1]
+        again = pivot1[:, None] == pivot0[None, :]
+        takes0 = (pivot0 >= 2 * NB) & ~jnp.any(again, axis=0)
+        place0 = jnp.where(takes0, local(pivot0), -1)
+        hit0 = local_row[:, None] == place0[None, :]
+        hit1 = local_row[:, None] == local(pivot1)[None, :]
+        shifted = (NB + index)[:, None] == pivot0[None, :]
+        top1 = jnp.where(
+            jnp.any(shifted, axis=1),
+            jnp.sum(jnp.where(shifted, index[None, :], 0), axis=1),
+            NB + index,
+        )
+        to_top = (top1[:, None] == jnp.arange(2 * NB, dtype=jnp.int32)[None, :]).astype(BF16)
+        hit1 = hit1.astype(BF16)
+        take = jnp.dot(hit1, to_top, preferred_element_type=F32)
+        take = take + jnp.concatenate([hit0, jnp.zeros_like(hit0)], axis=1).astype(F32)
+        replaced = jnp.any(hit1 > 0, axis=1) | jnp.any(hit0, axis=1)
+        replaced = replaced | ((rank == 1) & (local_row < NB))
+        keep = jnp.where(replaced, 0.0, 1.0).astype(F32)[:, None]
+        take = take.astype(BF16)
+
+
+        low_before, high_after = send(low, one=1), send(high, one=3)
+        high_before, low_after = send(high, one=1), send(low, one=3)
+        low_across, high_across = send(low_before, one=1), send(high_after, one=3)
+        pieces = [
+            low, high, low_after, high_after, low_across, high_across, low_before, high_before
+        ]
+        pieces = pieces + [swap_cores(value) for value in pieces]
+        return pieces, keep, take, hit1
+
+    def blank():
+        return jax.tree.map(lambda leaf: jnp.zeros(leaf.shape, leaf.dtype), jax.eval_shape(exchange))
+
+    pieces, keep, take, hit1 = lax.cond(pivots[0, 0] >= 0, exchange, blank)
+    tops, pieces[0] = lax.optimization_barrier((tops, pieces[0]))
+    other_tops = swap_cores(tops)
+    result = update(place, matrix, keep, hit1, lower_own, lower_last, inverses, pieces)
+    return put_tops(place, result, tops, other_tops, take)
 
 
 def solution(mesh):

time: 195 us -> 214 us (1.097)
  waiting for transfers between devices: 60.1 us -> 72.6 us
  starting transfers between devices: 45.6 us -> 56.9 us
  Pallas kernels: 58.9 us -> 54 us
    ppermute x3, waiting for transfers between devices: 0.01 us -> 19.8 us  [body(): lax.ppermute(lower_panels, 'pcol', pair)]
    ppermute x10 -> x11, starting transfers between devices: 17.7 us -> 29.5 us  [swap_cores(): return lax.ppermute(value, 'prow', [(rank, rank ^ 1) for rank in range(32)])]
    ppermute x16 -> x18, waiting for transfers between devices: 59.3 us -> 51.6 us  [send(): return lax.ppermute(value, 'prow', pairs)]
    pallas_call x1, Pallas kernels: 6.34 us -> 3.9 us  [own_tops(): pl.pallas_call(own_tops_kernel, out_shape=jax.ShapeDtypeStruct((NB, colum...]
    pallas_call x1, Pallas kernels: 21.5 us -> 19.2 us  [update(): pl.pallas_call(update_kernel, out_shape=jax.ShapeDtypeStruct(source.shape...]
    ppermute x16 -> x18, starting transfers between devices: 22.1 us -> 23.7 us  [send(): return lax.ppermute(value, 'prow', pairs)]
  transfers between devices with their start and end apart: 31 -> 33, of which waited for: 9 -> 14; matrix products, arithmetic and copies ran while one was open for 6% -> 5% of each run, Pallas kernels for 24% -> 16%
where the time goes in v4:
time: 214 us
  waiting for transfers between devices  72.6 us (34%)
  starting transfers between devices  56.9 us (27%)
  Pallas kernels  54 us (25%)
  between operations  14.3 us (7%)
  other arithmetic  9.79 us (5%)
  local copies, waits for them, and re-layouts  5.42 us (3%)
    ppermute x18, waiting for transfers between devices, send(): return lax.ppermute(value, 'prow', pairs)  51.6 us
    ppermute x11, starting transfers between devices, swap_cores(): return lax.ppermute(value, 'prow', [(rank, rank ^ 1) for rank in range(32)])  29.5 us
    ppermute x18, starting transfers between devices, send(): return lax.ppermute(value, 'prow', pairs)  23.7 us
    ppermute x3, waiting for transfers between devices, body(): lax.ppermute(lower_panels, 'pcol', pair)  19.8 us
    pallas_call x1, Pallas kernels, update(): pl.pallas_call(update_kernel, out_shape=jax.ShapeDtypeStruct(source.shape...  19.2 us
    pallas_call x2, Pallas kernels, pick_rows(): pl.pallas_call(pick_kernel, out_shape=jax.ShapeDtypeStruct(shape, F32), i...  13.4 us
    pallas_call x1, Pallas kernels, put_tops(): pl.pallas_call(tops_kernel, out_shape=jax.ShapeDtypeStruct(matrix.shape,...  13.3 us
  transfers between devices with their start and end apart: 33, of which 14 were waited for; matrix products, arithmetic and copies ran while one was open for 5% of the time, Pallas kernels for 16%

profile of v4, /device:TPU:1, one launch (start us, length us, event | category | flops | bytes accessed | tf_op | source)
XLA Modules:
  0.0 213.7 jit_solution(7357696571541762206)
XLA Ops:
  6.5 0.8 fusion.36
  7.3 0.2 fusion.23
  7.5 0.2 compare_reduce_fusion.3
  7.7 0.2 fusion.22.select_ref
  8.1 7.0 %pick_rows.2 = f32[4,4,512,128]{3,2,1,0:T(8,128)} custom-call(s32[4]{0:T(128)S(1)} %pad_add_fusion.3.place_ref, f32[768,4096]{1,0:T(8,128)} %source_ref.1, bf16[512,768]{1,0:T(8,128)(2,1)S(1)} %fusion.22.select_ref), custom_call_target="tpu_custom_call" | custom-call | flops 3221225472 | bytes 10485760 | tf_op jit(solution)/shard_map/pick_rows/pallas_call | solution.py:96
  15.1 1.5 collective-permute-start.26
  16.6 3.9 %own_tops.1 = f32[256,4096]{1,0:T(8,128)} custom-call(s32[5]{0:T(128)S(1)} %stack.55.place_ref, f32[768,4096]{1,0:T(8,128)} %source_ref.1), custom_call_target="tpu_custom_call" | custom-call | bytes 4194304 | tf_op jit(solution)/shard_map/own_tops/pallas_call | solution.py:399
  20.6 1.0 copy-done.2
  21.5 2.6 %collective-permute-start.27 = (f32[2,192,256]{2,1,0:T(8,128)S(1)}, f32[2,192,256]{2,1,0:T(8,128)S(1)}, u32[]{:S(2)}, u32[]{:S(2)}) collective-permute-start(f32[2,192,256]{2,1,0:T(8,128)S(1)} %copy-done.2), channel_id=1, source_target_pairs={{0,3},{1,0},{2,1},{3,2},{4,7},{5,4},{6,5},{7,6},{8,11},{9,8},{10,9... | collective-permute-start | bytes 1179656 | tf_op jit(solution)/shard_map/ppermute | solution.py:426
  24.1 0.5 collective-permute-start.28
  24.6 0.6 collective-permute-start.29
  25.3 15.6 %collective-permute-done.27 = f32[2,192,256]{2,1,0:T(8,128)S(1)} collective-permute-done((f32[2,192,256]{2,1,0:T(8,128)S(1)}, f32[2,192,256]{2,1,0:T(8,128)S(1)}, u32[]{:S(2)}, u32[]{:S(2)}) %collective-permute-start.27) | collective-permute-done | bytes 393248 | tf_op jit(solution)/shard_map/ppermute | solution.py:426
  41.0 4.2 %collective-permute-done.29 = f32[2,192,256]{2,1,0:T(8,128)S(1)} collective-permute-done((f32[2,192,256]{2,1,0:T(8,128)S(1)}, f32[2,192,256]{2,1,0:T(8,128)S(1)}, u32[]{:S(2)}, u32[]{:S(2)}) %collective-permute-start.29) | collective-permute-done | bytes 393248 | tf_op jit(solution)/shard_map/ppermute | solution.py:426
  45.2 0.7 slice_bitcast_fusion.8
  45.9 0.5 collective-permute-start.30
  46.4 0.6 slice.111
  47.6 0.3 fusion.21
  48.0 6.4 %pick_rows.3 = f32[4,4,512,128]{3,2,1,0:T(8,128)S(1)} custom-call(s32[5]{0:T(128)S(1)} %stack.55.place_ref, f32[768,4096]{1,0:T(8,128)} %source_ref.1, bf16[512,768]{1,0:T(8,128)(2,1)S(1)} %fusion.22.select_ref), custom_call_target="tpu_custom_call" | custom-call | flops 3221225472 | bytes 10485760 | tf_op jit(solution)/shard_map/pick_rows/pallas_call | solution.py:96
  54.4 116.5 %conditional.1 = (f32[2,544,128]{2,1,0:T(8,128)}, f32[2,544,128]{2,1,0:T(8,128)}, f32[2,544,128]{2,1,0:T(8,128)}, f32[2,544,128]{2,1,0:T(8,128)}, f32[2,544,128]...) conditional(s32[]{:T(128)} %bitcast.25, () %tuple.16, ...), branch_computations={%region_2.3_spmd, %region_3.9_spmd} | conditional | flops 1617268992 | bytes 88770224 | solution.py:510
  54.5 2.0 pick_extra.1
  56.5 2.7 %add_bitcast_fusion.3 = (f32[4,512,128]{2,1,0:T(8,128)S(1)}, f32[4,512,128]{2,1,0:T(8,128)S(1)}, f32[4,512,128]{2,1,0:T(8,128)S(1)}, f32[4,512,128]{2,1,0:T(8,128)S(1)}) fusion(f32[4,4,512,128]{3,2,1,0:T(8,128)} %get-tuple-element.30, f32[4,4,512,128]{3,2,1,0:T(8,128)S(1)} %get-tuple-element.10), kind=kLoop, calls=%fused_computation.12 | loop fusion | flops 1048576 | bytes 12582912 | tf_op jit(solution)/shard_map/cond/branch_1_fun/add | solution.py:460
  59.2 1.9 collective-permute-start.4
  61.1 9.9 %collective-permute-done.4 = f32[2,544,128]{2,1,0:T(8,128)S(1)} collective-permute-done((f32[2,544,128]{2,1,0:T(8,128)S(1)}, f32[2,544,128]{2,1,0:T(8,128)S(1)}, u32[]{:S(2)}, u32[]{:S(2)}) %collective-permute-start.4) | collective-permute-done | bytes 557088 | tf_op jit(solution)/shard_map/cond/branch_1_fun/ppermute | solution.py:34
  71.1 2.4 %collective-permute-start = (f32[2,544,128]{2,1,0:T(8,128)S(1)}, f32[2,544,128]{2,1,0:T(8,128)S(1)}, u32[]{:S(2)}, u32[]{:S(2)}) collective-permute-start(f32[2,544,128]{2,1,0:T(8,128)S(1)} %get-tuple-element.110), channel_id=1, source_target_pairs={{0,24},{4,100},{8,0},{12,108},{16,8},{20,116},{24,16},{28,124},{32... | collective-permute-start | bytes 1671176 | tf_op jit(solution)/shard_map/cond/branch_1_fun/ppermute | solution.py:34
  73.5 0.7 collective-permute-start.5
  74.3 0.8 collective-permute-start.2
  75.3 4.8 %collective-permute-done = f32[2,544,128]{2,1,0:T(8,128)S(1)} collective-permute-done((f32[2,544,128]{2,1,0:T(8,128)S(1)}, f32[2,544,128]{2,1,0:T(8,128)S(1)}, u32[]{:S(2)}, u32[]{:S(2)}) %collective-permute-start) | collective-permute-done | bytes 557088 | tf_op jit(solution)/shard_map/cond/branch_1_fun/ppermute | solution.py:34
  80.0 7.9 %collective-permute-done.5 = f32[2,544,128]{2,1,0:T(8,128)S(1)} collective-permute-done((f32[2,544,128]{2,1,0:T(8,128)S(1)}, f32[2,544,128]{2,1,0:T(8,128)S(1)}, u32[]{:S(2)}, u32[]{:S(2)}) %collective-permute-start.5) | collective-permute-done | bytes 557088 | tf_op jit(solution)/shard_map/cond/branch_1_fun/ppermute | solution.py:34
  88.0 5.0 %collective-permute-done.3 = f32[2,544,128]{2,1,0:T(8,128)S(1)} collective-permute-done((f32[2,544,128]{2,1,0:T(8,128)S(1)}, f32[2,544,128]{2,1,0:T(8,128)S(1)}, u32[]{:S(2)}, u32[]{:S(2)}) %collective-permute-start.3) | collective-permute-done | bytes 557088 | tf_op jit(solution)/shard_map/cond/branch_1_fun/ppermute | solution.py:34
  93.2 4.7 %collective-permute-start.6 = (f32[544,128]{1,0:T(8,128)S(1)}, f32[544,128]{1,0:T(8,128)S(1)}, u32[]{:S(2)}, u32[]{:S(2)}) collective-permute-start(f32[544,128]{1,0:T(8,128)S(1)} %get-tuple-element.116), channel_id=1, source_target_pairs={{0,64},{4,20},{8,72},{12,28},{16,80},{20,4},{24,88},{28,12},{32,96... | collective-permute-start | bytes 835592 | tf_op jit(solution)/shard_map/cond/branch_1_fun/ppermute | solution.py:34
  97.8 0.5 collective-permute-start.8
  98.3 1.2 collective-permute-start.7
  99.6 2.2 %collective-permute-done.6 = f32[544,128]{1,0:T(8,128)S(1)} collective-permute-done((f32[544,128]{1,0:T(8,128)S(1)}, f32[544,128]{1,0:T(8,128)S(1)}, u32[]{:S(2)}, u32[]{:S(2)}) %collective-permute-start.6) | collective-permute-done | bytes 278560 | tf_op jit(solution)/shard_map/cond/branch_1_fun/ppermute | solution.py:34
  101.8 4.3 %collective-permute-done.8 = f32[544,128]{1,0:T(8,128)S(1)} collective-permute-done((f32[544,128]{1,0:T(8,128)S(1)}, f32[544,128]{1,0:T(8,128)S(1)}, u32[]{:S(2)}, u32[]{:S(2)}) %collective-permute-start.8) | collective-permute-done | bytes 278560 | tf_op jit(solution)/shard_map/cond/branch_1_fun/ppermute | solution.py:34
  106.0 0.8 fusion.15.raw_ref
  106.8 2.3 %solve.1 = f32[544,128]{1,0:T(8,128)} custom-call(f32[544,128]{1,0:T(8,128)} %fusion.15.raw_ref, f32[2,256,256]{2,1,0:T(8,128)S(1)} %get-tuple-element.37.inverse_ref), custom_call_target="tpu_custom_call" | custom-call | flops 201326592 | bytes 1048576 | tf_op jit(solution)/shard_map/cond/branch_1_fun/solve/pallas_call | solution.py:159
  109.1 2.0 collective-permute-start.10
  111.0 0.5 collective-permute-start.11
  111.5 2.2 %collective-permute-start.9 = (f32[544,128]{1,0:T(8,128)}, f32[544,128]{1,0:T(8,128)S(1)}, u32[]{:S(2)}, u32[]{:S(2)}) collective-permute-start(f32[544,128]{1,0:T(8,128)} %solve.1), channel_id=1, source_target_pairs={{0,96},{4,28},{8,104},{12,4},{16,112},{20,12},{24,120},{28,20},{32... | collective-permute-start | bytes 835592 | tf_op jit(solution)/shard_map/cond/branch_1_fun/ppermute | solution.py:34
  113.7 8.4 %collective-permute-done.10 = f32[544,128]{1,0:T(8,128)S(1)} collective-permute-done((f32[544,128]{1,0:T(8,128)}, f32[544,128]{1,0:T(8,128)S(1)}, u32[]{:S(2)}, u32[]{:S(2)}) %collective-permute-start.10) | collective-permute-done | bytes 278560 | tf_op jit(solution)/shard_map/cond/branch_1_fun/ppermute | solution.py:34
  122.2 4.4 %collective-permute-done.11 = f32[544,128]{1,0:T(8,128)S(1)} collective-permute-done((f32[544,128]{1,0:T(8,128)}, f32[544,128]{1,0:T(8,128)S(1)}, u32[]{:S(2)}, u32[]{:S(2)}) %collective-permute-start.11) | collective-permute-done | bytes 278560 | tf_op jit(solution)/shard_map/cond/branch_1_fun/ppermute | solution.py:34
  126.6 0.8 pad_maximum_fusion.5
  127.5 1.5 collective-permute-start.17
  128.9 14.0 %collective-permute-start.19 = (f32[2,544,128]{2,1,0:T(8,128)}, f32[2,544,128]{2,1,0:T(8,128)}, u32[]{:S(2)}, u32[]{:S(2)}) collective-permute-start(f32[2,544,128]{2,1,0:T(8,128)} %pad_maximum_fusion.5), channel_id=1, source_target_pairs={{0,4},{4,0},{8,12},{12,8},{16,20},{20,16},{24,28},{28,24},{32,36},... | collective-permute-start | bytes 1671176 | tf_op jit(solution)/shard_map/cond/branch_1_fun/ppermute | solution.py:38
  142.9 1.9 pad_maximum_fusion.4
  144.8 2.7 %collective-permute-start.12 = (f32[2,544,128]{2,1,0:T(8,128)}, f32[2,544,128]{2,1,0:T(8,128)}, u32[]{:S(2)}, u32[]{:S(2)}) collective-permute-start(f32[2,544,128]{2,1,0:T(8,128)} %pad_maximum_fusion.4), channel_id=1, source_target_pairs={{0,24},{4,100},{8,0},{12,108},{16,8},{20,116},{24,16},{28,124},{32... | collective-permute-start | bytes 1671176 | tf_op jit(solution)/shard_map/cond/branch_1_fun/ppermute | solution.py:34
  147.5 0.2 compare_reduce_fusion.1
  147.8 3.0 %collective-permute-start.18 = (f32[2,544,128]{2,1,0:T(8,128)}, f32[2,544,128]{2,1,0:T(8,128)}, u32[]{:S(2)}, u32[]{:S(2)}) collective-permute-start(f32[2,544,128]{2,1,0:T(8,128)} %pad_maximum_fusion.4), channel_id=1, source_target_pairs={{0,4},{4,0},{8,12},{12,8},{16,20},{20,16},{24,28},{28,24},{32,36},... | collective-permute-start | bytes 1671176 | tf_op jit(solution)/shard_map/cond/branch_1_fun/ppermute | solution.py:38
  150.8 2.7 %collective-permute-start.16 = (f32[2,544,128]{2,1,0:T(8,128)}, f32[2,544,128]{2,1,0:T(8,128)}, u32[]{:S(2)}, u32[]{:S(2)}) collective-permute-start(f32[2,544,128]{2,1,0:T(8,128)} %collective-permute-done.13), channel_id=1, source_target_pairs={{0,24},{4,100},{8,0},{12,108},{16,8},{20,116},{24,16},{28,124},{32... | collective-permute-start | bytes 1671176 | tf_op jit(solution)/shard_map/cond/branch_1_fun/ppermute | solution.py:34
  153.4 1.6 collective-permute-done.14
  155.0 0.3 fusion.20
  155.3 0.3 compare_reduce_fusion
  155.8 3.8 %collective-permute-start.24 = (f32[2,544,128]{2,1,0:T(8,128)}, f32[2,544,128]{2,1,0:T(8,128)}, u32[]{:S(2)}, u32[]{:S(2)}) collective-permute-start(f32[2,544,128]{2,1,0:T(8,128)} %collective-permute-done.14), channel_id=1, source_target_pairs={{0,4},{4,0},{8,12},{12,8},{16,20},{20,16},{24,28},{28,24},{32,36},... | collective-permute-start | bytes 1671176 | tf_op jit(solution)/shard_map/cond/branch_1_fun/ppermute | solution.py:38
  159.8 0.5 collective-permute-done.16
  160.2 2.5 %collective-permute-start.20 = (f32[2,544,128]{2,1,0:T(8,128)}, f32[2,544,128]{2,1,0:T(8,128)}, u32[]{:S(2)}, u32[]{:S(2)}) collective-permute-start(f32[2,544,128]{2,1,0:T(8,128)} %collective-permute-done.12), channel_id=1, source_target_pairs={{0,4},{4,0},{8,12},{12,8},{16,20},{20,16},{24,28},{28,24},{32,36},... | collective-permute-start | bytes 1671176 | tf_op jit(solution)/shard_map/cond/branch_1_fun/ppermute | solution.py:38
  162.7 2.5 %collective-permute-done.15 = f32[2,544,128]{2,1,0:T(8,128)} collective-permute-done((f32[2,544,128]{2,1,0:T(8,128)}, f32[2,544,128]{2,1,0:T(8,128)}, u32[]{:S(2)}, u32[]{:S(2)}) %collective-permute-start.15) | collective-permute-done | bytes 557088 | tf_op jit(solution)/shard_map/cond/branch_1_fun/ppermute | solution.py:34
  165.2 3.8 %collective-permute-start.22 = (f32[2,544,128]{2,1,0:T(8,128)}, f32[2,544,128]{2,1,0:T(8,128)}, u32[]{:S(2)}, u32[]{:S(2)}) collective-permute-start(f32[2,544,128]{2,1,0:T(8,128)} %collective-permute-done.15), channel_id=1, source_target_pairs={{0,4},{4,0},{8,12},{12,8},{16,20},{20,16},{24,28},{28,24},{32,36},... | collective-permute-start | bytes 1671176 | tf_op jit(solution)/shard_map/cond/branch_1_fun/ppermute | solution.py:38
  169.2 0.5 add_convert_fusion
  169.7 1.2 collective-permute-done.22
  170.9 0.4 collective-permute-start.31
  171.3 1.0 pad_maximum_fusion.7.lower1_ref
  172.3 19.2 %update.1.matrix_ref = f32[768,4096]{1,0:T(8,128)} custom-call(s32[5]{0:T(128)S(1)} %stack.55.place_ref, f32[768,4096]{1,0:T(8,128)} %source_ref.1, f32[768,1]{1,0:T(8,128)S(1)} %get-tuple-element.94.keep_ref, bf16[768,256]{1,0:T(8,128)(2,1)S(1)} %get-tuple-element.74.hit_ref, f32[768,256]{1,0:T(8,128)S(1)} %pad_maximum_fusion.6.lower0_ref, ...), custom_call_target="tpu_custom_call" | custom-call | flops 9663676416 | bytes 34603008 | tf_op jit(solution)/shard_map/update/pallas_call | solution.py:343
  191.6 2.0 copy-done
  193.6 13.3 %put_tops.1 = f32[768,4096]{1,0:T(8,128)} custom-call(s32[5]{0:T(128)S(1)} %stack.55.place_ref, f32[768,4096]{1,0:T(8,128)} %update.1.matrix_ref, f32[256,4096]{1,0:T(8,128)} %all-reduce.3.cloned.1.call-done.top_ref, f32[256,4096]{1,0:T(8,128)} %copy-done, bf16[768,512]{1,0:T(8,128)(2,1)S(1)} %get-tuple-element.93.take_ref), custom_call_target="tpu_custom_call", output_to_operand_aliasing={{}: (1, {})} | custom-call | flops 6442450944 | bytes 33554432 | tf_op jit(solution)/shard_map/put_tops/pallas_call | solution.py:224
  (65 shorter events, 1.6 us)
Async XLA Ops:
  6.5 164.4 %all-reduce.3.cloned.1.call-start = ((), (), s32[]{:S(2)}) async-start(), calls=%async_computation | async-start | bytes 8388608 | tf_op jit(solution)/shard_map/psum | solution.py:423
  15.1 39.3 %collective-permute-start.26 = (f32[4,4,512,128]{3,2,1,0:T(8,128)}, f32[4,4,512,128]{3,2,1,0:T(8,128)}, u32[]{:S(2)}, u32[]{:S(2)}) collective-permute-start(f32[4,4,512,128]{3,2,1,0:T(8,128)} %pick_rows.2), channel_id=1, source_target_pairs={{0,4},{4,0},{8,12},{12,8},{16,20},{20,16},{24,28},{28,24},{32,36},... | collective-permute-start | bytes 12582920 | tf_op jit(solution)/shard_map/ppermute | solution.py:38
  20.5 1.0 copy-start.2
  21.5 19.4 %collective-permute-start.27 = (f32[2,192,256]{2,1,0:T(8,128)S(1)}, f32[2,192,256]{2,1,0:T(8,128)S(1)}, u32[]{:S(2)}, u32[]{:S(2)}) collective-permute-start(f32[2,192,256]{2,1,0:T(8,128)S(1)} %copy-done.2), channel_id=1, source_target_pairs={{0,3},{1,0},{2,1},{3,2},{4,7},{5,4},{6,5},{7,6},{8,11},{9,8},{10,9... | collective-permute-start | bytes 1179656 | tf_op jit(solution)/shard_map/ppermute | solution.py:426
  24.1 16.9 %collective-permute-start.28 = (f32[2,192,256]{2,1,0:T(8,128)S(1)}, f32[2,192,256]{2,1,0:T(8,128)S(1)}, u32[]{:S(2)}, u32[]{:S(2)}) collective-permute-start(f32[2,192,256]{2,1,0:T(8,128)S(1)} %copy-done.2), channel_id=1, source_target_pairs={{0,2},{1,3},{2,0},{3,1},{4,6},{5,7},{6,4},{7,5},{8,10},{9,11},{10,... | collective-permute-start | bytes 1179656 | tf_op jit(solution)/shard_map/ppermute | solution.py:426
  24.6 20.5 %collective-permute-start.29 = (f32[2,192,256]{2,1,0:T(8,128)S(1)}, f32[2,192,256]{2,1,0:T(8,128)S(1)}, u32[]{:S(2)}, u32[]{:S(2)}) collective-permute-start(f32[2,192,256]{2,1,0:T(8,128)S(1)} %copy-done.2), channel_id=1, source_target_pairs={{0,1},{1,2},{2,3},{3,0},{4,5},{5,6},{6,7},{7,4},{8,9},{9,10},{10,1... | collective-permute-start | bytes 1179656 | tf_op jit(solution)/shard_map/ppermute | solution.py:426
  40.9 5.5 %copy-start.3 = (s32[2,256]{1,0:T(2,128)S(1)}, s32[2,256]{1,0:T(2,128)}, u32[]{:S(2)}) copy-start(s32[2,256]{1,0:T(2,128)} %param.9) | copy-start | bytes 6148
  45.9 8.5 %collective-permute-start.30 = (f32[768,256]{1,0:T(8,128)S(1)}, f32[768,256]{1,0:T(8,128)S(1)}, u32[]{:S(2)}, u32[]{:S(2)}) collective-permute-start(f32[768,256]{1,0:T(8,128)S(1)} %pad_maximum_fusion.6.lower0_ref), channel_id=1, source_target_pairs={{0,4},{4,0},{8,12},{12,8},{16,20},{20,16},{24,28},{28,24},{32,36},... | collective-permute-start | bytes 2359304 | tf_op jit(solution)/shard_map/ppermute | solution.py:38
  48.0 6.4 %copy-start.1 = (f32[2,256,256]{2,1,0:T(8,128)S(1)}, f32[2,256,256]{2,1,0:T(8,128)}, u32[]{:S(2)}) copy-start(f32[2,256,256]{2,1,0:T(8,128)} %inverse_ref.1) | copy-start | bytes 1572868
  59.2 11.8 %collective-permute-start.4 = (f32[2,544,128]{2,1,0:T(8,128)S(1)}, f32[2,544,128]{2,1,0:T(8,128)S(1)}, u32[]{:S(2)}, u32[]{:S(2)}) collective-permute-start(f32[2,544,128]{2,1,0:T(8,128)S(1)} %get-tuple-element.115), channel_id=1, source_target_pairs={{0,24},{4,100},{8,0},{12,108},{16,8},{20,116},{24,16},{28,124},{32... | collective-permute-start | bytes 1671176 | tf_op jit(solution)/shard_map/cond/branch_1_fun/ppermute | solution.py:34
  61.1 13.2 %collective-permute-start.1 = (f32[2,544,128]{2,1,0:T(8,128)S(1)}, f32[2,544,128]{2,1,0:T(8,128)S(1)}, u32[]{:S(2)}, u32[]{:S(2)}) collective-permute-start(f32[2,544,128]{2,1,0:T(8,128)S(1)} %get-tuple-element.114), channel_id=1, source_target_pairs={{0,8},{4,36},{8,16},{12,44},{16,24},{20,52},{24,0},{28,60},{32,40}... | collective-permute-start | bytes 1671176 | tf_op jit(solution)/shard_map/cond/branch_1_fun/ppermute | solution.py:34
  71.1 8.9 %collective-permute-start = (f32[2,544,128]{2,1,0:T(8,128)S(1)}, f32[2,544,128]{2,1,0:T(8,128)S(1)}, u32[]{:S(2)}, u32[]{:S(2)}) collective-permute-start(f32[2,544,128]{2,1,0:T(8,128)S(1)} %get-tuple-element.110), channel_id=1, source_target_pairs={{0,24},{4,100},{8,0},{12,108},{16,8},{20,116},{24,16},{28,124},{32... | collective-permute-start | bytes 1671176 | tf_op jit(solution)/shard_map/cond/branch_1_fun/ppermute | solution.py:34
  73.5 14.4 %collective-permute-start.5 = (f32[2,544,128]{2,1,0:T(8,128)S(1)}, f32[2,544,128]{2,1,0:T(8,128)S(1)}, u32[]{:S(2)}, u32[]{:S(2)}) collective-permute-start(f32[2,544,128]{2,1,0:T(8,128)S(1)} %get-tuple-element.111), channel_id=1, source_target_pairs={{0,24},{4,100},{8,0},{12,108},{16,8},{20,116},{24,16},{28,124},{32... | collective-permute-start | bytes 1671176 | tf_op jit(solution)/shard_map/cond/branch_1_fun/ppermute | solution.py:34
  74.3 13.6 %collective-permute-start.2 = (f32[2,544,128]{2,1,0:T(8,128)S(1)}, f32[2,544,128]{2,1,0:T(8,128)S(1)}, u32[]{:S(2)}, u32[]{:S(2)}) collective-permute-start(f32[2,544,128]{2,1,0:T(8,128)S(1)} %get-tuple-element.112), channel_id=1, source_target_pairs={{0,8},{4,36},{8,16},{12,44},{16,24},{20,52},{24,0},{28,60},{32,40}... | collective-permute-start | bytes 1671176 | tf_op jit(solution)/shard_map/cond/branch_1_fun/ppermute | solution.py:34
  75.2 17.8 %collective-permute-start.3 = (f32[2,544,128]{2,1,0:T(8,128)S(1)}, f32[2,544,128]{2,1,0:T(8,128)S(1)}, u32[]{:S(2)}, u32[]{:S(2)}) collective-permute-start(f32[2,544,128]{2,1,0:T(8,128)S(1)} %get-tuple-element.113), channel_id=1, source_target_pairs={{0,8},{4,36},{8,16},{12,44},{16,24},{20,52},{24,0},{28,60},{32,40}... | collective-permute-start | bytes 1671176 | tf_op jit(solution)/shard_map/cond/branch_1_fun/ppermute | solution.py:34
  93.2 8.6 %collective-permute-start.6 = (f32[544,128]{1,0:T(8,128)S(1)}, f32[544,128]{1,0:T(8,128)S(1)}, u32[]{:S(2)}, u32[]{:S(2)}) collective-permute-start(f32[544,128]{1,0:T(8,128)S(1)} %get-tuple-element.116), channel_id=1, source_target_pairs={{0,64},{4,20},{8,72},{12,28},{16,80},{20,4},{24,88},{28,12},{32,96... | collective-permute-start | bytes 835592 | tf_op jit(solution)/shard_map/cond/branch_1_fun/ppermute | solution.py:34
  97.8 8.2 %collective-permute-start.8 = (f32[544,128]{1,0:T(8,128)S(1)}, f32[544,128]{1,0:T(8,128)S(1)}, u32[]{:S(2)}, u32[]{:S(2)}) collective-permute-start(f32[544,128]{1,0:T(8,128)S(1)} %get-tuple-element.117), channel_id=1, source_target_pairs={{0,96},{4,28},{8,104},{12,4},{16,112},{20,12},{24,120},{28,20},{32... | collective-permute-start | bytes 835592 | tf_op jit(solution)/shard_map/cond/branch_1_fun/ppermute | solution.py:34
  98.3 7.7 %collective-permute-start.7 = (f32[544,128]{1,0:T(8,128)S(1)}, f32[544,128]{1,0:T(8,128)S(1)}, u32[]{:S(2)}, u32[]{:S(2)}) collective-permute-start(f32[544,128]{1,0:T(8,128)S(1)} %slice_bitcast_fusion.1), channel_id=1, source_target_pairs={{0,32},{4,12},{8,40},{12,20},{16,48},{20,28},{24,56},{28,4},{32,64... | collective-permute-start | bytes 835592 | tf_op jit(solution)/shard_map/cond/branch_1_fun/ppermute | solution.py:34
  109.1 13.1 %collective-permute-start.10 = (f32[544,128]{1,0:T(8,128)}, f32[544,128]{1,0:T(8,128)S(1)}, u32[]{:S(2)}, u32[]{:S(2)}) collective-permute-start(f32[544,128]{1,0:T(8,128)} %solve.1), channel_id=1, source_target_pairs={{0,64},{4,20},{8,72},{12,28},{16,80},{20,4},{24,88},{28,12},{32,96... | collective-permute-start | bytes 835592 | tf_op jit(solution)/shard_map/cond/branch_1_fun/ppermute | solution.py:34
  111.0 15.6 %collective-permute-start.11 = (f32[544,128]{1,0:T(8,128)}, f32[544,128]{1,0:T(8,128)S(1)}, u32[]{:S(2)}, u32[]{:S(2)}) collective-permute-start(f32[544,128]{1,0:T(8,128)} %solve.1), channel_id=1, source_target_pairs={{0,32},{4,12},{8,40},{12,20},{16,48},{20,28},{24,56},{28,4},{32,64... | collective-permute-start | bytes 835592 | tf_op jit(solution)/shard_map/cond/branch_1_fun/ppermute | solution.py:34
  111.5 31.4 %collective-permute-start.9 = (f32[544,128]{1,0:T(8,128)}, f32[544,128]{1,0:T(8,128)S(1)}, u32[]{:S(2)}, u32[]{:S(2)}) collective-permute-start(f32[544,128]{1,0:T(8,128)} %solve.1), channel_id=1, source_target_pairs={{0,96},{4,28},{8,104},{12,4},{16,112},{20,12},{24,120},{28,20},{32... | collective-permute-start | bytes 835592 | tf_op jit(solution)/shard_map/cond/branch_1_fun/ppermute | solution.py:34
  127.5 20.3 %collective-permute-start.13 = (f32[2,544,128]{2,1,0:T(8,128)}, f32[2,544,128]{2,1,0:T(8,128)}, u32[]{:S(2)}, u32[]{:S(2)}) collective-permute-start(f32[2,544,128]{2,1,0:T(8,128)} %pad_maximum_fusion.5), channel_id=1, source_target_pairs={{0,24},{4,100},{8,0},{12,108},{16,8},{20,116},{24,16},{28,124},{32... | collective-permute-start | bytes 1671176 | tf_op jit(solution)/shard_map/cond/branch_1_fun/ppermute | solution.py:34
  127.5 23.3 %collective-permute-start.17 = (f32[2,544,128]{2,1,0:T(8,128)}, f32[2,544,128]{2,1,0:T(8,128)}, u32[]{:S(2)}, u32[]{:S(2)}) collective-permute-start(f32[2,544,128]{2,1,0:T(8,128)} %pad_maximum_fusion.5), channel_id=1, source_target_pairs={{0,8},{4,36},{8,16},{12,44},{16,24},{20,52},{24,0},{28,60},{32,40}... | collective-permute-start | bytes 1671176 | tf_op jit(solution)/shard_map/cond/branch_1_fun/ppermute | solution.py:34
  128.9 24.5 %collective-permute-start.19 = (f32[2,544,128]{2,1,0:T(8,128)}, f32[2,544,128]{2,1,0:T(8,128)}, u32[]{:S(2)}, u32[]{:S(2)}) collective-permute-start(f32[2,544,128]{2,1,0:T(8,128)} %pad_maximum_fusion.5), channel_id=1, source_target_pairs={{0,4},{4,0},{8,12},{12,8},{16,20},{20,16},{24,28},{28,24},{32,36},... | collective-permute-start | bytes 1671176 | tf_op jit(solution)/shard_map/cond/branch_1_fun/ppermute | solution.py:38
  144.8 10.2 %collective-permute-start.14 = (f32[2,544,128]{2,1,0:T(8,128)}, f32[2,544,128]{2,1,0:T(8,128)}, u32[]{:S(2)}, u32[]{:S(2)}) collective-permute-start(f32[2,544,128]{2,1,0:T(8,128)} %pad_maximum_fusion.4), channel_id=1, source_target_pairs={{0,8},{4,36},{8,16},{12,44},{16,24},{20,52},{24,0},{28,60},{32,40}... | collective-permute-start | bytes 1671176 | tf_op jit(solution)/shard_map/cond/branch_1_fun/ppermute | solution.py:34
  144.8 11.0 %collective-permute-start.12 = (f32[2,544,128]{2,1,0:T(8,128)}, f32[2,544,128]{2,1,0:T(8,128)}, u32[]{:S(2)}, u32[]{:S(2)}) collective-permute-start(f32[2,544,128]{2,1,0:T(8,128)} %pad_maximum_fusion.4), channel_id=1, source_target_pairs={{0,24},{4,100},{8,0},{12,108},{16,8},{20,116},{24,16},{28,124},{32... | collective-permute-start | bytes 1671176 | tf_op jit(solution)/shard_map/cond/branch_1_fun/ppermute | solution.py:34
  147.8 11.9 %collective-permute-start.18 = (f32[2,544,128]{2,1,0:T(8,128)}, f32[2,544,128]{2,1,0:T(8,128)}, u32[]{:S(2)}, u32[]{:S(2)}) collective-permute-start(f32[2,544,128]{2,1,0:T(8,128)} %pad_maximum_fusion.4), channel_id=1, source_target_pairs={{0,4},{4,0},{8,12},{12,8},{16,20},{20,16},{24,28},{28,24},{32,36},... | collective-permute-start | bytes 1671176 | tf_op jit(solution)/shard_map/cond/branch_1_fun/ppermute | solution.py:38
  150.8 9.5 %collective-permute-start.16 = (f32[2,544,128]{2,1,0:T(8,128)}, f32[2,544,128]{2,1,0:T(8,128)}, u32[]{:S(2)}, u32[]{:S(2)}) collective-permute-start(f32[2,544,128]{2,1,0:T(8,128)} %collective-permute-done.13), channel_id=1, source_target_pairs={{0,24},{4,100},{8,0},{12,108},{16,8},{20,116},{24,16},{28,124},{32... | collective-permute-start | bytes 1671176 | tf_op jit(solution)/shard_map/cond/branch_1_fun/ppermute | solution.py:34
  153.4 9.3 %collective-permute-start.21 = (f32[2,544,128]{2,1,0:T(8,128)}, f32[2,544,128]{2,1,0:T(8,128)}, u32[]{:S(2)}, u32[]{:S(2)}) collective-permute-start(f32[2,544,128]{2,1,0:T(8,128)} %collective-permute-done.13), channel_id=1, source_target_pairs={{0,4},{4,0},{8,12},{12,8},{16,20},{20,16},{24,28},{28,24},{32,36},... | collective-permute-start | bytes 1671176 | tf_op jit(solution)/shard_map/cond/branch_1_fun/ppermute | solution.py:38
  155.0 10.2 %collective-permute-start.15 = (f32[2,544,128]{2,1,0:T(8,128)}, f32[2,544,128]{2,1,0:T(8,128)}, u32[]{:S(2)}, u32[]{:S(2)}) collective-permute-start(f32[2,544,128]{2,1,0:T(8,128)} %collective-permute-done.14), channel_id=1, source_target_pairs={{0,8},{4,36},{8,16},{12,44},{16,24},{20,52},{24,0},{28,60},{32,40}... | collective-permute-start | bytes 1671176 | tf_op jit(solution)/shard_map/cond/branch_1_fun/ppermute | solution.py:34
  155.8 13.9 %collective-permute-start.24 = (f32[2,544,128]{2,1,0:T(8,128)}, f32[2,544,128]{2,1,0:T(8,128)}, u32[]{:S(2)}, u32[]{:S(2)}) collective-permute-start(f32[2,544,128]{2,1,0:T(8,128)} %collective-permute-done.14), channel_id=1, source_target_pairs={{0,4},{4,0},{8,12},{12,8},{16,20},{20,16},{24,28},{28,24},{32,36},... | collective-permute-start | bytes 1671176 | tf_op jit(solution)/shard_map/cond/branch_1_fun/ppermute | solution.py:38
  159.7 10.0 %collective-permute-start.25 = (f32[2,544,128]{2,1,0:T(8,128)}, f32[2,544,128]{2,1,0:T(8,128)}, u32[]{:S(2)}, u32[]{:S(2)}) collective-permute-start(f32[2,544,128]{2,1,0:T(8,128)} %collective-permute-done.17), channel_id=1, source_target_pairs={{0,4},{4,0},{8,12},{12,8},{16,20},{20,16},{24,28},{28,24},{32,36},... | collective-permute-start | bytes 1671176 | tf_op jit(solution)/shard_map/cond/branch_1_fun/ppermute | solution.py:38
  160.2 9.5 %collective-permute-start.20 = (f32[2,544,128]{2,1,0:T(8,128)}, f32[2,544,128]{2,1,0:T(8,128)}, u32[]{:S(2)}, u32[]{:S(2)}) collective-permute-start(f32[2,544,128]{2,1,0:T(8,128)} %collective-permute-done.12), channel_id=1, source_target_pairs={{0,4},{4,0},{8,12},{12,8},{16,20},{20,16},{24,28},{28,24},{32,36},... | collective-permute-start | bytes 1671176 | tf_op jit(solution)/shard_map/cond/branch_1_fun/ppermute | solution.py:38
  162.7 7.0 %collective-permute-start.23 = (f32[2,544,128]{2,1,0:T(8,128)}, f32[2,544,128]{2,1,0:T(8,128)}, u32[]{:S(2)}, u32[]{:S(2)}) collective-permute-start(f32[2,544,128]{2,1,0:T(8,128)} %collective-permute-done.16), channel_id=1, source_target_pairs={{0,4},{4,0},{8,12},{12,8},{16,20},{20,16},{24,28},{28,24},{32,36},... | collective-permute-start | bytes 1671176 | tf_op jit(solution)/shard_map/cond/branch_1_fun/ppermute | solution.py:38
  165.2 5.7 %collective-permute-start.22 = (f32[2,544,128]{2,1,0:T(8,128)}, f32[2,544,128]{2,1,0:T(8,128)}, u32[]{:S(2)}, u32[]{:S(2)}) collective-permute-start(f32[2,544,128]{2,1,0:T(8,128)} %collective-permute-done.15), channel_id=1, source_target_pairs={{0,4},{4,0},{8,12},{12,8},{16,20},{20,16},{24,28},{28,24},{32,36},... | collective-permute-start | bytes 1671176 | tf_op jit(solution)/shard_map/cond/branch_1_fun/ppermute | solution.py:38
  170.9 20.6 %collective-permute-start.31 = (f32[256,4096]{1,0:T(8,128)}, f32[256,4096]{1,0:T(8,128)S(1)}, u32[]{:S(2)}, u32[]{:S(2)}) collective-permute-start(f32[256,4096]{1,0:T(8,128)} %all-reduce.3.cloned.1.call-done.top_ref), channel_id=1, source_target_pairs={{0,4},{4,0},{8,12},{12,8},{16,20},{20,16},{24,28},{28,24},{32,36},... | collective-permute-start | bytes 12582920 | tf_op jit(solution)/shard_map/ppermute | solution.py:38
  191.5 2.0 copy-start
Sparse Core Ops, SparseCore 0:
  20.7 116.4 all-reduce.2

commit v5 on v3

--- a/solution.py
+++ b/solution.py
@@ -240,16 +240,20 @@
     out_ref, left_ref, held_ref, flat_ref, blocks_ref, piece_sems, in_sems, out_sems = refs[16:]
     core, rank = place_ref[0], place_ref[3]
     width = 2 * LANES
-    copies = [
-        pltpu.make_async_copy(
-            pieces[side * 8 + slot],
-            held_ref.at[side, slot // 2, pl.ds(slot % 2 * 2, 2)],
-            piece_sems.at[side * 8 + slot],
-        )
-        for side in range(2)
-        for slot in range(8)
-    ]
-    for copy in copies:
+
+    def copies_of(first, count, part):
+        return [
+            pltpu.make_async_copy(
+                pieces[side * 8 + slot].at[:, pl.ds(first, count)],
+                held_ref.at[side, slot // 2, pl.ds(slot % 2 * 2, 2), pl.ds(first, count)],
+                piece_sems.at[part, side * 8 + slot],
+            )
+            for side in range(2)
+            for slot in range(8)
+        ]
+
+    extras, copies = copies_of(2 * NB, EXTRA, 0), copies_of(0, 2 * NB, 1)
+    for copy in extras + copies:
         copy.start()
 
     def lanes(step):
@@ -270,7 +274,7 @@
     def _(step):
         fetch(step).start()
 
-    for copy in copies:
+    for copy in extras:
         copy.wait()
     for side in range(2):
         for turn in range(4):
@@ -293,6 +297,8 @@
     high, low = split_two(-jnp.concatenate([lower0, lower1], axis=1))
     for i, part in enumerate((high, high, low)):
         left_ref[:, i * 2 * NB : (i + 1) * 2 * NB] = part
+    for copy in copies:
+        copy.wait()
 
     @pl.loop(0, 16)
     def _(step):
@@ -330,7 +336,7 @@
             pltpu.VMEM((2, 4, 4, SHARE, LANES), F32),
             pltpu.VMEM((4 * NB, LANES), F32),
             pltpu.VMEM((16, rows, 2 * LANES), F32),
-            pltpu.SemaphoreType.DMA((16,)),
+            pltpu.SemaphoreType.DMA((2, 16)),
             pltpu.SemaphoreType.DMA((16,)),
             pltpu.SemaphoreType.DMA((16,)),
         ],
@@ -368,14 +374,25 @@
 
         @pl.when(rank == panel)
         def _(panel=panel):
-            load = pltpu.make_async_copy(matrix_ref.at[pl.ds(0, NB)], held_ref, sems.at[0])
-            load.start()
-            load.wait()
-            store = pltpu.make_async_copy(
-                held_ref, out_ref.at[pl.ds(panel * NB, NB)], sems.at[1]
-            )
-            store.start()
-            store.wait()
+            part = NB // 4
+            chunks = [pl.ds(i * part, part) for i in range(4)]
+            loads = [
+                pltpu.make_async_copy(matrix_ref.at[rows], held_ref.at[rows], sems.at[0, i])
+                for i, rows in enumerate(chunks)
+            ]
+            stores = [
+                pltpu.make_async_copy(
+                    held_ref.at[rows], out_ref.at[pl.ds(panel * NB + i * part, part)], sems.at[1, i]
+                )
+                for i, rows in enumerate(chunks)
+            ]
+            for load in loads:
+                load.start()
+            for load, store in zip(loads, stores):
+                load.wait()
+                store.start()
+            for store in stores:
+                store.wait()
 
     for panel in range(2):
 
@@ -396,7 +413,7 @@
         scratch_shapes=[
             pltpu.VMEM((NB, columns // 4), F32),
             pltpu.VMEM((NB, columns), F32),
-            pltpu.SemaphoreType.DMA((2,)),
+            pltpu.SemaphoreType.DMA((2, 4)),
             pltpu.SemaphoreType.DMA((2, 4)),
         ],
         compiler_params=pltpu.CompilerParams(vmem_limit_bytes=VMEM_LIMIT),
@@ -456,13 +473,11 @@
         part = [jnp.concatenate([kept[d] + other[d], extra[d]], axis=1) for d in range(4)]
         ahead = send(part[2][:2], one=1)
         behind = send(part[2][2:], one=3)
-        part[1] = jnp.concatenate([part[1][:2] + ahead, part[1][2:]])
-        part[3] = jnp.concatenate([part[3][:2], part[3][2:] + behind])
-        part = part[0] + send(part[1], one=1) + send(part[3], one=3)
-
-        raw = part[0]
-        for d in (2, 1, 3):
-            raw = raw + send(part[d], two=d)
+        high = part[0][2:] + send(part[1][2:], one=1)
+        low = part[0][:2] + send(part[3][:2], one=3)
+        low = low + send(part[1][:2] + ahead, one=1)
+        high = high + send(part[3][2:] + behind, one=3)
+        raw = low[0] + send(high[0], two=2) + send(low[1], two=1) + send(high[1], two=3)
 
         return solve(raw, inverses)
 

time: 195 us -> 194 us (level)
  waiting for transfers between devices: 60.1 us -> 52.2 us
  starting transfers between devices: 45.6 us -> 52.6 us
  Pallas kernels: 58.9 us -> 56.8 us
    ppermute x16 -> x18, waiting for transfers between devices: 59.3 us -> 50.5 us  [send(): return lax.ppermute(value, 'prow', pairs)]
    ppermute x16 -> x18, starting transfers between devices: 22.1 us -> 26.2 us  [send(): return lax.ppermute(value, 'prow', pairs)]
    ppermute x10, starting transfers between devices: 17.7 us -> 20.7 us  [swap_cores(): return lax.ppermute(value, 'prow', [(rank, rank ^ 1) for rank in range(32)])]
  transfers between devices with their start and end apart: 31 -> 33, of which waited for: 9 -> 12; matrix products, arithmetic and copies ran while one was open for 6% -> 6% of each run, Pallas kernels for 24% -> 23%
where the time goes in v5:
time: 194 us; the launch traced here: 192 us
  Pallas kernels  56.8 us (29%)
  starting transfers between devices  52.6 us (27%)
  waiting for transfers between devices  52.2 us (27%)
  between operations  15.9 us (8%)
  other arithmetic  8.29 us (4%)
  local copies, waits for them, and re-layouts  5.62 us (3%)
    ppermute x18, waiting for transfers between devices, send(): return lax.ppermute(value, 'prow', pairs)  50.5 us
    ppermute x18, starting transfers between devices, send(): return lax.ppermute(value, 'prow', pairs)  26.2 us
    ppermute x10, starting transfers between devices, swap_cores(): return lax.ppermute(value, 'prow', [(rank, rank ^ 1) for rank in range(32)])  20.7 us
    pallas_call x1, Pallas kernels, update(): pl.pallas_call(update_kernel, out_shape=jax.ShapeDtypeStruct(source.shape...  20 us
    pallas_call x2, Pallas kernels, pick_rows(): pl.pallas_call(pick_kernel, out_shape=jax.ShapeDtypeStruct(shape, F32), i...  14.2 us
    pallas_call x1, Pallas kernels, put_tops(): pl.pallas_call(tops_kernel, out_shape=jax.ShapeDtypeStruct(matrix.shape,...  12.6 us
    pallas_call x1, Pallas kernels, own_tops(): pl.pallas_call(own_tops_kernel, out_shape=jax.ShapeDtypeStruct((2 * NB, c...  5.79 us
    ppermute x3, starting transfers between devices, body(): lax.ppermute(lower_own, 'pcol', [(i, (i - d) % 4) for i in range(4)])  5.71 us
  transfers between devices with their start and end apart: 33, of which 12 were waited for; matrix products, arithmetic and copies ran while one was open for 6% of the time, Pallas kernels for 23%

profile of v5, /device:TPU:1, one launch (start us, length us, event | category | flops | bytes accessed | tf_op | source)
XLA Modules:
  0.0 192.0 jit_solution(3610024237386135901)
XLA Ops:
  7.4 0.7 all-gather.2.cloned.1.call-update
  8.1 0.9 slice_bitcast_fusion.8
  9.1 2.1 %collective-permute-start.13 = (f32[192,256]{1,0:T(8,128)S(1)}, f32[192,256]{1,0:T(8,128)S(1)}, u32[]{:S(2)}, u32[]{:S(2)}) collective-permute-start(f32[192,256]{1,0:T(8,128)S(1)} %slice_bitcast_fusion.8), channel_id=1, source_target_pairs={{0,1},{1,2},{2,3},{3,0},{4,5},{5,6},{6,7},{7,4},{8,9},{9,10},{10,1... | collective-permute-start | bytes 589832 | tf_op jit(solution)/shard_map/ppermute | solution.py:440
  11.2 2.5 %collective-permute-start.12 = (f32[192,256]{1,0:T(8,128)S(1)}, f32[192,256]{1,0:T(8,128)S(1)}, u32[]{:S(2)}, u32[]{:S(2)}) collective-permute-start(f32[192,256]{1,0:T(8,128)S(1)} %slice_bitcast_fusion.8), channel_id=1, source_target_pairs={{0,2},{1,3},{2,0},{3,1},{4,6},{5,7},{6,4},{7,5},{8,10},{9,11},{10,... | collective-permute-start | bytes 589832 | tf_op jit(solution)/shard_map/ppermute | solution.py:440
  13.6 1.2 collective-permute-start.11
  14.9 5.8 %own_tops.1 = f32[512,4096]{1,0:T(8,128)} custom-call(s32[4]{0:T(128)S(1)} %add_add_fusion.place_ref, f32[768,4096]{1,0:T(8,128)} %matrix_ref.1), custom_call_target="tpu_custom_call" | custom-call | bytes 8388608 | tf_op jit(solution)/shard_map/own_tops/pallas_call | solution.py:408
  20.7 0.6 copy-done.15
  21.4 0.5 slice.90
  22.1 0.2 fusion.28
  23.2 0.7 broadcast_in_dim.58
  24.0 73.5 %while.11 = (s32[]{:T(128)}, f32[544,128]{1,0:T(8,128)}, s32[]{:T(128)}, s32[4]{0:T(128)S(1)}, s32[4]{0:T(128)S(1)}, /*index=5*/f32[768,4096]{1,0:T(8,128)}, f32...) while((s32[]{:T(128)}, f32[544,128]{1,0:T(8,128)}, ...), condition=%wide.region_3.4_spmd.clone, body=%wide.region_2.3_spmd.clone.sunk | while | flops 7857500160 | bytes 111991440 | solution.py:485
  24.0 0.2 fusion.57.select_ref
  24.2 7.0 %pick_rows.2 = f32[4,4,512,128]{3,2,1,0:T(8,128)} custom-call(s32[4]{0:T(128)S(1)} %get-tuple-element.231.place_ref, f32[768,4096]{1,0:T(8,128)} %get-tuple-element.281.matrix_ref, bf16[512,768]{1,0:T(8,128)(2,1)S(1)} %fusion.57.select_ref), custom_call_target="tpu_custom_call" | custom-call | flops 3221225472 | bytes 10485760 | tf_op jit(solution)/shard_map/while/body/pick_rows/pallas_call | solution.py:96
  31.2 1.9 %collective-permute-start = (f32[4,4,512,128]{3,2,1,0:T(8,128)}, f32[4,4,512,128]{3,2,1,0:T(8,128)}, u32[]{:S(2)}, u32[]{:S(2)}) collective-permute-start(f32[4,4,512,128]{3,2,1,0:T(8,128)} %pick_rows.2), channel_id=1, source_target_pairs={{0,4},{4,0},{8,12},{12,8},{16,20},{20,16},{24,28},{28,24},{32,36},... | collective-permute-start | bytes 12582920 | tf_op jit(solution)/shard_map/while/body/ppermute | solution.py:38
  33.3 0.3 fusion.59.select_ref
  33.6 7.2 %pick_rows.3 = f32[4,4,512,128]{3,2,1,0:T(8,128)} custom-call(s32[4]{0:T(128)S(1)} %get-tuple-element.233.place_ref, f32[768,4096]{1,0:T(8,128)} %get-tuple-element.281.matrix_ref, bf16[512,768]{1,0:T(8,128)(2,1)S(1)} %fusion.57.select_ref), custom_call_target="tpu_custom_call" | custom-call | flops 3221225472 | bytes 10485760 | tf_op jit(solution)/shard_map/while/body/pick_rows/pallas_call | solution.py:96
  40.8 0.9 collective-permute-done.1.other_ref
  41.7 2.0 %pick_extra.1 = f32[4,4,32,128]{3,2,1,0:T(8,128)S(1)} custom-call(s32[4]{0:T(128)S(1)} %get-tuple-element.279.place_ref, bf16[2,512,768]{2,1,0:T(8,128)(2,1)S(1)} %fusion.59.select_ref, f32[768,256]{1,0:T(8,128)S(1)} %get-tuple-element.282.own_ref, f32[768,256]{1,0:T(8,128)S(1)} %collective-permute-done.1.other_ref), custom_call_target="tpu_custom_call" | custom-call | flops 1207959552 | bytes 4194304 | tf_op jit(solution)/shard_map/while/body/pick_extra/pallas_call | solution.py:138
  43.8 2.7 %fusion.58 = (f32[4,512,128]{2,1,0:T(8,128)S(1)}, f32[4,512,128]{2,1,0:T(8,128)S(1)}, f32[4,512,128]{2,1,0:T(8,128)S(1)}, f32[4,512,128]{2,1,0:T(8,128)S(1)}) fusion(f32[4,4,512,128]{3,2,1,0:T(8,128)} %collective-permute-done, f32[4,4,512,128]{3,2,1,0:T(8,128)S(1)} %copy-done), kind=kLoop, calls=%fused_computation.21.clone.1 | loop fusion | flops 1048576 | bytes 12582912 | tf_op jit(solution)/shard_map/while/body/add | solution.py:473
  46.7 2.7 %collective-permute-start.4 = (f32[2,544,128]{2,1,0:T(8,128)S(1)}, f32[2,544,128]{2,1,0:T(8,128)S(1)}, u32[]{:S(2)}, u32[]{:S(2)}) collective-permute-start(f32[2,544,128]{2,1,0:T(8,128)S(1)} %get-tuple-element.242), channel_id=1, source_target_pairs={{0,24},{4,100},{8,0},{12,108},{16,8},{20,116},{24,16},{28,124},{32... | collective-permute-start | bytes 1671176 | tf_op jit(solution)/shard_map/while/body/ppermute | solution.py:34
  49.3 12.7 %collective-permute-done.2 = f32[2,544,128]{2,1,0:T(8,128)S(1)} collective-permute-done((f32[2,544,128]{2,1,0:T(8,128)S(1)}, f32[2,544,128]{2,1,0:T(8,128)S(1)}, u32[]{:S(2)}, u32[]{:S(2)}) %collective-permute-start.2) | collective-permute-done | bytes 557088 | tf_op jit(solution)/shard_map/while/body/ppermute | solution.py:34
  62.5 2.6 %collective-permute-start.5 = (f32[2,544,128]{2,1,0:T(8,128)S(1)}, f32[2,544,128]{2,1,0:T(8,128)S(1)}, u32[]{:S(2)}, u32[]{:S(2)}) collective-permute-start(f32[2,544,128]{2,1,0:T(8,128)S(1)} %get-tuple-element.243), channel_id=1, source_target_pairs={{0,24},{4,100},{8,0},{12,108},{16,8},{20,116},{24,16},{28,124},{32... | collective-permute-start | bytes 1671176 | tf_op jit(solution)/shard_map/while/body/ppermute | solution.py:34
  65.2 1.4 collective-permute-start.6
  66.6 5.6 %collective-permute-done.3 = f32[2,544,128]{2,1,0:T(8,128)S(1)} collective-permute-done((f32[2,544,128]{2,1,0:T(8,128)S(1)}, f32[2,544,128]{2,1,0:T(8,128)S(1)}, u32[]{:S(2)}, u32[]{:S(2)}) %collective-permute-start.3) | collective-permute-done | bytes 557088 | tf_op jit(solution)/shard_map/while/body/ppermute | solution.py:34
  72.1 7.4 %collective-permute-done.7 = f32[2,544,128]{2,1,0:T(8,128)S(1)} collective-permute-done((f32[2,544,128]{2,1,0:T(8,128)S(1)}, f32[2,544,128]{2,1,0:T(8,128)S(1)}, u32[]{:S(2)}, u32[]{:S(2)}) %collective-permute-start.7) | collective-permute-done | bytes 557088 | tf_op jit(solution)/shard_map/while/body/ppermute | solution.py:34
  79.5 0.5 collective-permute-done.6
  80.2 0.7 slice_bitcast_fusion.14
  80.9 1.6 collective-permute-start.9
  82.5 1.8 collective-permute-start.8
  84.4 1.2 collective-permute-start.10
  85.6 3.6 %collective-permute-done.9 = f32[544,128]{1,0:T(8,128)S(1)} collective-permute-done((f32[544,128]{1,0:T(8,128)}, f32[544,128]{1,0:T(8,128)S(1)}, u32[]{:S(2)}, u32[]{:S(2)}) %collective-permute-start.9) | collective-permute-done | bytes 278560 | tf_op jit(solution)/shard_map/while/body/ppermute | solution.py:34
  89.2 1.9 collective-permute-done.8
  91.0 2.4 %collective-permute-done.10 = f32[544,128]{1,0:T(8,128)} collective-permute-done((f32[544,128]{1,0:T(8,128)S(1)}, f32[544,128]{1,0:T(8,128)}, u32[]{:S(2)}, u32[]{:S(2)}) %collective-permute-start.10) | collective-permute-done | bytes 278560 | tf_op jit(solution)/shard_map/while/body/ppermute | solution.py:34
  93.4 1.7 fusion.64.raw_ref
  95.2 2.3 %solve.1 = f32[544,128]{1,0:T(8,128)} custom-call(f32[544,128]{1,0:T(8,128)} %fusion.64.raw_ref, f32[2,256,256]{2,1,0:T(8,128)S(1)} %get-tuple-element.283.inverse_ref), custom_call_target="tpu_custom_call" | custom-call | flops 201326592 | bytes 1048576 | tf_op jit(solution)/shard_map/while/body/solve/pallas_call | solution.py:159
  97.4 1.0 collective-permute-start.16
  98.4 0.5 collective-permute-start.15
  98.9 0.7 collective-permute-start.14
  99.6 5.7 %collective-permute-done.16 = f32[544,128]{1,0:T(8,128)S(1)} collective-permute-done((f32[544,128]{1,0:T(8,128)}, f32[544,128]{1,0:T(8,128)S(1)}, u32[]{:S(2)}, u32[]{:S(2)}) %collective-permute-start.16) | collective-permute-done | bytes 278560 | tf_op jit(solution)/shard_map/ppermute | solution.py:34
  105.3 1.0 pad_maximum_fusion.6.refs_0_
  106.3 4.0 %collective-permute-start.23 = (f32[2,544,128]{2,1,0:T(8,128)S(1)}, f32[2,544,128]{2,1,0:T(8,128)S(1)}, u32[]{:S(2)}, u32[]{:S(2)}) collective-permute-start(f32[2,544,128]{2,1,0:T(8,128)S(1)} %pad_maximum_fusion.6.refs_0_), channel_id=1, source_target_pairs={{0,4},{4,0},{8,12},{12,8},{16,20},{20,16},{24,28},{28,24},{32,36},... | collective-permute-start | bytes 1671176 | tf_op jit(solution)/shard_map/ppermute | solution.py:38
  110.3 1.6 collective-permute-start.19
  111.9 1.0 collective-permute-start.17
  113.0 1.9 collective-permute-start.24
  114.9 3.3 %collective-permute-start.18 = (f32[2,544,128]{2,1,0:T(8,128)S(1)}, f32[2,544,128]{2,1,0:T(8,128)S(1)}, u32[]{:S(2)}, u32[]{:S(2)}) collective-permute-start(f32[2,544,128]{2,1,0:T(8,128)S(1)} %pad_maximum_fusion.5.refs_1_), channel_id=1, source_target_pairs={{0,24},{4,100},{8,0},{12,108},{16,8},{20,116},{24,16},{28,124},{32... | collective-permute-start | bytes 1671176 | tf_op jit(solution)/shard_map/ppermute | solution.py:34
  118.1 0.2 compare_reduce_fusion.1
  118.5 1.7 collective-permute-done.19.refs_6_
  120.2 1.6 collective-permute-start.29
  121.8 3.1 %collective-permute-start.20 = (f32[2,544,128]{2,1,0:T(8,128)S(1)}, f32[2,544,128]{2,1,0:T(8,128)S(1)}, u32[]{:S(2)}, u32[]{:S(2)}) collective-permute-start(f32[2,544,128]{2,1,0:T(8,128)S(1)} %collective-permute-done.19.refs_6_), channel_id=1, source_target_pairs={{0,8},{4,36},{8,16},{12,44},{16,24},{20,52},{24,0},{28,60},{32,40}... | collective-permute-start | bytes 1671176 | tf_op jit(solution)/shard_map/ppermute | solution.py:34
  124.9 2.8 %collective-permute-done.18.refs_3_ = f32[2,544,128]{2,1,0:T(8,128)S(1)} collective-permute-done((f32[2,544,128]{2,1,0:T(8,128)S(1)}, f32[2,544,128]{2,1,0:T(8,128)S(1)}, u32[]{:S(2)}, u32[]{:S(2)}) %collective-permute-start.18) | collective-permute-done | bytes 557088 | tf_op jit(solution)/shard_map/ppermute | solution.py:34
  127.7 3.2 %collective-permute-start.21 = (f32[2,544,128]{2,1,0:T(8,128)S(1)}, f32[2,544,128]{2,1,0:T(8,128)S(1)}, u32[]{:S(2)}, u32[]{:S(2)}) collective-permute-start(f32[2,544,128]{2,1,0:T(8,128)S(1)} %collective-permute-done.18.refs_3_), channel_id=1, source_target_pairs={{0,24},{4,100},{8,0},{12,108},{16,8},{20,116},{24,16},{28,124},{32... | collective-permute-start | bytes 1671176 | tf_op jit(solution)/shard_map/ppermute | solution.py:34
  130.9 0.2 iota_compare_fusion.2
  131.1 0.2 fusion.23
  131.5 4.2 %collective-permute-start.26 = (f32[2,544,128]{2,1,0:T(8,128)S(1)}, f32[2,544,128]{2,1,0:T(8,128)S(1)}, u32[]{:S(2)}, u32[]{:S(2)}) collective-permute-start(f32[2,544,128]{2,1,0:T(8,128)S(1)} %collective-permute-done.18.refs_3_), channel_id=1, source_target_pairs={{0,4},{4,0},{8,12},{12,8},{16,20},{20,16},{24,28},{28,24},{32,36},... | collective-permute-start | bytes 1671176 | tf_op jit(solution)/shard_map/ppermute | solution.py:38
  135.8 0.4 collective-permute-start.30
  136.2 6.4 %collective-permute-done.20.refs_4_ = f32[2,544,128]{2,1,0:T(8,128)S(1)} collective-permute-done((f32[2,544,128]{2,1,0:T(8,128)S(1)}, f32[2,544,128]{2,1,0:T(8,128)S(1)}, u32[]{:S(2)}, u32[]{:S(2)}) %collective-permute-start.20) | collective-permute-done | bytes 557088 | tf_op jit(solution)/shard_map/ppermute | solution.py:34
  142.6 1.5 collective-permute-start.27
  144.1 5.1 %collective-permute-start.28 = (f32[2,544,128]{2,1,0:T(8,128)S(1)}, f32[2,544,128]{2,1,0:T(8,128)}, u32[]{:S(2)}, u32[]{:S(2)}) collective-permute-start(f32[2,544,128]{2,1,0:T(8,128)S(1)} %collective-permute-done.21.refs_5_), channel_id=1, source_target_pairs={{0,4},{4,0},{8,12},{12,8},{16,20},{20,16},{24,28},{28,24},{32,36},... | collective-permute-start | bytes 1671176 | tf_op jit(solution)/shard_map/ppermute | solution.py:38
  149.4 0.5 add_convert_fusion.take_ref
  150.0 0.7 copy-done.12
  150.7 0.3 copy-done.13
  151.1 0.8 copy-done.14
  152.0 20.0 %update.1.matrix_ref = f32[768,4096]{1,0:T(8,128)} custom-call(s32[4]{0:T(128)S(1)} %get-tuple-element.356, f32[768,4096]{1,0:T(8,128)} %get-tuple-element.297, f32[768,1]{1,0:T(8,128)S(1)} %fusion.27.keep_ref, bf16[768,256]{1,0:T(8,128)(2,1)S(1)} %get-tuple-element.146.hit_ref, f32[2,768,256]{2,1,0:T(8,128)} %all-gather.2.cloned.1.call-done.lower_ref, ...), custom_call_target="tpu_custom_call" | custom-call | flops 9663676416 | bytes 34603008 | tf_op jit(solution)/shard_map/update/pallas_call | solution.py:329
  172.0 12.6 %put_tops.1 = f32[768,4096]{1,0:T(8,128)} custom-call(f32[768,4096]{1,0:T(8,128)} %update.1.matrix_ref, f32[512,4096]{1,0:T(8,128)} %all-reduce.3.cloned.1.call-done.top_ref, bf16[768,512]{1,0:T(8,128)(2,1)S(1)} %add_convert_fusion.take_ref), custom_call_target="tpu_custom_call", output_to_operand_aliasing={{}: (0, {})} | custom-call | flops 6442450944 | bytes 33554432 | tf_op jit(solution)/shard_map/put_tops/pallas_call | solution.py:217
  (86 shorter events, 2.6 us)
Async XLA Ops:
  7.4 144.6 %all-gather.2.cloned.1.call-start = ((), (), s32[]{:S(2)}) async-start(), calls=%async_computation | async-start | bytes 1966080 | tf_op jit(solution)/shard_map/all_gather | solution.py:438
  8.1 163.9 %all-reduce.3.cloned.1.call-start = ((), (), s32[]{:S(2)}) async-start(), calls=%async_computation.1 | async-start | bytes 16777216 | tf_op jit(solution)/shard_map/psum | solution.py:436
  9.1 14.1 %collective-permute-start.13 = (f32[192,256]{1,0:T(8,128)S(1)}, f32[192,256]{1,0:T(8,128)S(1)}, u32[]{:S(2)}, u32[]{:S(2)}) collective-permute-start(f32[192,256]{1,0:T(8,128)S(1)} %slice_bitcast_fusion.8), channel_id=1, source_target_pairs={{0,1},{1,2},{2,3},{3,0},{4,5},{5,6},{6,7},{7,4},{8,9},{9,10},{10,1... | collective-permute-start | bytes 589832 | tf_op jit(solution)/shard_map/ppermute | solution.py:440
  11.2 12.0 %collective-permute-start.12 = (f32[192,256]{1,0:T(8,128)S(1)}, f32[192,256]{1,0:T(8,128)S(1)}, u32[]{:S(2)}, u32[]{:S(2)}) collective-permute-start(f32[192,256]{1,0:T(8,128)S(1)} %slice_bitcast_fusion.8), channel_id=1, source_target_pairs={{0,2},{1,3},{2,0},{3,1},{4,6},{5,7},{6,4},{7,5},{8,10},{9,11},{10,... | collective-permute-start | bytes 589832 | tf_op jit(solution)/shard_map/ppermute | solution.py:440
  13.6 9.5 %collective-permute-start.11 = (f32[192,256]{1,0:T(8,128)S(1)}, f32[192,256]{1,0:T(8,128)S(1)}, u32[]{:S(2)}, u32[]{:S(2)}) collective-permute-start(f32[192,256]{1,0:T(8,128)S(1)} %slice_bitcast_fusion.8), channel_id=1, source_target_pairs={{0,3},{1,0},{2,1},{3,2},{4,7},{5,4},{6,5},{7,6},{8,11},{9,8},{10,9... | collective-permute-start | bytes 589832 | tf_op jit(solution)/shard_map/ppermute | solution.py:440
  20.7 0.7 copy-start.15
  20.7 3.3 %copy-start.1 = (f32[2,256,256]{2,1,0:T(8,128)S(1)}, f32[2,256,256]{2,1,0:T(8,128)}, u32[]{:S(2)}) copy-start(f32[2,256,256]{2,1,0:T(8,128)} %inverse_ref.1) | copy-start | bytes 1572868
  31.2 12.5 %collective-permute-start = (f32[4,4,512,128]{3,2,1,0:T(8,128)}, f32[4,4,512,128]{3,2,1,0:T(8,128)}, u32[]{:S(2)}, u32[]{:S(2)}) collective-permute-start(f32[4,4,512,128]{3,2,1,0:T(8,128)} %pick_rows.2), channel_id=1, source_target_pairs={{0,4},{4,0},{8,12},{12,8},{16,20},{20,16},{24,28},{28,24},{32,36},... | collective-permute-start | bytes 12582920 | tf_op jit(solution)/shard_map/while/body/ppermute | solution.py:38
  33.2 8.5 %collective-permute-start.1 = (f32[768,256]{1,0:T(8,128)S(1)}, f32[768,256]{1,0:T(8,128)S(1)}, u32[]{:S(2)}, u32[]{:S(2)}) collective-permute-start(f32[768,256]{1,0:T(8,128)S(1)} %broadcast_select_fusion.2), channel_id=1, source_target_pairs={{0,4},{4,0},{8,12},{12,8},{16,20},{20,16},{24,28},{28,24},{32,36},... | collective-permute-start | bytes 2359304 | tf_op jit(solution)/shard_map/while/body/ppermute | solution.py:38
  40.8 2.9 %copy-start = (f32[4,4,512,128]{3,2,1,0:T(8,128)S(1)}, f32[4,4,512,128]{3,2,1,0:T(8,128)}, u32[]{:S(2)}) copy-start(f32[4,4,512,128]{3,2,1,0:T(8,128)} %pick_rows.3) | copy-start | bytes 12582916 | tf_op jit(solution)/shard_map/while
  46.6 15.4 %collective-permute-start.2 = (f32[2,544,128]{2,1,0:T(8,128)S(1)}, f32[2,544,128]{2,1,0:T(8,128)S(1)}, u32[]{:S(2)}, u32[]{:S(2)}) collective-permute-start(f32[2,544,128]{2,1,0:T(8,128)S(1)} %get-tuple-element.236), channel_id=1, source_target_pairs={{0,8},{4,36},{8,16},{12,44},{16,24},{20,52},{24,0},{28,60},{32,40}... | collective-permute-start | bytes 1671176 | tf_op jit(solution)/shard_map/while/body/ppermute | solution.py:34
  46.7 15.8 %collective-permute-start.4 = (f32[2,544,128]{2,1,0:T(8,128)S(1)}, f32[2,544,128]{2,1,0:T(8,128)S(1)}, u32[]{:S(2)}, u32[]{:S(2)}) collective-permute-start(f32[2,544,128]{2,1,0:T(8,128)S(1)} %get-tuple-element.242), channel_id=1, source_target_pairs={{0,24},{4,100},{8,0},{12,108},{16,8},{20,116},{24,16},{28,124},{32... | collective-permute-start | bytes 1671176 | tf_op jit(solution)/shard_map/while/body/ppermute | solution.py:34
  62.2 10.0 %collective-permute-start.3 = (f32[2,544,128]{2,1,0:T(8,128)S(1)}, f32[2,544,128]{2,1,0:T(8,128)S(1)}, u32[]{:S(2)}, u32[]{:S(2)}) collective-permute-start(f32[2,544,128]{2,1,0:T(8,128)S(1)} %get-tuple-element.239), channel_id=1, source_target_pairs={{0,8},{4,36},{8,16},{12,44},{16,24},{20,52},{24,0},{28,60},{32,40}... | collective-permute-start | bytes 1671176 | tf_op jit(solution)/shard_map/while/body/ppermute | solution.py:34
  62.2 17.2 %collective-permute-start.7 = (f32[2,544,128]{2,1,0:T(8,128)S(1)}, f32[2,544,128]{2,1,0:T(8,128)S(1)}, u32[]{:S(2)}, u32[]{:S(2)}) collective-permute-start(f32[2,544,128]{2,1,0:T(8,128)S(1)} %get-tuple-element.247), channel_id=1, source_target_pairs={{0,8},{4,36},{8,16},{12,44},{16,24},{20,52},{24,0},{28,60},{32,40}... | collective-permute-start | bytes 1671176 | tf_op jit(solution)/shard_map/while/body/ppermute | solution.py:34
  62.5 16.9 %collective-permute-start.5 = (f32[2,544,128]{2,1,0:T(8,128)S(1)}, f32[2,544,128]{2,1,0:T(8,128)S(1)}, u32[]{:S(2)}, u32[]{:S(2)}) collective-permute-start(f32[2,544,128]{2,1,0:T(8,128)S(1)} %get-tuple-element.243), channel_id=1, source_target_pairs={{0,24},{4,100},{8,0},{12,108},{16,8},{20,116},{24,16},{28,124},{32... | collective-permute-start | bytes 1671176 | tf_op jit(solution)/shard_map/while/body/ppermute | solution.py:34
  65.2 14.8 %collective-permute-start.6 = (f32[2,544,128]{2,1,0:T(8,128)S(1)}, f32[2,544,128]{2,1,0:T(8,128)S(1)}, u32[]{:S(2)}, u32[]{:S(2)}) collective-permute-start(f32[2,544,128]{2,1,0:T(8,128)S(1)} %get-tuple-element.246), channel_id=1, source_target_pairs={{0,24},{4,100},{8,0},{12,108},{16,8},{20,116},{24,16},{28,124},{32... | collective-permute-start | bytes 1671176 | tf_op jit(solution)/shard_map/while/body/ppermute | solution.py:34
  80.9 8.3 %collective-permute-start.9 = (f32[544,128]{1,0:T(8,128)}, f32[544,128]{1,0:T(8,128)S(1)}, u32[]{:S(2)}, u32[]{:S(2)}) collective-permute-start(f32[544,128]{1,0:T(8,128)} %slice_bitcast_fusion.14), channel_id=1, source_target_pairs={{0,32},{4,12},{8,40},{12,20},{16,48},{20,28},{24,56},{28,4},{32,64... | collective-permute-start | bytes 835592 | tf_op jit(solution)/shard_map/while/body/ppermute | solution.py:34
  82.5 8.5 %collective-permute-start.8 = (f32[544,128]{1,0:T(8,128)S(1)}, f32[544,128]{1,0:T(8,128)S(1)}, u32[]{:S(2)}, u32[]{:S(2)}) collective-permute-start(f32[544,128]{1,0:T(8,128)S(1)} %get-tuple-element.249), channel_id=1, source_target_pairs={{0,96},{4,28},{8,104},{12,4},{16,112},{20,12},{24,120},{28,20},{32... | collective-permute-start | bytes 835592 | tf_op jit(solution)/shard_map/while/body/ppermute | solution.py:34
  84.4 9.1 %collective-permute-start.10 = (f32[544,128]{1,0:T(8,128)S(1)}, f32[544,128]{1,0:T(8,128)}, u32[]{:S(2)}, u32[]{:S(2)}) collective-permute-start(f32[544,128]{1,0:T(8,128)S(1)} %get-tuple-element.251), channel_id=1, source_target_pairs={{0,64},{4,20},{8,72},{12,28},{16,80},{20,4},{24,88},{28,12},{32,96... | collective-permute-start | bytes 835592 | tf_op jit(solution)/shard_map/while/body/ppermute | solution.py:34
  97.4 7.9 %collective-permute-start.16 = (f32[544,128]{1,0:T(8,128)}, f32[544,128]{1,0:T(8,128)S(1)}, u32[]{:S(2)}, u32[]{:S(2)}) collective-permute-start(f32[544,128]{1,0:T(8,128)} %get-tuple-element.61), channel_id=1, source_target_pairs={{0,96},{4,28},{8,104},{12,4},{16,112},{20,12},{24,120},{28,20},{32... | collective-permute-start | bytes 835592 | tf_op jit(solution)/shard_map/ppermute | solution.py:34
  98.4 14.5 %collective-permute-start.15 = (f32[544,128]{1,0:T(8,128)}, f32[544,128]{1,0:T(8,128)S(1)}, u32[]{:S(2)}, u32[]{:S(2)}) collective-permute-start(f32[544,128]{1,0:T(8,128)} %get-tuple-element.61), channel_id=1, source_target_pairs={{0,32},{4,12},{8,40},{12,20},{16,48},{20,28},{24,56},{28,4},{32,64... | collective-permute-start | bytes 835592 | tf_op jit(solution)/shard_map/ppermute | solution.py:34
  98.9 14.1 %collective-permute-start.14 = (f32[544,128]{1,0:T(8,128)}, f32[544,128]{1,0:T(8,128)S(1)}, u32[]{:S(2)}, u32[]{:S(2)}) collective-permute-start(f32[544,128]{1,0:T(8,128)} %get-tuple-element.61), channel_id=1, source_target_pairs={{0,64},{4,20},{8,72},{12,28},{16,80},{20,4},{24,88},{28,12},{32,96... | collective-permute-start | bytes 835592 | tf_op jit(solution)/shard_map/ppermute | solution.py:34
  106.3 12.1 %collective-permute-start.23 = (f32[2,544,128]{2,1,0:T(8,128)S(1)}, f32[2,544,128]{2,1,0:T(8,128)S(1)}, u32[]{:S(2)}, u32[]{:S(2)}) collective-permute-start(f32[2,544,128]{2,1,0:T(8,128)S(1)} %pad_maximum_fusion.6.refs_0_), channel_id=1, source_target_pairs={{0,4},{4,0},{8,12},{12,8},{16,20},{20,16},{24,28},{28,24},{32,36},... | collective-permute-start | bytes 1671176 | tf_op jit(solution)/shard_map/ppermute | solution.py:38
  110.3 9.9 %collective-permute-start.19 = (f32[2,544,128]{2,1,0:T(8,128)S(1)}, f32[2,544,128]{2,1,0:T(8,128)S(1)}, u32[]{:S(2)}, u32[]{:S(2)}) collective-permute-start(f32[2,544,128]{2,1,0:T(8,128)S(1)} %pad_maximum_fusion.6.refs_0_), channel_id=1, source_target_pairs={{0,8},{4,36},{8,16},{12,44},{16,24},{20,52},{24,0},{28,60},{32,40}... | collective-permute-start | bytes 1671176 | tf_op jit(solution)/shard_map/ppermute | solution.py:34
  111.9 9.9 %collective-permute-start.17 = (f32[2,544,128]{2,1,0:T(8,128)S(1)}, f32[2,544,128]{2,1,0:T(8,128)S(1)}, u32[]{:S(2)}, u32[]{:S(2)}) collective-permute-start(f32[2,544,128]{2,1,0:T(8,128)S(1)} %pad_maximum_fusion.6.refs_0_), channel_id=1, source_target_pairs={{0,24},{4,100},{8,0},{12,108},{16,8},{20,116},{24,16},{28,124},{32... | collective-permute-start | bytes 1671176 | tf_op jit(solution)/shard_map/ppermute | solution.py:34
  113.0 18.5 %collective-permute-start.24 = (f32[2,544,128]{2,1,0:T(8,128)S(1)}, f32[2,544,128]{2,1,0:T(8,128)S(1)}, u32[]{:S(2)}, u32[]{:S(2)}) collective-permute-start(f32[2,544,128]{2,1,0:T(8,128)S(1)} %pad_maximum_fusion.5.refs_1_), channel_id=1, source_target_pairs={{0,4},{4,0},{8,12},{12,8},{16,20},{20,16},{24,28},{28,24},{32,36},... | collective-permute-start | bytes 1671176 | tf_op jit(solution)/shard_map/ppermute | solution.py:38
  114.9 12.8 %collective-permute-start.18 = (f32[2,544,128]{2,1,0:T(8,128)S(1)}, f32[2,544,128]{2,1,0:T(8,128)S(1)}, u32[]{:S(2)}, u32[]{:S(2)}) collective-permute-start(f32[2,544,128]{2,1,0:T(8,128)S(1)} %pad_maximum_fusion.5.refs_1_), channel_id=1, source_target_pairs={{0,24},{4,100},{8,0},{12,108},{16,8},{20,116},{24,16},{28,124},{32... | collective-permute-start | bytes 1671176 | tf_op jit(solution)/shard_map/ppermute | solution.py:34
  118.4 12.7 %copy-start.2 = (f32[2,544,128]{2,1,0:T(8,128)}, f32[2,544,128]{2,1,0:T(8,128)S(1)}, u32[]{:S(2)}) copy-start(f32[2,544,128]{2,1,0:T(8,128)S(1)} %collective-permute-done.23.refs_8_) | copy-start | bytes 1671172
  118.4 17.3 %collective-permute-start.22 = (f32[2,544,128]{2,1,0:T(8,128)S(1)}, f32[2,544,128]{2,1,0:T(8,128)S(1)}, u32[]{:S(2)}, u32[]{:S(2)}) collective-permute-start(f32[2,544,128]{2,1,0:T(8,128)S(1)} %pad_maximum_fusion.5.refs_1_), channel_id=1, source_target_pairs={{0,8},{4,36},{8,16},{12,44},{16,24},{20,52},{24,0},{28,60},{32,40}... | collective-permute-start | bytes 1671176 | tf_op jit(solution)/shard_map/ppermute | solution.py:34
  120.2 29.1 %copy-start.3 = (f32[2,544,128]{2,1,0:T(8,128)}, f32[2,544,128]{2,1,0:T(8,128)S(1)}, u32[]{:S(2)}) copy-start(f32[2,544,128]{2,1,0:T(8,128)S(1)} %collective-permute-done.19.refs_6_) | copy-start | bytes 1671172
  120.2 15.6 %collective-permute-start.29 = (f32[2,544,128]{2,1,0:T(8,128)S(1)}, f32[2,544,128]{2,1,0:T(8,128)S(1)}, u32[]{:S(2)}, u32[]{:S(2)}) collective-permute-start(f32[2,544,128]{2,1,0:T(8,128)S(1)} %collective-permute-done.19.refs_6_), channel_id=1, source_target_pairs={{0,4},{4,0},{8,12},{12,8},{16,20},{20,16},{24,28},{28,24},{32,36},... | collective-permute-start | bytes 1671176 | tf_op jit(solution)/shard_map/ppermute | solution.py:38
  121.8 27.6 %copy-start.4 = (f32[2,544,128]{2,1,0:T(8,128)}, f32[2,544,128]{2,1,0:T(8,128)S(1)}, u32[]{:S(2)}) copy-start(f32[2,544,128]{2,1,0:T(8,128)S(1)} %collective-permute-done.17.refs_2_) | copy-start | bytes 1671172
  121.8 20.8 %collective-permute-start.20 = (f32[2,544,128]{2,1,0:T(8,128)S(1)}, f32[2,544,128]{2,1,0:T(8,128)S(1)}, u32[]{:S(2)}, u32[]{:S(2)}) collective-permute-start(f32[2,544,128]{2,1,0:T(8,128)S(1)} %collective-permute-done.19.refs_6_), channel_id=1, source_target_pairs={{0,8},{4,36},{8,16},{12,44},{16,24},{20,52},{24,0},{28,60},{32,40}... | collective-permute-start | bytes 1671176 | tf_op jit(solution)/shard_map/ppermute | solution.py:34
  127.7 22.2 %copy-start.6 = (f32[2,544,128]{2,1,0:T(8,128)}, f32[2,544,128]{2,1,0:T(8,128)S(1)}, u32[]{:S(2)}) copy-start(f32[2,544,128]{2,1,0:T(8,128)S(1)} %collective-permute-done.18.refs_3_) | copy-start | bytes 1671172
  127.7 16.4 %collective-permute-start.21 = (f32[2,544,128]{2,1,0:T(8,128)S(1)}, f32[2,544,128]{2,1,0:T(8,128)S(1)}, u32[]{:S(2)}, u32[]{:S(2)}) collective-permute-start(f32[2,544,128]{2,1,0:T(8,128)S(1)} %collective-permute-done.18.refs_3_), channel_id=1, source_target_pairs={{0,24},{4,100},{8,0},{12,108},{16,8},{20,116},{24,16},{28,124},{32... | collective-permute-start | bytes 1671176 | tf_op jit(solution)/shard_map/ppermute | solution.py:34
  131.5 17.8 %copy-start.5 = (f32[2,544,128]{2,1,0:T(8,128)}, f32[2,544,128]{2,1,0:T(8,128)S(1)}, u32[]{:S(2)}) copy-start(f32[2,544,128]{2,1,0:T(8,128)S(1)} %collective-permute-done.24.refs_9_) | copy-start | bytes 1671172
  131.5 18.4 %collective-permute-start.26 = (f32[2,544,128]{2,1,0:T(8,128)S(1)}, f32[2,544,128]{2,1,0:T(8,128)S(1)}, u32[]{:S(2)}, u32[]{:S(2)}) collective-permute-start(f32[2,544,128]{2,1,0:T(8,128)S(1)} %collective-permute-done.18.refs_3_), channel_id=1, source_target_pairs={{0,4},{4,0},{8,12},{12,8},{16,20},{20,16},{24,28},{28,24},{32,36},... | collective-permute-start | bytes 1671176 | tf_op jit(solution)/shard_map/ppermute | solution.py:38
  135.7 14.2 %copy-start.7 = (f32[2,544,128]{2,1,0:T(8,128)}, f32[2,544,128]{2,1,0:T(8,128)S(1)}, u32[]{:S(2)}) copy-start(f32[2,544,128]{2,1,0:T(8,128)S(1)} %collective-permute-done.22.refs_7_) | copy-start | bytes 1671172
  135.7 14.2 %collective-permute-start.25 = (f32[2,544,128]{2,1,0:T(8,128)S(1)}, f32[2,544,128]{2,1,0:T(8,128)S(1)}, u32[]{:S(2)}, u32[]{:S(2)}) collective-permute-start(f32[2,544,128]{2,1,0:T(8,128)S(1)} %collective-permute-done.17.refs_2_), channel_id=1, source_target_pairs={{0,4},{4,0},{8,12},{12,8},{16,20},{20,16},{24,28},{28,24},{32,36},... | collective-permute-start | bytes 1671176 | tf_op jit(solution)/shard_map/ppermute | solution.py:38
  135.8 13.5 %copy-start.8 = (f32[2,544,128]{2,1,0:T(8,128)}, f32[2,544,128]{2,1,0:T(8,128)S(1)}, u32[]{:S(2)}) copy-start(f32[2,544,128]{2,1,0:T(8,128)S(1)} %collective-permute-done.29.refs_14_) | copy-start | bytes 1671172
  135.8 14.1 %collective-permute-start.30 = (f32[2,544,128]{2,1,0:T(8,128)S(1)}, f32[2,544,128]{2,1,0:T(8,128)S(1)}, u32[]{:S(2)}, u32[]{:S(2)}) collective-permute-start(f32[2,544,128]{2,1,0:T(8,128)S(1)} %collective-permute-done.22.refs_7_), channel_id=1, source_target_pairs={{0,4},{4,0},{8,12},{12,8},{16,20},{20,16},{24,28},{28,24},{32,36},... | collective-permute-start | bytes 1671176 | tf_op jit(solution)/shard_map/ppermute | solution.py:38
  142.6 7.4 %copy-start.9 = (f32[2,544,128]{2,1,0:T(8,128)}, f32[2,544,128]{2,1,0:T(8,128)S(1)}, u32[]{:S(2)}) copy-start(f32[2,544,128]{2,1,0:T(8,128)S(1)} %collective-permute-done.20.refs_4_) | copy-start | bytes 1671172
  142.6 7.4 %collective-permute-start.27 = (f32[2,544,128]{2,1,0:T(8,128)S(1)}, f32[2,544,128]{2,1,0:T(8,128)S(1)}, u32[]{:S(2)}, u32[]{:S(2)}) collective-permute-start(f32[2,544,128]{2,1,0:T(8,128)S(1)} %collective-permute-done.20.refs_4_), channel_id=1, source_target_pairs={{0,4},{4,0},{8,12},{12,8},{16,20},{20,16},{24,28},{28,24},{32,36},... | collective-permute-start | bytes 1671176 | tf_op jit(solution)/shard_map/ppermute | solution.py:38
  144.1 5.9 %copy-start.10 = (f32[2,544,128]{2,1,0:T(8,128)}, f32[2,544,128]{2,1,0:T(8,128)S(1)}, u32[]{:S(2)}) copy-start(f32[2,544,128]{2,1,0:T(8,128)S(1)} %collective-permute-done.21.refs_5_) | copy-start | bytes 1671172
  144.1 7.9 %collective-permute-start.28 = (f32[2,544,128]{2,1,0:T(8,128)S(1)}, f32[2,544,128]{2,1,0:T(8,128)}, u32[]{:S(2)}, u32[]{:S(2)}) collective-permute-start(f32[2,544,128]{2,1,0:T(8,128)S(1)} %collective-permute-done.21.refs_5_), channel_id=1, source_target_pairs={{0,4},{4,0},{8,12},{12,8},{16,20},{20,16},{24,28},{28,24},{32,36},... | collective-permute-start | bytes 1671176 | tf_op jit(solution)/shard_map/ppermute | solution.py:38
  149.9 0.8 copy-start.12
  149.9 1.1 copy-start.13
  149.9 1.2 copy-start.11
  151.1 0.8 copy-start.14
Sparse Core Ops, SparseCore 0:
  9.8 29.6 all-gather.1
Sparse Core Ops, SparseCore 1:
  20.8 139.0 all-reduce.2
